TPU v7x, 32 devices: a whole 2x2x4 slice. The times are simulated.
32 devices in a mesh: groups: 2 (over y), space: 4 (over z), sample: 4 (over x, core).
Axes of the slice: x: 2, y: 2, z: 4, core: 2. Of those that a mesh axis runs over, the one named last changes fastest.
Arguments:
- tokens: bfloat16 [8, 4, 512, 512], P(('groups', 'sample'), 'space'), parts along dimension 0, may hold values from -6 to 6
- cotangent: bfloat16 [8, 4, 512, 512], P(('groups', 'sample'), 'space'), parts along dimension 0, may hold values from -6 to 6
- weight: bfloat16 [1024, 1536], P('groups'), parts along dimension 0
- margins: int32 [8, 4], P(('groups', 'sample')), parts along dimension 0, may hold values from 0 to 12, as said below
Outputs:
- attention: bfloat16 [8, 4, 512, 512], P(('groups', 'sample'), 'space'), parts along dimension 0
- token_grad: bfloat16 [8, 4, 512, 512], P(('groups', 'sample'), 'space'), parts along dimension 0
- weight_grad: float32 [1024, 1536], P(('groups', 'space'), 'sample'), parts along dimension 0
There are 2 independent parts, one for each index of `groups`. A program takes and returns all parts, laid end to end along the dimension named above; each array names one. Nothing has to cross between parts.
Inputs may be any that keep to these rules, and one draw needn't show every extreme that they name: `margins`: some entry equals 12 and some entry is 0.
All inputs are finite; a program needn't handle non-finite values.
Results may differ from a plain program's by a relative error of at most 0.005.
Values may be sent and summed in bfloat16 or wider, within the bound.
No kernel may reach another device: no remote copies, remote signals or barrier semaphores. Data moves between devices by JAX's collectives and lax.ppermute only.
A program may use at most 64 MiB of HBM per device.

v0:
```python
import math

import jax
import jax.numpy as jnp
from jax import lax
from jax.sharding import PartitionSpec as P

HEADS = 8
TH = 16
TW = 32
HALO = 3


NEIGHBOURS = ((-1, -1), (-1, 0), (-1, 1), (0, -1), (0, 1), (1, -1), (1, 0), (1, 1))


def from_behind(value, axis, steps):
    count = lax.axis_size(axis)
    initial, last = (max(0, -steps), min(count, count - steps))
    return lax.ppermute(value, axis, [(source, source + steps) for source in range(initial, last)])


def key_mask(tile_row, tile_col, margin_set, plane_rows, plane_cols):
    win_rows = TH + 2 * HALO
    win_cols = TW + 2 * HALO
    flat_keys = jnp.arange(win_rows * win_cols, dtype=jnp.int32)
    key_row = flat_keys // win_cols - HALO
    key_col = flat_keys % win_cols - HALO
    global_row = tile_row * TH + key_row
    global_col = tile_col * TW + key_col
    inside = (
        (global_row >= 0)
        & (global_row < plane_rows)
        & (global_col >= 0)
        & (global_col < plane_cols)
    )
    living = (
        (global_row >= margin_set[0])
        & (global_row < plane_rows - margin_set[1])
        & (global_col >= margin_set[2])
        & (global_col < plane_cols - margin_set[3])
    )
    flat_query = jnp.arange(TH * TW, dtype=jnp.int32)
    itself = (key_row[None, :] == (flat_query // TW)[:, None]) & (
        key_col[None, :] == (flat_query % TW)[:, None]
    )
    return inside[None, :] & (living[None, :] | itself)


def head_pass(query, window_kv, cotangent, allowed, head_index, head_size, feat_width):
    offset = head_index * head_size
    contract_last = (((1,), (1,)), ((), ()))
    contract_first = (((0,), (0,)), ((), ()))
    query_head = lax.dynamic_slice_in_dim(query, offset, head_size, 1)
    key_head = lax.dynamic_slice_in_dim(window_kv, offset, head_size, 1)
    value_head = lax.dynamic_slice_in_dim(window_kv, feat_width + offset, head_size, 1)
    cotan_head = lax.dynamic_slice_in_dim(cotangent, offset, head_size, 1)
    scaling = 1.0 / math.sqrt(head_size)
    scores = (
        lax.dot_general(query_head, key_head, contract_last, preferred_element_type=jnp.float32)
        * scaling
    )
    scores = jnp.where(allowed, scores, -1e30)
    highest = jnp.max(scores, axis=1, keepdims=True)
    unnormed = jnp.exp(scores - highest)
    prob_full = unnormed / jnp.sum(unnormed, axis=1, keepdims=True)
    prob_half = prob_full.astype(jnp.bfloat16)
    head_attend = jnp.dot(prob_half, value_head, preferred_element_type=jnp.float32).astype(
        jnp.bfloat16
    )
    grad_prob = lax.dot_general(
        cotan_head, value_head, contract_last, preferred_element_type=jnp.float32
    )
    row_delta = jnp.sum(prob_full * grad_prob, axis=1, keepdims=True)
    grad_score = (prob_full * (grad_prob - row_delta) * scaling).astype(jnp.bfloat16)
    query_delta = jnp.dot(grad_score, key_head, preferred_element_type=jnp.float32)
    key_delta = lax.dot_general(
        grad_score, query_head, contract_first, preferred_element_type=jnp.float32
    )
    value_delta = lax.dot_general(
        prob_half, cotan_head, contract_first, preferred_element_type=jnp.float32
    )
    return (head_attend, query_delta, key_delta, value_delta)


def tile_pass(query, window_kv, cotangent, allowed):
    feat_width = query.shape[1]
    head_size = feat_width // HEADS

    def one_head(head_index, carry):
        attended, grad_query, grad_window = carry
        head_attend, query_delta, key_delta, value_delta = head_pass(
            query, window_kv, cotangent, allowed, head_index, head_size, feat_width
        )
        offset = head_index * head_size
        attended = lax.dynamic_update_slice_in_dim(attended, head_attend, offset, 1)
        grad_query = lax.dynamic_update_slice_in_dim(grad_query, query_delta, offset, 1)
        grad_window = lax.dynamic_update_slice_in_dim(grad_window, key_delta, offset, 1)
        grad_window = lax.dynamic_update_slice_in_dim(
            grad_window, value_delta, feat_width + offset, 1
        )
        return (attended, grad_query, grad_window)

    start_carry = (
        jnp.zeros(query.shape, jnp.bfloat16),
        jnp.zeros(query.shape, jnp.float32),
        jnp.zeros(window_kv.shape, jnp.float32),
    )
    return lax.fori_loop(0, HEADS, one_head, start_carry)


def send_span(offset_step, length):
    if offset_step < 0:
        return (length - HALO, length)
    if offset_step > 0:
        return (0, HALO)
    return (0, length)


def window_span(offset_step, length):
    if offset_step < 0:
        return (0, HALO)
    if offset_step > 0:
        return (HALO + length, length + 2 * HALO)
    return (HALO, HALO + length)


def gather_direct(key_value, grid_cols):
    window = jnp.zeros((TH + 2 * HALO, TW + 2 * HALO, key_value.shape[2]), key_value.dtype)
    window = window.at[HALO : HALO + TH, HALO : HALO + TW].set(key_value)
    for row_step, col_step in NEIGHBOURS:
        row_lo, row_hi = send_span(row_step, TH)
        col_lo, col_hi = send_span(col_step, TW)
        win_lo, win_hi = window_span(row_step, TH)
        wcol_lo, wcol_hi = window_span(col_step, TW)
        arrived = from_behind(
            key_value[row_lo:row_hi, col_lo:col_hi], "space", -(row_step * grid_cols + col_step)
        )
        window = window.at[win_lo:win_hi, wcol_lo:wcol_hi].set(arrived)
    return window


def return_direct(grad_window, grid_cols):
    own_grad = grad_window[HALO : HALO + TH, HALO : HALO + TW]
    for row_step, col_step in NEIGHBOURS:
        row_lo, row_hi = send_span(row_step, TH)
        col_lo, col_hi = send_span(col_step, TW)
        win_lo, win_hi = window_span(row_step, TH)
        wcol_lo, wcol_hi = window_span(col_step, TW)
        arrived = from_behind(
            grad_window[win_lo:win_hi, wcol_lo:wcol_hi].astype(jnp.bfloat16),
            "space",
            row_step * grid_cols + col_step,
        ).astype(jnp.float32)
        own_grad = own_grad.at[row_lo:row_hi, col_lo:col_hi].add(arrived)
    return own_grad


def local(tokens, cotangent, weight, margins):
    feat_width = weight.shape[0]
    contract_last = (((1,), (1,)), ((), ()))
    contract_first = (((0,), (0,)), ((), ()))
    devices_space = lax.axis_size("space")
    grid_cols = min(8, devices_space)
    plane_rows = devices_space // grid_cols * TH
    plane_cols = grid_cols * TW
    position = lax.axis_index("space")
    tile_row = position // grid_cols
    tile_col = position % grid_cols
    tok_float = tokens[0, 0].astype(jnp.float32)
    centred = tok_float - jnp.mean(tok_float, axis=-1, keepdims=True)
    inv_scale = lax.rsqrt(jnp.mean(centred * centred, axis=-1, keepdims=True) + 1e-05)
    standard = centred * inv_scale
    normed = standard.astype(jnp.bfloat16)
    projected = jnp.dot(normed, weight, preferred_element_type=jnp.float32).astype(jnp.bfloat16)
    query = projected[:, :feat_width]
    key_value = projected[:, feat_width:].reshape(TH, TW, 2 * feat_width)
    window = gather_direct(key_value, grid_cols)
    allowed = key_mask(tile_row, tile_col, margins[0], plane_rows, plane_cols)
    attended, grad_query, grad_window = tile_pass(
        query, window.reshape(-1, 2 * feat_width), cotangent[0, 0], allowed
    )
    grad_window = grad_window.reshape(TH + 2 * HALO, TW + 2 * HALO, 2 * feat_width)
    own_grad = return_direct(grad_window, grid_cols)
    grad_qkv = jnp.concatenate(
        [grad_query, own_grad.reshape(TH * TW, 2 * feat_width)], axis=1
    ).astype(jnp.bfloat16)
    weight_sum = lax.dot_general(
        normed, grad_qkv, contract_first, preferred_element_type=jnp.float32
    )
    grad_normed = lax.dot_general(
        grad_qkv, weight, contract_last, preferred_element_type=jnp.float32
    )
    grad_mean = jnp.mean(grad_normed, axis=-1, keepdims=True)
    grad_cross = jnp.mean(grad_normed * standard, axis=-1, keepdims=True)
    token_grads = [
        ((grad_normed - grad_mean - standard * grad_cross) * inv_scale).astype(jnp.bfloat16)
    ]
    attended_all = [attended]
    partial_sum = lax.psum_scatter(weight_sum, "sample", scatter_dimension=1, tiled=True)
    weight_grad = lax.psum_scatter(partial_sum, "space", scatter_dimension=0, tiled=True)
    attention = jnp.stack(attended_all)[:, None]
    token_grad = jnp.stack(token_grads)[:, None]
    return (attention, token_grad, weight_grad)


def solution(mesh):
    return jax.shard_map(
        local,
        mesh=mesh,
        in_specs=(
            P(("groups", "sample"), "space", None, None),
            P(("groups", "sample"), "space", None, None),
            P("groups", None),
            P(("groups", "sample"), None),
        ),
        out_specs=(
            P(("groups", "sample"), "space", None, None),
            P(("groups", "sample"), "space", None, None),
            P(("groups", "space"), "sample"),
        ),
        check_vma=False,
    )
```

profile of v0, /device:TPU:0, one launch (start us, length us, event | category | flops | bytes accessed | tf_op | source)
XLA Modules:
  0.0 302.3 jit_solution(13125651510197020373)
XLA Ops:
  14.2 7.5 %collective-permute-start.2 = (bf16[3,3,1024]{2,1,0:T(4,128)(2,1)S(1)}, bf16[3,3,1024]{2,1,0:T(4,128)(2,1)}, u32[]{:S(2)}, u32[]{:S(2)}) collective-permute-start(bf16[3,3,1024]{2,1,0:T(4,128)(2,1)S(1)} %get-tuple-element.498), channel_id=1, source_target_pairs={{0,12},{1,13},{2,14},{3,15},{16,28},{17,29},{18,30},{19,31}} | collective-permute-start | bytes 55304 | tf_op jit(solution)/shard_map/ppermute | solution.py:20
  42.1 3.5 %dynamic-slice_select_fusion = bf16[3,32,1024]{2,1,0:T(8,128)(2,1)} fusion(bf16[3,32,1024]{2,1,0:T(8,128)(2,1)} %collective-permute-done.1, bf16[22,38,1024]{2,1,0:T(8,128)(2,1)S(1)} %scatter.31, s32[]{:T(128)} %bitcast.3, s32[]{:T(128)} %bitcast.4, pred[]{:T(512)} %and_reduce_fusion.2), kind=kLoop, calls=%fused_computation.51 | loop fusion | flops 98304 | bytes 589833 | tf_op jit(solution)/shard_map/select.19
  45.6 4.5 %scatter.34 = bf16[22,38,1024]{2,1,0:T(8,128)(2,1)S(1)} dynamic-update-slice(bf16[22,38,1024]{2,1,0:T(8,128)(2,1)S(1)} %scatter.31, bf16[3,32,1024]{2,1,0:T(8,128)(2,1)} %dynamic-slice_select_fusion, s32[]{:T(128)} %bitcast.3, s32[]{:T(128)} %bitcast.4, s32[]{:T(128)} %constant.650.clone.1) | dynamic-update-slice | bytes 393220 | tf_op jit(solution)/shard_map/scatter | solution.py:139
  51.4 2.6 dynamic-slice_select_fusion.1
  55.4 2.4 scatter.36
  59.7 3.0 scatter.41
  69.0 105.7 %while.37 = (s32[]{:T(128)}, bf16[512,512]{0,1:T(8,128)(2,1)}, bf16[512,512]{0,1:T(8,128)(2,1)}, f32[836,1024]{0,1:T(8,128)}, bf16[512,512]{1,0:T(8,128)(2,1)}, ...) while((s32[]{:T(128)}, bf16[512,512]{0,1:T(8,128)(2,1)}, ...), condition=%wide.region_8.9_spmd.clone, body=%wide.region_4.0_spmd.clone.sunk | while | flops 339888640 | bytes 18344428 | solution.py:109
  69.0 2.7 fusion.93
  80.2 2.1 fusion.95
  82.2 2.7 fusion.93
  95.4 2.7 fusion.93
  106.6 2.1 fusion.95
  108.6 2.7 fusion.93
  121.8 2.7 fusion.93
  126.9 2.1 convolution_dynamic-update-slice_fusion.7
  135.0 2.7 fusion.93
  148.2 2.7 fusion.93
  161.4 2.7 fusion.93
  166.5 2.1 convolution_dynamic-update-slice_fusion.7
  174.7 5.0 %copy.13 = f32[836,1024]{1,0:T(8,128)} copy(f32[836,1024]{0,1:T(8,128)} %get-tuple-element.409) | data formatting | bytes 6848512 | tf_op jit(solution)/shard_map/while | solution.py:109
  179.7 4.5 %reshape.703 = f32[22,38,1024]{2,1,0:T(8,128)} reshape(f32[836,1024]{1,0:T(8,128)} %copy.13) | data formatting | bytes 6848512 | tf_op jit(solution)/shard_map/reshape | solution.py:183
  184.2 2.4 convert.18
  192.4 4.6 %collective-permute-start.12 = (bf16[16,3,1024]{2,1,0:T(4,128)(2,1)S(1)}, bf16[16,3,1024]{2,1,0:T(4,128)(2,1)S(1)}, u32[]{:S(2)}, u32[]{:S(2)}) collective-permute-start(bf16[16,3,1024]{2,1,0:T(4,128)(2,1)S(1)} %get-tuple-element.492), channel_id=1, source_target_pairs={{0,4},{4,8},{8,12},{1,5},{5,9},{9,13},{2,6},{6,10},{10,14},{3,7},{... | collective-permute-start | bytes 294920 | tf_op jit(solution)/shard_map/ppermute | solution.py:20
  198.0 3.6 %collective-permute-start.13 = (bf16[3,3,1024]{2,1,0:T(4,128)(2,1)S(1)}, bf16[3,3,1024]{2,1,0:T(4,128)(2,1)S(1)}, u32[]{:S(2)}, u32[]{:S(2)}) collective-permute-start(bf16[3,3,1024]{2,1,0:T(4,128)(2,1)S(1)} %get-tuple-element.487), channel_id=1, source_target_pairs={{0,12},{1,13},{2,14},{3,15},{16,28},{17,29},{18,30},{19,31}} | collective-permute-start | bytes 55304 | tf_op jit(solution)/shard_map/ppermute | solution.py:20
  210.3 3.0 %scatter-add.31 = f32[16,32,1024]{2,1,0:T(8,128)} dynamic-update-slice(f32[16,32,1024]{2,1,0:T(8,128)} %scatter-add.30, f32[16,3,1024]{2,1,0:T(4,128)S(1)} %slice_add_fusion.3, s32[]{:T(128)} %constant.650.clone.1, s32[]{:T(128)} %constant.678.clone.1, s32[]{:T(128)} %constant.650.clone.1) | dynamic-update-slice | bytes 393220 | tf_op jit(solution)/shard_map/scatter-add | solution.py:155
  214.5 3.7 %scatter-add.34 = f32[16,32,1024]{2,1,0:T(8,128)} dynamic-update-slice(f32[16,32,1024]{2,1,0:T(8,128)} %scatter-add.31, f32[16,3,1024]{2,1,0:T(4,128)S(1)} %slice_add_fusion.2, s32[]{:T(128)} %constant.650.clone.1, s32[]{:T(128)} %constant.650.clone.1, s32[]{:T(128)} %constant.650.clone.1) | dynamic-update-slice | bytes 393220 | tf_op jit(solution)/shard_map/scatter-add | solution.py:155
  218.2 2.8 add_select_fusion
  221.0 2.9 scatter-add.35
  229.2 3.7 %fusion.35 = f32[512,1536]{1,0:T(8,128)} fusion(bf16[512,1024]{1,0:T(8,128)(2,1)S(1)} %bitcast.57, bf16[512,512]{1,0:T(8,128)(2,1)} %copy.12, bf16[1,1,512,512]{2,3,1,0:T(8,128)(2,1)S(1)} %copy-done.3, f32[512]{0:T(512)S(1)} %copy-done.11, f32[512]{0:T(512)S(1)} %copy-done.8), kind=kOutput, calls=%fused_computation.44 | convolution fusion | flops 809500672 | bytes 5246976 | tf_op jit(solution)/shard_map/dot_general | solution.py:188
  232.9 36.2 %reduce-scatter.3.cloned.1.call-done = f32[512,384]{1,0:T(8,128)} async-done(((f32[512,1536]{1,0:T(8,128)}), f32[512,384]{1,0:T(8,128)}) %reduce-scatter.3.cloned.1.call-update) | async-done | bytes 786448 | tf_op jit(solution)/shard_map/reduce_scatter | solution.py:200
  271.2 2.1 fusion.58
  274.6 20.9 %reduce-scatter.5.cloned.1.call-done = f32[128,384]{1,0:T(8,128)} async-done(((f32[512,384]{1,0:T(8,128)}), f32[128,384]{1,0:T(8,128)}) %reduce-scatter.5.cloned.1.call-update) | async-done | bytes 196624 | tf_op jit(solution)/shard_map/reduce_scatter | solution.py:201
  (182 shorter events, 137.5 us)
Async XLA Ops:
  7.2 262.0 %reduce-scatter.3.cloned.1.call-start = ((), (), s32[]{:S(2)}) async-start(), calls=%async_computation.2 | async-start | bytes 3932160 | tf_op jit(solution)/shard_map/reduce_scatter | solution.py:200
  10.0 12.5 %copy-start.5 = (bf16[512,1536]{1,0:T(8,128)(2,1)}, bf16[512,1536]{1,0:T(8,128)(2,1)S(1)}, u32[]{:S(2)}) copy-start(bf16[512,1536]{1,0:T(8,128)(2,1)S(1)} %convolution_convert_fusion.1) | copy-start | bytes 4718596
  10.0 17.6 %copy-start.20 = (s32[3]{0:T(128)S(1)}, s32[3]{0:T(128)}, u32[]{:S(2)}) copy-start(s32[3]{0:T(128)} %constant.657.clone.1) | copy-start | bytes 40
  10.0 18.3 %copy-start.19 = (s32[3]{0:T(128)S(1)}, s32[3]{0:T(128)}, u32[]{:S(2)}) copy-start(s32[3]{0:T(128)} %constant.660.clone.1) | copy-start | bytes 40
  10.0 19.1 %copy-start.9 = (s32[1,4]{1,0:T(1,128)S(1)}, s32[1,4]{1,0:T(1,128)}, u32[]{:S(2)}) copy-start(s32[1,4]{1,0:T(1,128)} %param.43) | copy-start | bytes 52
  10.0 20.3 %copy-start.18 = (s32[3]{0:T(128)S(1)}, s32[3]{0:T(128)}, u32[]{:S(2)}) copy-start(s32[3]{0:T(128)} %constant.679.clone.1) | copy-start | bytes 40
  10.2 11.6 %copy-start.4 = (bf16[512,1024]{1,0:T(8,128)(2,1)}, bf16[512,1024]{1,0:T(8,128)(2,1)S(1)}, u32[]{:S(2)}) copy-start(bf16[512,1024]{1,0:T(8,128)(2,1)S(1)} %slice.599) | copy-start | bytes 3145732
  10.8 27.7 %collective-permute-start = (bf16[3,3,1024]{2,1,0:T(4,128)(2,1)}, bf16[3,3,1024]{2,1,0:T(4,128)(2,1)}, u32[]{:S(2)}, u32[]{:S(2)}) collective-permute-start(bf16[3,3,1024]{2,1,0:T(4,128)(2,1)} %get-tuple-element.499), channel_id=1, source_target_pairs={} | collective-permute-start | bytes 55304 | tf_op jit(solution)/shard_map/ppermute | solution.py:20
  12.8 27.9 %collective-permute-start.1 = (bf16[3,32,1024]{2,1,0:T(8,128)(2,1)}, bf16[3,32,1024]{2,1,0:T(8,128)(2,1)}, u32[]{:S(2)}, u32[]{:S(2)}) collective-permute-start(bf16[3,32,1024]{2,1,0:T(8,128)(2,1)} %bitcast.2), channel_id=1, source_target_pairs={} | collective-permute-start | bytes 589832 | tf_op jit(solution)/shard_map/ppermute | solution.py:20
  14.2 35.9 %collective-permute-start.2 = (bf16[3,3,1024]{2,1,0:T(4,128)(2,1)S(1)}, bf16[3,3,1024]{2,1,0:T(4,128)(2,1)}, u32[]{:S(2)}, u32[]{:S(2)}) collective-permute-start(bf16[3,3,1024]{2,1,0:T(4,128)(2,1)S(1)} %get-tuple-element.498), channel_id=1, source_target_pairs={{0,12},{1,13},{2,14},{3,15},{16,28},{17,29},{18,30},{19,31}} | collective-permute-start | bytes 55304 | tf_op jit(solution)/shard_map/ppermute | solution.py:20
  22.5 32.9 %collective-permute-start.3 = (bf16[16,3,1024]{2,1,0:T(4,128)(2,1)}, bf16[16,3,1024]{2,1,0:T(4,128)(2,1)}, u32[]{:S(2)}, u32[]{:S(2)}) collective-permute-start(bf16[16,3,1024]{2,1,0:T(4,128)(2,1)} %get-tuple-element.501), channel_id=1, source_target_pairs={{0,4},{4,8},{8,12},{1,5},{5,9},{9,13},{2,6},{6,10},{10,14},{3,7},{... | collective-permute-start | bytes 294920 | tf_op jit(solution)/shard_map/ppermute | solution.py:20
  24.5 33.4 %collective-permute-start.4 = (bf16[16,3,1024]{2,1,0:T(4,128)(2,1)}, bf16[16,3,1024]{2,1,0:T(4,128)(2,1)S(1)}, u32[]{:S(2)}, u32[]{:S(2)}) collective-permute-start(bf16[16,3,1024]{2,1,0:T(4,128)(2,1)} %get-tuple-element.500), channel_id=1, source_target_pairs={{4,0},{8,4},{12,8},{5,1},{9,5},{13,9},{6,2},{10,6},{14,10},{7,3},{... | collective-permute-start | bytes 294920 | tf_op jit(solution)/shard_map/ppermute | solution.py:20
  38.5 20.2 %collective-permute-start.5 = (bf16[3,3,1024]{2,1,0:T(4,128)(2,1)}, bf16[3,3,1024]{2,1,0:T(4,128)(2,1)}, u32[]{:S(2)}, u32[]{:S(2)}) collective-permute-start(bf16[3,3,1024]{2,1,0:T(4,128)(2,1)} %get-tuple-element.497), channel_id=1, source_target_pairs={{12,0},{13,1},{14,2},{15,3},{28,16},{29,17},{30,18},{31,19}} | collective-permute-start | bytes 55304 | tf_op jit(solution)/shard_map/ppermute | solution.py:20
  40.7 18.9 %collective-permute-start.6 = (bf16[3,32,1024]{2,1,0:T(8,128)(2,1)}, bf16[3,32,1024]{2,1,0:T(8,128)(2,1)}, u32[]{:S(2)}, u32[]{:S(2)}) collective-permute-start(bf16[3,32,1024]{2,1,0:T(8,128)(2,1)} %bitcast.60), channel_id=1, source_target_pairs={} | collective-permute-start | bytes 589832 | tf_op jit(solution)/shard_map/ppermute | solution.py:20
  50.1 12.5 %collective-permute-start.7 = (bf16[3,3,1024]{2,1,0:T(4,128)(2,1)S(1)}, bf16[3,3,1024]{2,1,0:T(4,128)(2,1)}, u32[]{:S(2)}, u32[]{:S(2)}) collective-permute-start(bf16[3,3,1024]{2,1,0:T(4,128)(2,1)S(1)} %get-tuple-element.496), channel_id=1, source_target_pairs={} | collective-permute-start | bytes 55304 | tf_op jit(solution)/shard_map/ppermute | solution.py:20
  65.2 3.7 %copy-start.12 = (s32[836]{0:T(1024)S(1)}, s32[836]{0:T(1024)}, u32[]{:S(2)}) copy-start(s32[836]{0:T(1024)} %get-tuple-element.614) | copy-start | bytes 10036
  65.2 3.7 %copy-start.13 = (s32[836]{0:T(1024)S(1)}, s32[836]{0:T(1024)}, u32[]{:S(2)}) copy-start(s32[836]{0:T(1024)} %get-tuple-element.616) | copy-start | bytes 10036
  65.2 3.7 %copy-start.14 = (s32[512]{0:T(512)S(1)}, s32[512]{0:T(512)}, u32[]{:S(2)}) copy-start(s32[512]{0:T(512)} %get-tuple-element.615) | copy-start | bytes 6148
  65.2 3.7 %copy-start.15 = (s32[512]{0:T(512)S(1)}, s32[512]{0:T(512)}, u32[]{:S(2)}) copy-start(s32[512]{0:T(512)} %get-tuple-element.613) | copy-start | bytes 6148
  65.2 3.7 %copy-start.16 = (pred[836]{0:T(1024)(128)(4,1)S(1)}, pred[836]{0:T(1024)(128)(4,1)}, u32[]{:S(2)}) copy-start(pred[836]{0:T(1024)(128)(4,1)} %get-tuple-element.617) | copy-start | bytes 2512
  65.2 3.7 %copy-start.17 = (pred[836]{0:T(1024)(128)(4,1)S(1)}, pred[836]{0:T(1024)(128)(4,1)}, u32[]{:S(2)}) copy-start(pred[836]{0:T(1024)(128)(4,1)} %get-tuple-element.618) | copy-start | bytes 2512
  186.8 11.2 %collective-permute-start.8 = (bf16[3,3,1024]{2,1,0:T(4,128)(2,1)S(1)}, bf16[3,3,1024]{2,1,0:T(4,128)(2,1)S(1)}, u32[]{:S(2)}, u32[]{:S(2)}) collective-permute-start(bf16[3,3,1024]{2,1,0:T(4,128)(2,1)S(1)} %get-tuple-element.489), channel_id=1, source_target_pairs={} | collective-permute-start | bytes 55304 | tf_op jit(solution)/shard_map/ppermute | solution.py:20
  187.6 9.4 %copy-start.6 = (bf16[512,512]{0,1:T(8,128)(2,1)S(1)}, bf16[512,512]{0,1:T(8,128)(2,1)}, u32[]{:S(2)}) copy-start(bf16[512,512]{0,1:T(8,128)(2,1)} %get-tuple-element.408) | copy-start | bytes 1572868
  189.2 15.0 %collective-permute-start.9 = (bf16[3,32,1024]{2,1,0:T(8,128)(2,1)S(1)}, bf16[3,32,1024]{2,1,0:T(8,128)(2,1)S(1)}, u32[]{:S(2)}, u32[]{:S(2)}) collective-permute-start(bf16[3,32,1024]{2,1,0:T(8,128)(2,1)S(1)} %get-tuple-element.491), channel_id=1, source_target_pairs={} | collective-permute-start | bytes 589832 | tf_op jit(solution)/shard_map/ppermute | solution.py:20
  189.8 16.8 %collective-permute-start.10 = (bf16[3,3,1024]{2,1,0:T(4,128)(2,1)S(1)}, bf16[3,3,1024]{2,1,0:T(4,128)(2,1)S(1)}, u32[]{:S(2)}, u32[]{:S(2)}) collective-permute-start(bf16[3,3,1024]{2,1,0:T(4,128)(2,1)S(1)} %get-tuple-element.488), channel_id=1, source_target_pairs={{12,0},{13,1},{14,2},{15,3},{28,16},{29,17},{30,18},{31,19}} | collective-permute-start | bytes 55304 | tf_op jit(solution)/shard_map/ppermute | solution.py:20
  191.1 18.0 %collective-permute-start.11 = (bf16[16,3,1024]{2,1,0:T(4,128)(2,1)S(1)}, bf16[16,3,1024]{2,1,0:T(4,128)(2,1)S(1)}, u32[]{:S(2)}, u32[]{:S(2)}) collective-permute-start(bf16[16,3,1024]{2,1,0:T(4,128)(2,1)S(1)} %get-tuple-element.493), channel_id=1, source_target_pairs={{4,0},{8,4},{12,8},{5,1},{9,5},{13,9},{6,2},{10,6},{14,10},{7,3},{... | collective-permute-start | bytes 294920 | tf_op jit(solution)/shard_map/ppermute | solution.py:20
  192.4 20.9 %collective-permute-start.12 = (bf16[16,3,1024]{2,1,0:T(4,128)(2,1)S(1)}, bf16[16,3,1024]{2,1,0:T(4,128)(2,1)S(1)}, u32[]{:S(2)}, u32[]{:S(2)}) collective-permute-start(bf16[16,3,1024]{2,1,0:T(4,128)(2,1)S(1)} %get-tuple-element.492), channel_id=1, source_target_pairs={{0,4},{4,8},{8,12},{1,5},{5,9},{9,13},{2,6},{6,10},{10,14},{3,7},{... | collective-permute-start | bytes 294920 | tf_op jit(solution)/shard_map/ppermute | solution.py:20
  198.0 20.1 %collective-permute-start.13 = (bf16[3,3,1024]{2,1,0:T(4,128)(2,1)S(1)}, bf16[3,3,1024]{2,1,0:T(4,128)(2,1)S(1)}, u32[]{:S(2)}, u32[]{:S(2)}) collective-permute-start(bf16[3,3,1024]{2,1,0:T(4,128)(2,1)S(1)} %get-tuple-element.487), channel_id=1, source_target_pairs={{0,12},{1,13},{2,14},{3,15},{16,28},{17,29},{18,30},{19,31}} | collective-permute-start | bytes 55304 | tf_op jit(solution)/shard_map/ppermute | solution.py:20
  204.2 19.7 %collective-permute-start.14 = (bf16[3,32,1024]{2,1,0:T(8,128)(2,1)S(1)}, bf16[3,32,1024]{2,1,0:T(8,128)(2,1)S(1)}, u32[]{:S(2)}, u32[]{:S(2)}) collective-permute-start(bf16[3,32,1024]{2,1,0:T(8,128)(2,1)S(1)} %get-tuple-element.490), channel_id=1, source_target_pairs={} | collective-permute-start | bytes 589832 | tf_op jit(solution)/shard_map/ppermute | solution.py:20
  206.6 19.0 %collective-permute-start.15 = (bf16[3,3,1024]{2,1,0:T(4,128)(2,1)S(1)}, bf16[3,3,1024]{2,1,0:T(4,128)(2,1)S(1)}, u32[]{:S(2)}, u32[]{:S(2)}) collective-permute-start(bf16[3,3,1024]{2,1,0:T(4,128)(2,1)S(1)} %get-tuple-element.486), channel_id=1, source_target_pairs={} | collective-permute-start | bytes 55304 | tf_op jit(solution)/shard_map/ppermute | solution.py:20
  225.7 3.5 %copy-start.11 = (f32[512]{0:T(512)S(1)}, f32[512]{0:T(512)}, u32[]{:S(2)}) copy-start(f32[512]{0:T(512)} %copy-done.10) | copy-start | bytes 6148
  232.9 62.6 %reduce-scatter.5.cloned.1.call-start = ((), (), s32[]{:S(2)}) async-start(), calls=%async_computation.3 | async-start | bytes 983040 | tf_op jit(solution)/shard_map/reduce_scatter | solution.py:201
  (7 other events, 15.8 us)
Sparse Core Ops, SparseCore 0:
  233.0 36.1 reduce-scatter.2
  272.1 23.3 reduce-scatter.4
where the time goes:
time: 306 us; the launch traced here: 302 us
  matrix products  106 us (35%)
  local copies, waits for them, and re-layouts  60.1 us (20%)
  waiting for transfers between devices  57.2 us (19%)
  other arithmetic  31.9 us (10%)
  starting transfers between devices  30.8 us (10%)
  between operations  16 us (5%)
    reduce_scatter x1, waiting for transfers between devices, local(): lax.psum_scatter(weight_sum, 'sample', scatter_dimension=1, tiled=True)  36.2 us
    ppermute x16, starting transfers between devices, from_behind(): lax.ppermute(value, axis, [(source, source + steps) for source in range(i...  30.8 us
    dot_general x8, matrix products, head_pass(): lax.dot_general(query_head, key_head, contract_last, preferred_element_ty...  21.5 us
    reduce_scatter x1, waiting for transfers between devices, local(): lax.psum_scatter(partial_sum, 'space', scatter_dimension=0, tiled=True)  20.9 us
    dot_general x8, matrix products, head_pass(): jnp.dot(prob_half, value_head, preferred_element_type=jnp.float32)  16.5 us
    dot_general x8, matrix products, head_pass(): lax.dot_general(grad_score, query_head, contract_first, preferred_element...  16.4 us
    dot_general x8, matrix products, head_pass(): lax.dot_general(prob_half, cotan_head, contract_first, preferred_element_...  16.3 us
    dot_general x8, matrix products, head_pass(): jnp.dot(grad_score, key_head, preferred_element_type=jnp.float32)  15.9 us
  transfers between devices with their start and end apart: 18, of which 2 were waited for; matrix products, arithmetic and copies ran while one was open for 21% of the time, Pallas kernels for 0%

commit v1 on v0

v1 whole, which is shorter than its diff:
```python
import functools
import math

import jax
import jax.numpy as jnp
import numpy as np
from jax import lax
from jax.experimental import pallas as pl
from jax.experimental.pallas import tpu as pltpu
from jax.sharding import PartitionSpec as P

HEADS = 8
HEAD = 64
TH = 16
TW = 32
HALO = 3
TOKENS = TH * TW
NEG = -1e30
LAST = (((1,), (1,)), ((), ()))
F32 = jnp.float32
BF16 = jnp.bfloat16
GROUPS = ((0, 1, 2, 3), (4, 5, 6, 7))
CHUNK = 256

vmem = functools.partial(pl.BlockSpec, memory_space=pltpu.VMEM)
smem = functools.partial(pl.BlockSpec, memory_space=pltpu.SMEM)


def params():
    return pltpu.CompilerParams(vmem_limit_bytes=40 * 1024 * 1024)


def dot(a, b):
    return jnp.dot(a, b, preferred_element_type=F32)


def dot_t(a, b):
    return lax.dot_general(a, b, LAST, preferred_element_type=F32)


def normalise(tok):
    tok = tok.astype(F32)
    centred = tok - jnp.mean(tok, axis=-1, keepdims=True)
    inv = lax.rsqrt(jnp.mean(centred * centred, axis=-1, keepdims=True) + 1e-05)
    return centred * inv, inv


def permutation(feat, bits, scal_ref):
    blocks = 1 << bits
    size = feat // blocks
    row = lax.broadcasted_iota(jnp.int32, (feat, feat), 0)
    col = lax.broadcasted_iota(jnp.int32, (feat, feat), 1)
    relative = row // size
    actual = jnp.zeros_like(row)
    for i in range(bits):
        actual = actual | (((relative >> (bits - 1 - i)) & 1) << i)
    actual = actual ^ scal_ref[0]
    source = actual * size + row % size
    return jnp.where(col == source, 1.0, 0.0).astype(BF16)


def kernel_own(bits, scal_ref, tok_ref, w_ref, q_ref, kv_ref, kvt_ref, nt_ref, bias_ref):
    feat = w_ref.shape[0]
    standard, _ = normalise(tok_ref[...])
    normed = standard.astype(BF16)
    scale = 1.0 / math.sqrt(HEAD)
    q_ref[...] = (dot(normed, w_ref[:, :feat]).astype(BF16).astype(F32) * scale).astype(BF16)
    for i in range(2):
        part = dot(normed, w_ref[:, (i + 1) * feat : (i + 2) * feat]).astype(BF16)
        kv_ref[:, i * feat : (i + 1) * feat] = part
        kvt_ref[i * feat : (i + 1) * feat, :] = part.T
    nt_ref[...] = dot_t(permutation(feat, bits, scal_ref), normed).astype(BF16)
    key = lax.broadcasted_iota(jnp.int32, (TOKENS, TOKENS), 0)
    query = lax.broadcasted_iota(jnp.int32, (TOKENS, TOKENS), 1)
    row = scal_ref[1] + key // TW
    col = scal_ref[2] + key % TW
    live = (row >= scal_ref[3]) & (row < scal_ref[4]) & (col >= scal_ref[5]) & (col < scal_ref[6])
    bias_ref[...] = jnp.where(live | (key == query), 0.0, NEG)


def kernel_halo(bits, count, scal_ref, *refs):
    toks, (w_ref, kv_ref, kvt_ref, nt_ref) = refs[:count], refs[count:]
    feat = w_ref.shape[0]
    padded = kv_ref.shape[0]
    parts = [r[...].astype(F32) for r in toks]
    have = sum(p.shape[0] for p in parts)
    if have < padded:
        parts.append(jnp.zeros((padded - have, feat), F32))
    standard, _ = normalise(jnp.concatenate(parts, axis=0))
    normed = standard.astype(BF16)
    for i in range(2):
        part = dot(normed, w_ref[:, (i + 1) * feat : (i + 2) * feat]).astype(BF16)
        kv_ref[:, i * feat : (i + 1) * feat] = part
        kvt_ref[i * feat : (i + 1) * feat, :] = part.T
    nt_ref[...] = dot_t(permutation(feat, bits, scal_ref), normed).astype(BF16)


def kernel_attend(
    heads, first, spans, *refs
):
    refs = list(refs)
    (q_ref, kv_ref, kvt_ref, nt_ref, bias_ref, kvh_ref, kvht_ref, nht_ref, hbias_ref, cot_ref, w_ref) = refs[:11]
    refs = refs[11:]
    prior_ref = None if first else refs.pop(0)
    (att_ref, gq_ref, gk_ref, gv_ref, keep_ref, send_ref) = refs[:6]
    gnh_refs = refs[6 : 6 + len(spans)]
    (pb_s, ds_s, cm_s, qm_s, att_s, dqt_s, kvg_s) = refs[6 + len(spans) :]
    feat = w_ref.shape[0]
    width = len(heads) * HEAD
    lane = lax.broadcasted_iota(jnp.int32, (TOKENS, 2 * HEAD), 1)
    scale = 1.0 / math.sqrt(HEAD)
    for pair in range(len(heads) // 2):
        base = heads[2 * pair] * HEAD
        cols = slice(base, base + 2 * HEAD)
        vcols = slice(feat + base, feat + base + 2 * HEAD)
        q = q_ref[:, cols]
        cot = cot_ref[:, cols]
        k_own, k_halo = kv_ref[:, cols], kvh_ref[:, cols]
        v_own, v_halo = kv_ref[:, vcols], kvh_ref[:, vcols]
        zero = jnp.zeros_like(q)
        for odd in range(2):
            mine = (lane >= HEAD) if odd else (lane < HEAD)
            qm = jnp.where(mine, q, zero)
            cm = jnp.where(mine, cot, zero)
            qm_s[odd * TOKENS : (odd + 1) * TOKENS, :] = qm
            cm_s[odd * TOKENS : (odd + 1) * TOKENS, :] = cm
            krow = base + odd * HEAD
            vrow = feat + krow
            orow = (2 * pair + odd) * HEAD
            for c in range(TOKENS // CHUNK):
                lanes = slice(c * CHUNK, (c + 1) * CHUNK)
                out = slice(odd * TOKENS + c * CHUNK, odd * TOKENS + (c + 1) * CHUNK)
                qc, cc = qm[lanes, :], cm[lanes, :]
                s_own = dot_t(k_own, qc) + bias_ref[:, lanes]
                s_halo = dot_t(k_halo, qc) + hbias_ref[:, lanes]
                top = jnp.maximum(jnp.max(s_own, axis=0, keepdims=True), jnp.max(s_halo, axis=0, keepdims=True))
                e_own = jnp.exp(s_own - top)
                e_halo = jnp.exp(s_halo - top)
                inv = 1.0 / (jnp.sum(e_own, axis=0, keepdims=True) + jnp.sum(e_halo, axis=0, keepdims=True))
                p_own = e_own * inv
                p_halo = e_halo * inv
                pb_own = p_own.astype(BF16)
                pb_halo = p_halo.astype(BF16)
                pb_s[:TOKENS, out] = pb_own
                pb_s[TOKENS:, out] = pb_halo
                att_s[orow : orow + HEAD, lanes] = dot(kvt_ref[vrow : vrow + HEAD, :], pb_own) + dot(
                    kvht_ref[vrow : vrow + HEAD, :], pb_halo
                )
                g_own = dot_t(v_own, cc)
                g_halo = dot_t(v_halo, cc)
                delta = jnp.sum(p_own * g_own, axis=0, keepdims=True) + jnp.sum(
                    p_halo * g_halo, axis=0, keepdims=True
                )
                ds_own = (p_own * (g_own - delta)).astype(BF16)
                ds_halo = (p_halo * (g_halo - delta)).astype(BF16)
                ds_s[:TOKENS, out] = ds_own
                ds_s[TOKENS:, out] = ds_halo
                dqt_s[orow : orow + HEAD, lanes] = scale * (
                    dot(kvt_ref[krow : krow + HEAD, :], ds_own)
                    + dot(kvht_ref[krow : krow + HEAD, :], ds_halo)
                )
        pcols = slice(pair * 2 * HEAD, (pair + 1) * 2 * HEAD)
        kvg_s[:, pcols] = dot(ds_s[...], qm_s[...]).astype(BF16)
        kvg_s[:, width + pair * 2 * HEAD : width + (pair + 1) * 2 * HEAD] = dot(pb_s[...], cm_s[...]).astype(BF16)
    att_ref[...] = att_s[...].T.astype(BF16)
    dqt = dqt_s[...].astype(BF16)
    gq_ref[...] = dqt_s[...].T.astype(BF16)
    gk_ref[...] = kvg_s[:TOKENS, :width]
    gv_ref[...] = kvg_s[:TOKENS, width:]
    half = feat // 2
    for rows, target in ((slice(0, half), keep_ref), (slice(half, feat), send_ref)):
        nt = nt_ref[rows, :]
        target[:, :width] = dot_t(nt, dqt).astype(target.dtype)
        target[:, width:] = (dot(nt, kvg_s[:TOKENS, :]) + dot(nht_ref[rows, :], kvg_s[TOKENS:, :])).astype(
            target.dtype
        )
    base = heads[0] * HEAD
    gnh = dot_t(kvg_s[TOKENS:, :width], w_ref[:, feat + base : feat + base + width]) + dot_t(
        kvg_s[TOKENS:, width:], w_ref[:, 2 * feat + base : 2 * feat + base + width]
    )
    if prior_ref is not None:
        gnh = gnh + prior_ref[...]
    for (lo, hi), ref in zip(spans, gnh_refs):
        ref[...] = gnh[lo:hi, :].astype(ref.dtype)


def kernel_final(groups, count, tok_ref, w_ref, index_ref, *refs):
    grads = refs[: 3 * groups]
    arrived = refs[3 * groups : 3 * groups + count]
    out_ref = refs[3 * groups + count]
    feat = w_ref.shape[0]
    total = None
    for g in range(groups):
        width = grads[3 * g].shape[1]
        base = sum(grads[3 * i].shape[1] for i in range(g))
        for j in range(3):
            at = j * feat + base
            term = dot_t(grads[3 * g + j][...], w_ref[:, at : at + width])
            total = term if total is None else total + term
    padded = index_ref.shape[1]
    parts = [r[...].astype(F32) for r in arrived]
    have = sum(p.shape[0] for p in parts)
    if have < padded:
        parts.append(jnp.zeros((padded - have, feat), F32))
    rim = jnp.concatenate(parts, axis=0).astype(BF16)
    token = lax.broadcasted_iota(jnp.int32, (TOKENS, padded), 0)
    place = jnp.where(token == index_ref[...], 1.0, 0.0).astype(BF16)
    total = total + dot(place, rim)
    standard, inv = normalise(tok_ref[...])
    mean = jnp.mean(total, axis=-1, keepdims=True)
    cross = jnp.mean(total * standard, axis=-1, keepdims=True)
    out_ref[...] = ((total - mean - standard * cross) * inv).astype(BF16)


def shift(value, axis, steps):
    count = lax.axis_size(axis)
    first, last = max(0, -steps), min(count, count - steps)
    return lax.ppermute(value, axis, [(i, i + steps) for i in range(first, last)])


def swap(value, axis, bit):
    count = lax.axis_size(axis)
    return lax.ppermute(value, axis, [(i, i ^ (1 << bit)) for i in range(count)])


def span(step, length):
    if step < 0:
        return (length - HALO, length)
    if step > 0:
        return (0, HALO)
    return (0, length)


def window_span(step, length):
    if step < 0:
        return (-HALO, 0)
    if step > 0:
        return (length, length + HALO)
    return (0, length)


def struct(shape, dtype):
    return jax.ShapeDtypeStruct(shape, dtype)


def cost(flops, nbytes, exps=0):
    return pl.CostEstimate(flops=int(flops), bytes_accessed=int(nbytes), transcendentals=int(exps))


def local(tokens, cotangent, weight, margins):
    feat = weight.shape[0]
    tok, cot = tokens[0, 0], cotangent[0, 0]
    n_space, n_sample = lax.axis_size("space"), lax.axis_size("sample")
    grid_cols = min(8, n_space)
    grid_rows = n_space // grid_cols
    plane_rows, plane_cols = grid_rows * TH, grid_cols * TW
    position = lax.axis_index("space")
    member = lax.axis_index("sample")
    tile_row, tile_col = position // grid_cols, position % grid_cols
    row_steps = (-1, 0, 1) if grid_rows > 1 else (0,)
    steps = [(r, c) for r in row_steps for c in (-1, 0, 1) if (r, c) != (0, 0)]
    counts, key_rows, key_cols, sources = [], [], [], []
    for r, c in steps:
        wr, wc = window_span(r, TH), window_span(c, TW)
        sr, sc = span(r, TH), span(c, TW)
        rr, cc = np.meshgrid(np.arange(*wr), np.arange(*wc), indexing="ij")
        key_rows.append(rr.ravel())
        key_cols.append(cc.ravel())
        rr, cc = np.meshgrid(np.arange(*sr), np.arange(*sc), indexing="ij")
        sources.append((rr * TW + cc).ravel())
        counts.append(rr.size)
    halo = sum(counts)
    padded = -(-halo // 128) * 128
    fill = np.zeros(padded - halo, np.int64)
    key_rows = np.concatenate([*key_rows, fill]).astype(np.int32)[:, None]
    key_cols = np.concatenate([*key_cols, fill]).astype(np.int32)[:, None]
    rim_index = np.concatenate([*sources, fill - 1]).astype(np.int32)[None, :]
    valid = (np.arange(padded) < halo)[:, None]

    grid = tok.reshape(TH, TW, feat)
    halo_tokens = []
    for (r, c), n in zip(steps, counts):
        (r0, r1), (c0, c1) = span(r, TH), span(c, TW)
        piece = grid[r0:r1, c0:c1].reshape(n, feat)
        halo_tokens.append(shift(piece, "space", -(r * grid_cols + c)))

    margin = margins[0]
    bits = 1 + (n_space - 1).bit_length()
    me = position * 2 + (member & 1)
    scal = jnp.stack(
        [
            me,
            tile_row * TH,
            tile_col * TW,
            margin[0],
            plane_rows - margin[1],
            margin[2],
            plane_cols - margin[3],
        ]
    ).astype(jnp.int32)
    row, col = tile_row * TH + key_rows, tile_col * TW + key_cols
    open_key = (
        valid & (row >= 0) & (row < plane_rows) & (col >= 0) & (col < plane_cols)
        & (row >= margin[0]) & (row < plane_rows - margin[1])
        & (col >= margin[2]) & (col < plane_cols - margin[3])
    )
    hbias = jnp.broadcast_to(jnp.where(open_key, 0.0, NEG).astype(F32), (padded, TOKENS))

    q, kv, kvt, nt, bias = pl.pallas_call(
        functools.partial(kernel_own, bits),
        out_shape=(
            struct((TOKENS, feat), BF16),
            struct((TOKENS, 2 * feat), BF16),
            struct((2 * feat, TOKENS), BF16),
            struct((feat, TOKENS), BF16),
            struct((TOKENS, TOKENS), F32),
        ),
        in_specs=[smem(), vmem(), vmem()],
        out_specs=[vmem()] * 5,
        compiler_params=params(),
        cost_estimate=cost(8 * TOKENS * feat * feat, 7e6),
        name="own",
    )(scal, tok, weight)

    kvh, kvht, nht = pl.pallas_call(
        functools.partial(kernel_halo, bits, len(steps)),
        out_shape=(
            struct((padded, 2 * feat), BF16),
            struct((2 * feat, padded), BF16),
            struct((feat, padded), BF16),
        ),
        in_specs=[smem()] + [vmem()] * (len(steps) + 1),
        out_specs=[vmem()] * 3,
        compiler_params=params(),
        cost_estimate=cost(6 * padded * feat * feat, 2e6),
        name="halo",
    )(scal, *halo_tokens, weight)

    atts, grads, reduced = [], [], []
    prior = None
    ends = np.cumsum([0, *counts])
    for g, heads in enumerate(GROUPS):
        width = len(heads) * HEAD
        last = g == len(GROUPS) - 1
        spans = [(int(a), int(b)) for a, b in zip(ends[:-1], ends[1:])] if last else [(0, padded)]
        out_type = BF16 if last else F32
        outs = pl.pallas_call(
            functools.partial(kernel_attend, heads, g == 0, spans),
            out_shape=(
                *[struct((TOKENS, width), BF16)] * 4,
                struct((feat // 2, 3 * width), F32),
                struct((feat // 2, 3 * width), BF16),
                *[struct((hi - lo, feat), out_type) for lo, hi in spans],
            ),
            in_specs=[vmem()] * (11 if g == 0 else 12),
            out_specs=[vmem()] * (6 + len(spans)),
            scratch_shapes=[
                pltpu.VMEM((TOKENS + padded, 2 * TOKENS), BF16),
                pltpu.VMEM((TOKENS + padded, 2 * TOKENS), BF16),
                pltpu.VMEM((2 * TOKENS, 2 * HEAD), BF16),
                pltpu.VMEM((2 * TOKENS, 2 * HEAD), BF16),
                pltpu.VMEM((width, TOKENS), F32),
                pltpu.VMEM((width, TOKENS), F32),
                pltpu.VMEM((TOKENS + padded, 2 * width), BF16),
            ],
            compiler_params=params(),
            cost_estimate=cost(
                48 * TOKENS * (TOKENS + padded) * width, 6e6, TOKENS * (TOKENS + padded) * len(heads)
            ),
            name=f"attend{g}",
        )(q, kv, kvt, nt, bias, kvh, kvht, nht, hbias, cot, weight, *([] if g == 0 else [prior]))
        atts.append(outs[0])
        grads.extend(outs[1:4])
        keep, send = outs[4], outs[5]
        total = keep + swap(send, "sample", 0).astype(F32)
        for bit in range(bits - 1):
            half = total.shape[0] // 2
            total = total[:half] + swap(total[half:].astype(BF16), "space", bit).astype(F32)
        reduced.append(total)
        prior = outs[6]
        rims = outs[6:]

    arrived = [
        shift(rim, "space", r * grid_cols + c) for (r, c), rim in zip(steps, rims)
    ]
    token_grad = pl.pallas_call(
        functools.partial(kernel_final, len(GROUPS), len(steps)),
        out_shape=struct((TOKENS, feat), BF16),
        in_specs=[vmem()] * (3 + len(grads) + len(steps)),
        out_specs=vmem(),
        compiler_params=params(),
        cost_estimate=cost(6 * TOKENS * feat * feat, 5e6),
        name="final",
    )(tok, weight, jnp.asarray(rim_index), *grads, *arrived)

    pieces = []
    for j in range(3):
        for g, heads in enumerate(GROUPS):
            width = len(heads) * HEAD
            pieces.append(reduced[g][:, j * width : (j + 1) * width])
    total = jnp.concatenate(pieces, axis=1)
    for bit in range((n_sample - 1).bit_length() - 1, 0, -1):
        half = total.shape[1] // 2
        upper = ((member >> bit) & 1) == 1
        mine = jnp.where(upper, total[:, half:], total[:, :half])
        other = jnp.where(upper, total[:, :half], total[:, half:])
        total = mine + swap(other.astype(BF16), "sample", bit).astype(F32)
    half = total.shape[1] // 2
    upper = (member & 1) == 1
    mine = jnp.where(upper, total[:, half:], total[:, :half])
    other = jnp.where(upper, total[:, :half], total[:, half:])
    got = swap(other, "sample", 0)
    weight_grad = jnp.where(
        upper, jnp.concatenate([got, mine], axis=0), jnp.concatenate([mine, got], axis=0)
    )
    attention = jnp.concatenate(atts, axis=1)[None, None]
    return (attention, token_grad[None, None], weight_grad)


def solution(mesh):
    return jax.shard_map(
        local,
        mesh=mesh,
        in_specs=(
            P(("groups", "sample"), "space", None, None),
            P(("groups", "sample"), "space", None, None),
            P("groups", None),
            P(("groups", "sample"), None),
        ),
        out_specs=(
            P(("groups", "sample"), "space", None, None),
            P(("groups", "sample"), "space", None, None),
            P(("groups", "space"), "sample"),
        ),
        check_vma=False,
    )
```

time: 306 us -> 82.2 us (0.27); the launches traced: 302 us -> 81.6 us
  matrix products: 106 us -> 0 us
  local copies, waits for them, and re-layouts: 60.1 us -> 11.6 us
  waiting for transfers between devices: 57.2 us -> 12.4 us
  Pallas kernels: 0 us -> 24.2 us
  other arithmetic: 31.9 us -> 8.47 us
  between operations: 16 us -> 2.21 us
  starting transfers between devices: 30.8 us -> 22.8 us
    dot_general x51 -> x0, matrix products: 106 us -> none  [the longest x8 21.5 us: head_pass(): lax.dot_general(query_head, key_head, contract_last, preferred_element_ty...]
    reduce_scatter x2 -> x0, waiting for transfers between devices: 57.1 us -> none  [the longest x1 36.2 us: local(): lax.psum_scatter(weight_sum, 'sample', scatter_dimension=1, tiled=True)]
    pallas_call x0 -> x5, Pallas kernels: none -> 24.2 us  [the longest x2 18.7 us: local(): pl.pallas_call(functools.partial(kernel_attend, heads, g == 0, spans), ou...]
    scatter x9 -> x0, local copies, waits for them, and re-layouts: 16.5 us -> none  [the longest x8 14.9 us: gather_direct(): window = window.at[win_lo:win_hi, wcol_lo:wcol_hi].set(arrived)]
    another operation x12 -> x0, other arithmetic: 15.6 us -> none
    scatter-add x6 -> x0, local copies, waits for them, and re-layouts: 14.6 us -> none  [return_direct(): own_grad = own_grad.at[row_lo:row_hi, col_lo:col_hi].add(arrived)]
    ppermute x16 -> x12, waiting for transfers between devices: 0.04 us -> 12.4 us  [the longest x8 12.4 us: swap(): return lax.ppermute(value, axis, [(i, i ^ 1 << bit) for i in range(count)])]
    while x3 -> x0, local copies, waits for them, and re-layouts: 8.09 us -> none  [tile_pass(): return lax.fori_loop(0, HEADS, one_head, start_carry)]
  transfers between devices with their start and end apart: 18 -> 12, of which waited for: 2 -> 4; matrix products, arithmetic and copies ran while one was open for 21% -> 12% of each run, Pallas kernels for 0% -> 5%
where the time goes in v1:
time: 82.2 us; the launch traced here: 81.6 us
  Pallas kernels  24.2 us (29%)
  starting transfers between devices  22.8 us (28%)
  waiting for transfers between devices  12.4 us (15%)
  local copies, waits for them, and re-layouts  11.6 us (14%)
  other arithmetic  8.47 us (10%)
  between operations  2.21 us (3%)
    pallas_call x2, Pallas kernels, local(): pl.pallas_call(functools.partial(kernel_attend, heads, g == 0, spans), ou...  18.7 us
    ppermute x8, waiting for transfers between devices, swap(): return lax.ppermute(value, axis, [(i, i ^ 1 << bit) for i in range(count)])  12.4 us
    ppermute x4, starting transfers between devices, shift(): lax.ppermute(value, axis, [(i, i + steps) for i in range(first, last)])  12.2 us
    ppermute x8, starting transfers between devices, swap(): return lax.ppermute(value, axis, [(i, i ^ 1 << bit) for i in range(count)])  10.6 us
    unnamed x48, local copies, waits for them, and re-layouts  7.49 us
    pallas_call x1, Pallas kernels, local(): pl.pallas_call(functools.partial(kernel_own, bits), out_shape=(struct((TO...  2.2 us
    pallas_call x1, Pallas kernels, local(): pl.pallas_call(functools.partial(kernel_final, len(GROUPS), len(steps)),...  2.15 us
    add x2, other arithmetic, local(): total = keep + swap(send, 'sample', 0).astype(F32)  2.12 us
  transfers between devices with their start and end apart: 12, of which 4 were waited for; matrix products, arithmetic and copies ran while one was open for 12% of the time, Pallas kernels for 5%

profile of v1, /device:TPU:0, one launch (start us, length us, event | category | flops | bytes accessed | tf_op | source)
XLA Modules:
  0.0 81.6 jit_solution(15463595879248417998)
XLA Ops:
  0.6 1.0 %fusion.1 = (bf16[16,3,512]{2,1,0:T(4,128)(2,1)S(1)}, bf16[16,3,512]{2,1,0:T(4,128)(2,1)S(1)}) fusion(bf16[16,32,512]{2,1,0:T(8,128)(2,1)} %bitcast.19), kind=kLoop, calls=%fused_computation.20 | loop fusion | bytes 196608 | tf_op jit(solution)/shard_map/slice | solution.py:284
  1.7 4.9 %collective-permute-start = (bf16[48,512]{1,0:T(8,128)(2,1)S(1)}, bf16[48,512]{1,0:T(8,128)(2,1)S(1)}, u32[]{:S(2)}, u32[]{:S(2)}) collective-permute-start(bf16[48,512]{1,0:T(8,128)(2,1)S(1)} %reshape.26), channel_id=1, source_target_pairs={{0,4},{4,8},{8,12},{1,5},{5,9},{9,13},{2,6},{6,10},{10,14},{3,7},{... | collective-permute-start | bytes 147464 | tf_op jit(solution)/shard_map/ppermute | solution.py:218
  6.7 1.3 %collective-permute-start.1 = (bf16[48,512]{1,0:T(8,128)(2,1)S(1)}, bf16[48,512]{1,0:T(8,128)(2,1)S(1)}, u32[]{:S(2)}, u32[]{:S(2)}) collective-permute-start(bf16[48,512]{1,0:T(8,128)(2,1)S(1)} %reshape.27), channel_id=1, source_target_pairs={{4,0},{8,4},{12,8},{5,1},{9,5},{13,9},{6,2},{10,6},{14,10},{7,3},{... | collective-permute-start | bytes 147464 | tf_op jit(solution)/shard_map/ppermute | solution.py:218
  8.0 1.5 %fusion.4 = (s32[1,1]{1,0:T(1,128)}, s32[1,1]{1,0:T(1,128)}, s32[1,1]{1,0:T(1,128)}, s32[1,1]{1,0:T(1,128)}) fusion(s32[1,4]{1,0:T(1,128)} %param.11), kind=kLoop, calls=%fused_computation.23 | loop fusion | bytes 32 | tf_op jit(solution)/shard_map/slice | solution.py:298
  10.6 1.3 %stack.23.scal_ref = s32[7]{0:T(128)S(1)} concatenate(s32[1]{0:T(128)} %bitcast, s32[1]{0:T(128)} %bitcast.1, s32[1]{0:T(128)} %bitcast.2, s32[1]{0:T(128)} %bitcast.3, s32[1]{0:T(128)} %bitcast.4, s32[1]{0:T(128)} %bitcast.5, s32[1]{0:T(128)} %bitcast.6), dimensions={0} | concatenate | bytes 56 | tf_op jit(solution)/shard_map/stack | solution.py:290
  11.9 1.9 %fusion = f32[128]{0:T(128)S(1)} fusion(s32[128,1]{0,1:T(1,128)} %constant.61.clone, pred[128,1]{0,1:T(4,128)(4,1)} %constant.62.clone, s32[128,1]{0,1:T(1,128)} %constant.60.clone, s32[]{:T(128)} %bitcast.12, s32[]{:T(128)} %bitcast.11, s32[]{:T(128)} %bitcast.10, s32[]{:T(128)} %bitcast.9, s32[]{:T(128)} %mul.13, s32[]{:T(128)} %mul.12), kind=kLoop, calls=%fused_computation.19 | loop fusion | flops 2432 | bytes 1688 | tf_op jit(solution)/shard_map/broadcast_in_dim | solution.py:307
  13.9 1.4 %copy-done = bf16[512,1536]{1,0:T(8,128)(2,1)S(1)} copy-done((bf16[512,1536]{1,0:T(8,128)(2,1)S(1)}, bf16[512,1536]{1,0:T(8,128)(2,1)}, u32[]{:S(2)}) %copy-start) | copy-done | bytes 1572888
  15.3 1.0 %copy-done.2 = bf16[1,1,512,512]{3,2,1,0:T(8,128)(2,1)S(1)} copy-done((bf16[1,1,512,512]{3,2,1,0:T(8,128)(2,1)S(1)}, bf16[1,1,512,512]{3,2,1,0:T(8,128)(2,1)}, u32[]{:S(2)}) %copy-start.2) | copy-done | bytes 524312
  16.3 2.2 %own.1 = (bf16[512,512]{1,0:T(8,128)(2,1)S(1)}, bf16[512,1024]{1,0:T(8,128)(2,1)S(1)}, bf16[1024,512]{1,0:T(8,128)(2,1)S(1)}, bf16[512,512]{1,0:T(8,128)(2,1)S(1)}, f32[512,512]{1,0:T(8,128)S(1)}) custom-call(s32[7]{0:T(128)S(1)} %stack.23.scal_ref, bf16[512,512]{1,0:T(8,128)(2,1)S(1)} %bitcast.20, bf16[512,1536]{1,0:T(8,128)(2,1)S(1)} %copy-done), custom_call_target="tpu_custom_call" | custom-call | flops 1073741824 | bytes 7000000 | tf_op jit(solution)/shard_map/own/pallas_call | solution.py:309
  18.6 1.2 %halo.1 = (bf16[128,1024]{1,0:T(8,128)(2,1)S(1)}, bf16[1024,128]{1,0:T(8,128)(2,1)S(1)}, bf16[512,128]{1,0:T(8,128)(2,1)S(1)}) custom-call(s32[7]{0:T(128)S(1)} %stack.23.scal_ref, bf16[48,512]{1,0:T(8,128)(2,1)S(1)} %collective-permute-done.refs_0_, bf16[48,512]{1,0:T(8,128)(2,1)S(1)} %collective-permute-done.1.refs_1_, bf16[512,1536]{1,0:T(8,128)(2,1)S(1)} %copy-done.1), custom_call_target="tpu_custom_call" | custom-call | flops 201326592 | bytes 2000000 | tf_op jit(solution)/shard_map/halo/pallas_call | solution.py:325
  19.8 9.3 %attend0.1 = (bf16[512,256]{1,0:T(8,128)(2,1)S(1)}, bf16[512,256]{1,0:T(8,128)(2,1)S(1)}, bf16[512,256]{1,0:T(8,128)(2,1)S(1)}, bf16[512,256]{1,0:T(8,128)(2,1)S...) custom-call(bf16[512,512]{1,0:T(8,128)(2,1)S(1)} %get-tuple-element.26.refs_0_, ...), custom_call_target="tpu_custom_call" | custom-call | flops 4026531840 | bytes 6000000 | tf_op jit(solution)/shard_map/attend0/pallas_call | solution.py:347
  29.1 0.7 copy-done.4
  29.8 0.7 copy-done.6
  30.5 0.7 copy-done.14
  31.2 9.4 %attend1.1 = (bf16[512,256]{1,0:T(8,128)(2,1)S(1)}, bf16[512,256]{1,0:T(8,128)(2,1)S(1)}, bf16[512,256]{1,0:T(8,128)(2,1)S(1)}, bf16[512,256]{1,0:T(8,128)(2,1)S...) custom-call(bf16[512,512]{1,0:T(8,128)(2,1)S(1)} %get-tuple-element., ...), custom_call_target="tpu_custom_call" | custom-call | flops 4026531840 | bytes 6000000 | tf_op jit(solution)/shard_map/attend1/pallas_call | solution.py:347
  40.6 0.7 copy-done.8
  42.8 0.7 copy-done.15
  44.0 1.6 %collective-permute-done.4 = bf16[256,768]{1,0:T(8,128)(2,1)} collective-permute-done((bf16[256,768]{1,0:T(8,128)(2,1)}, bf16[256,768]{1,0:T(8,128)(2,1)}, u32[]{:S(2)}, u32[]{:S(2)}) %collective-permute-start.4) | collective-permute-done | bytes 393248 | tf_op jit(solution)/shard_map/ppermute | solution.py:223
  45.6 1.1 %convert_add_fusion.1 = f32[256,768]{1,0:T(8,128)S(1)} fusion(f32[256,768]{1,0:T(8,128)S(1)} %get-tuple-element.45, bf16[256,768]{1,0:T(8,128)(2,1)} %collective-permute-done.4), kind=kLoop, calls=%fused_computation.1 | loop fusion | flops 393216 | bytes 1966080 | tf_op jit(solution)/shard_map/add | solution.py:375
  46.7 2.7 %collective-permute-start.5 = (bf16[128,768]{1,0:T(8,128)(2,1)S(1)}, bf16[128,768]{1,0:T(8,128)(2,1)S(1)}, u32[]{:S(2)}, u32[]{:S(2)}) collective-permute-start(bf16[128,768]{1,0:T(8,128)(2,1)S(1)} %slice.145), channel_id=1, source_target_pairs={{0,4},{4,0},{8,12},{12,8},{1,5},{5,1},{9,13},{13,9},{2,6},{6,2},{1... | collective-permute-start | bytes 589832 | tf_op jit(solution)/shard_map/ppermute | solution.py:223
  49.4 1.1 %convert_add_fusion = f32[256,768]{1,0:T(8,128)S(1)} fusion(f32[256,768]{1,0:T(8,128)S(1)} %get-tuple-element.47, bf16[256,768]{1,0:T(8,128)(2,1)} %collective-permute-done.7), kind=kLoop, calls=%fused_computation | loop fusion | flops 393216 | bytes 1966080 | tf_op jit(solution)/shard_map/add | solution.py:375
  50.6 4.5 %collective-permute-done.5 = bf16[128,768]{1,0:T(8,128)(2,1)S(1)} collective-permute-done((bf16[128,768]{1,0:T(8,128)(2,1)S(1)}, bf16[128,768]{1,0:T(8,128)(2,1)S(1)}, u32[]{:S(2)}, u32[]{:S(2)}) %collective-permute-start.5) | collective-permute-done | bytes 196640 | tf_op jit(solution)/shard_map/ppermute | solution.py:223
  55.1 3.1 %collective-permute-start.6 = (bf16[64,768]{1,0:T(8,128)(2,1)S(1)}, bf16[64,768]{1,0:T(8,128)(2,1)S(1)}, u32[]{:S(2)}, u32[]{:S(2)}) collective-permute-start(bf16[64,768]{1,0:T(8,128)(2,1)S(1)} %slice.147), channel_id=1, source_target_pairs={{0,8},{4,12},{8,0},{12,4},{1,9},{5,13},{9,1},{13,5},{2,10},{6,14},... | collective-permute-start | bytes 294920 | tf_op jit(solution)/shard_map/ppermute | solution.py:223
  58.3 1.6 %collective-permute-done.8 = bf16[128,768]{1,0:T(8,128)(2,1)S(1)} collective-permute-done((bf16[128,768]{1,0:T(8,128)(2,1)S(1)}, bf16[128,768]{1,0:T(8,128)(2,1)S(1)}, u32[]{:S(2)}, u32[]{:S(2)}) %collective-permute-start.8) | collective-permute-done | bytes 196640 | tf_op jit(solution)/shard_map/ppermute | solution.py:223
  59.9 2.6 %collective-permute-start.9 = (bf16[64,768]{1,0:T(8,128)(2,1)S(1)}, bf16[64,768]{1,0:T(8,128)(2,1)S(1)}, u32[]{:S(2)}, u32[]{:S(2)}) collective-permute-start(bf16[64,768]{1,0:T(8,128)(2,1)S(1)} %slice.146), channel_id=1, source_target_pairs={{0,8},{4,12},{8,0},{12,4},{1,9},{5,13},{9,1},{13,5},{2,10},{6,14},... | collective-permute-start | bytes 294920 | tf_op jit(solution)/shard_map/ppermute | solution.py:223
  62.6 4.8 %collective-permute-done.9 = bf16[64,768]{1,0:T(8,128)(2,1)S(1)} collective-permute-done((bf16[64,768]{1,0:T(8,128)(2,1)S(1)}, bf16[64,768]{1,0:T(8,128)(2,1)S(1)}, u32[]{:S(2)}, u32[]{:S(2)}) %collective-permute-start.9) | collective-permute-done | bytes 98336 | tf_op jit(solution)/shard_map/ppermute | solution.py:223
  68.2 1.5 %collective-permute-start.10 = (bf16[64,768]{1,0:T(8,128)(2,1)}, bf16[64,768]{1,0:T(8,128)(2,1)}, u32[]{:S(2)}, u32[]{:S(2)}) collective-permute-start(bf16[64,768]{1,0:T(8,128)(2,1)} %select_convert_fusion), channel_id=1, source_target_pairs={{0,2},{1,3},{2,0},{3,1},{4,6},{5,7},{6,4},{7,5},{8,10},{9,11},{10,... | collective-permute-start | bytes 294920 | tf_op jit(solution)/shard_map/ppermute | solution.py:223
  69.7 1.4 %collective-permute-start.2 = (bf16[48,512]{1,0:T(8,128)(2,1)S(1)}, bf16[48,512]{1,0:T(8,128)(2,1)S(1)}, u32[]{:S(2)}, u32[]{:S(2)}) collective-permute-start(bf16[48,512]{1,0:T(8,128)(2,1)S(1)} %get-tuple-element.43), channel_id=1, source_target_pairs={{4,0},{8,4},{12,8},{5,1},{9,5},{13,9},{6,2},{10,6},{14,10},{7,3},{... | collective-permute-start | bytes 147464 | tf_op jit(solution)/shard_map/ppermute | solution.py:218
  71.1 4.5 %collective-permute-start.3 = (bf16[48,512]{1,0:T(8,128)(2,1)S(1)}, bf16[48,512]{1,0:T(8,128)(2,1)S(1)}, u32[]{:S(2)}, u32[]{:S(2)}) collective-permute-start(bf16[48,512]{1,0:T(8,128)(2,1)S(1)} %get-tuple-element.44), channel_id=1, source_target_pairs={{0,4},{4,8},{8,12},{1,5},{5,9},{9,13},{2,6},{6,10},{10,14},{3,7},{... | collective-permute-start | bytes 147464 | tf_op jit(solution)/shard_map/ppermute | solution.py:218
  75.7 1.1 %convert_add_fusion.2 = f32[64,768]{1,0:T(8,128)S(1)} fusion(bf16[64,768]{1,0:T(8,128)(2,1)} %collective-permute-done.10, f32[64,256]{1,0:T(8,128)} %copy-done.22, f32[64,256]{1,0:T(8,128)} %copy-done.19, f32[64,256]{1,0:T(8,128)} %copy-done.23, f32[64,256]{1,0:T(8,128)} %copy-done.20, f32[64,256]{1,0:T(8,128)} %copy-done.21, f32[64,256]{1,0:T(8,128)} %copy-done.18, ...), kind=kLoop, calls=%fused_computation.14 | loop fusion | flops 344064 | bytes 688129 | tf_op jit(solution)/shard_map/add | solution.py:407
  76.9 1.9 %maximum_bitcast_fusion = bf16[1,1,512,512]{3,2,1,0:T(8,128)(2,1)} fusion(bf16[512,256]{1,0:T(8,128)(2,1)} %copy-done.15, bf16[512,256]{1,0:T(8,128)(2,1)} %copy-done.14), kind=kLoop, calls=%fused_computation.2 | loop fusion | flops 1048576 | bytes 1048576 | tf_op jit(solution)/shard_map/broadcast_in_dim | solution.py:416
  78.8 2.1 %final.1 = bf16[512,512]{1,0:T(8,128)(2,1)} custom-call(bf16[512,512]{1,0:T(8,128)(2,1)S(1)} %bitcast.21, bf16[512,1536]{1,0:T(8,128)(2,1)S(1)} %copy-done.1, s32[1,128]{1,0:T(1,128)S(1)} %copy-done.16, bf16[512,256]{1,0:T(8,128)(2,1)S(1)} %get-tuple-element.37.refs_0_, bf16[512,256]{1,0:T(8,128)(2,1)S(1)} %copy-done.5, bf16[512,256]{1,0:T(8,128)(2,1)S(1)} %copy-done.7, ...), custom_call_target="tpu_custom_call" | custom-call | flops 805306368 | bytes 5000000 | tf_op jit(solution)/shard_map/final/pallas_call | solution.py:386
  (69 shorter events, 3.9 us)
Async XLA Ops:
  1.7 16.8 %collective-permute-start = (bf16[48,512]{1,0:T(8,128)(2,1)S(1)}, bf16[48,512]{1,0:T(8,128)(2,1)S(1)}, u32[]{:S(2)}, u32[]{:S(2)}) collective-permute-start(bf16[48,512]{1,0:T(8,128)(2,1)S(1)} %reshape.26), channel_id=1, source_target_pairs={{0,4},{4,8},{8,12},{1,5},{5,9},{9,13},{2,6},{6,10},{10,14},{3,7},{... | collective-permute-start | bytes 147464 | tf_op jit(solution)/shard_map/ppermute | solution.py:218
  6.7 11.8 %collective-permute-start.1 = (bf16[48,512]{1,0:T(8,128)(2,1)S(1)}, bf16[48,512]{1,0:T(8,128)(2,1)S(1)}, u32[]{:S(2)}, u32[]{:S(2)}) collective-permute-start(bf16[48,512]{1,0:T(8,128)(2,1)S(1)} %reshape.27), channel_id=1, source_target_pairs={{4,0},{8,4},{12,8},{5,1},{9,5},{13,9},{6,2},{10,6},{14,10},{7,3},{... | collective-permute-start | bytes 147464 | tf_op jit(solution)/shard_map/ppermute | solution.py:218
  13.9 1.4 %copy-start = (bf16[512,1536]{1,0:T(8,128)(2,1)S(1)}, bf16[512,1536]{1,0:T(8,128)(2,1)}, u32[]{:S(2)}) copy-start(bf16[512,1536]{1,0:T(8,128)(2,1)} %w_ref.3) | copy-start | bytes 4718596
  15.3 1.0 %copy-start.2 = (bf16[1,1,512,512]{3,2,1,0:T(8,128)(2,1)S(1)}, bf16[1,1,512,512]{3,2,1,0:T(8,128)(2,1)}, u32[]{:S(2)}) copy-start(bf16[1,1,512,512]{3,2,1,0:T(8,128)(2,1)} %param.8) | copy-start | bytes 1572868
  16.3 2.2 %copy-start.1 = (bf16[512,1536]{1,0:T(8,128)(2,1)S(1)}, bf16[512,1536]{1,0:T(8,128)(2,1)}, u32[]{:S(2)}) copy-start(bf16[512,1536]{1,0:T(8,128)(2,1)} %w_ref.3) | copy-start | bytes 4718596
  18.5 1.3 %copy-start.17 = (bf16[1,1,512,512]{3,2,1,0:T(8,128)(2,1)S(1)}, bf16[1,1,512,512]{3,2,1,0:T(8,128)(2,1)}, u32[]{:S(2)}) copy-start(bf16[1,1,512,512]{3,2,1,0:T(8,128)(2,1)} %param.9) | copy-start | bytes 1572868
  29.8 0.7 copy-start.6
  30.5 0.7 copy-start.14
  40.6 0.7 copy-start.8
  42.8 0.7 copy-start.15
  43.5 2.1 %collective-permute-start.4 = (bf16[256,768]{1,0:T(8,128)(2,1)}, bf16[256,768]{1,0:T(8,128)(2,1)}, u32[]{:S(2)}, u32[]{:S(2)}) collective-permute-start(bf16[256,768]{1,0:T(8,128)(2,1)} %get-tuple-element.46), channel_id=1, source_target_pairs={{0,1},{1,0},{2,3},{3,2},{4,5},{5,4},{6,7},{7,6},{8,9},{9,8},{10,11... | collective-permute-start | bytes 1179656 | tf_op jit(solution)/shard_map/ppermute | solution.py:223
  43.5 5.9 %collective-permute-start.7 = (bf16[256,768]{1,0:T(8,128)(2,1)}, bf16[256,768]{1,0:T(8,128)(2,1)}, u32[]{:S(2)}, u32[]{:S(2)}) collective-permute-start(bf16[256,768]{1,0:T(8,128)(2,1)} %get-tuple-element.48), channel_id=1, source_target_pairs={{0,1},{1,0},{2,3},{3,2},{4,5},{5,4},{6,7},{7,6},{8,9},{9,8},{10,11... | collective-permute-start | bytes 1179656 | tf_op jit(solution)/shard_map/ppermute | solution.py:223
  46.7 8.4 %collective-permute-start.5 = (bf16[128,768]{1,0:T(8,128)(2,1)S(1)}, bf16[128,768]{1,0:T(8,128)(2,1)S(1)}, u32[]{:S(2)}, u32[]{:S(2)}) collective-permute-start(bf16[128,768]{1,0:T(8,128)(2,1)S(1)} %slice.145), channel_id=1, source_target_pairs={{0,4},{4,0},{8,12},{12,8},{1,5},{5,1},{9,13},{13,9},{2,6},{6,2},{1... | collective-permute-start | bytes 589832 | tf_op jit(solution)/shard_map/ppermute | solution.py:223
  50.5 9.4 %collective-permute-start.8 = (bf16[128,768]{1,0:T(8,128)(2,1)S(1)}, bf16[128,768]{1,0:T(8,128)(2,1)S(1)}, u32[]{:S(2)}, u32[]{:S(2)}) collective-permute-start(bf16[128,768]{1,0:T(8,128)(2,1)S(1)} %slice.144), channel_id=1, source_target_pairs={{0,4},{4,0},{8,12},{12,8},{1,5},{5,1},{9,13},{13,9},{2,6},{6,2},{1... | collective-permute-start | bytes 589832 | tf_op jit(solution)/shard_map/ppermute | solution.py:223
  55.1 7.4 %collective-permute-start.6 = (bf16[64,768]{1,0:T(8,128)(2,1)S(1)}, bf16[64,768]{1,0:T(8,128)(2,1)S(1)}, u32[]{:S(2)}, u32[]{:S(2)}) collective-permute-start(bf16[64,768]{1,0:T(8,128)(2,1)S(1)} %slice.147), channel_id=1, source_target_pairs={{0,8},{4,12},{8,0},{12,4},{1,9},{5,13},{9,1},{13,5},{2,10},{6,14},... | collective-permute-start | bytes 294920 | tf_op jit(solution)/shard_map/ppermute | solution.py:223
  59.9 7.4 %collective-permute-start.9 = (bf16[64,768]{1,0:T(8,128)(2,1)S(1)}, bf16[64,768]{1,0:T(8,128)(2,1)S(1)}, u32[]{:S(2)}, u32[]{:S(2)}) collective-permute-start(bf16[64,768]{1,0:T(8,128)(2,1)S(1)} %slice.146), channel_id=1, source_target_pairs={{0,8},{4,12},{8,0},{12,4},{1,9},{5,13},{9,1},{13,5},{2,10},{6,14},... | collective-permute-start | bytes 294920 | tf_op jit(solution)/shard_map/ppermute | solution.py:223
  62.5 4.9 %copy-start.18 = (f32[64,256]{1,0:T(8,128)}, f32[64,256]{1,0:T(8,128)S(1)}, u32[]{:S(2)}) copy-start(f32[64,256]{1,0:T(8,128)S(1)} %get-tuple-element.53) | copy-start | bytes 196612
  62.5 5.6 %copy-start.19 = (f32[64,256]{1,0:T(8,128)}, f32[64,256]{1,0:T(8,128)S(1)}, u32[]{:S(2)}) copy-start(f32[64,256]{1,0:T(8,128)S(1)} %get-tuple-element.54) | copy-start | bytes 196612
  62.6 5.6 %copy-start.20 = (f32[64,256]{1,0:T(8,128)}, f32[64,256]{1,0:T(8,128)S(1)}, u32[]{:S(2)}) copy-start(f32[64,256]{1,0:T(8,128)S(1)} %get-tuple-element.55) | copy-start | bytes 196612
  67.3 11.4 %copy-start.3 = (bf16[1,1,512,512]{3,2,1,0:T(8,128)(2,1)S(1)}, bf16[1,1,512,512]{3,2,1,0:T(8,128)(2,1)}, u32[]{:S(2)}) copy-start(bf16[1,1,512,512]{3,2,1,0:T(8,128)(2,1)} %param.8) | copy-start | bytes 1572868
  67.3 11.4 %copy-start.5 = (bf16[512,256]{1,0:T(8,128)(2,1)S(1)}, bf16[512,256]{1,0:T(8,128)(2,1)}, u32[]{:S(2)}) copy-start(bf16[512,256]{1,0:T(8,128)(2,1)} %copy-done.4) | copy-start | bytes 786436
  67.4 11.4 %copy-start.7 = (bf16[512,256]{1,0:T(8,128)(2,1)S(1)}, bf16[512,256]{1,0:T(8,128)(2,1)}, u32[]{:S(2)}) copy-start(bf16[512,256]{1,0:T(8,128)(2,1)} %copy-done.6) | copy-start | bytes 786436
  67.4 11.4 %copy-start.9 = (bf16[512,256]{1,0:T(8,128)(2,1)S(1)}, bf16[512,256]{1,0:T(8,128)(2,1)}, u32[]{:S(2)}) copy-start(bf16[512,256]{1,0:T(8,128)(2,1)} %copy-done.8) | copy-start | bytes 786436
  67.4 11.4 %copy-start.11 = (bf16[512,256]{1,0:T(8,128)(2,1)S(1)}, bf16[512,256]{1,0:T(8,128)(2,1)}, u32[]{:S(2)}) copy-start(bf16[512,256]{1,0:T(8,128)(2,1)} %copy-done.10) | copy-start | bytes 786436
  67.4 11.4 %copy-start.16 = (s32[1,128]{1,0:T(1,128)S(1)}, s32[1,128]{1,0:T(1,128)}, u32[]{:S(2)}) copy-start(s32[1,128]{1,0:T(1,128)} %constant.63.clone.index_ref) | copy-start | bytes 1540
  67.4 0.7 copy-start.21
  67.4 0.7 copy-start.22
  68.2 7.5 %collective-permute-start.10 = (bf16[64,768]{1,0:T(8,128)(2,1)}, bf16[64,768]{1,0:T(8,128)(2,1)}, u32[]{:S(2)}, u32[]{:S(2)}) collective-permute-start(bf16[64,768]{1,0:T(8,128)(2,1)} %select_convert_fusion), channel_id=1, source_target_pairs={{0,2},{1,3},{2,0},{3,1},{4,6},{5,7},{6,4},{7,5},{8,10},{9,11},{10,... | collective-permute-start | bytes 294920 | tf_op jit(solution)/shard_map/ppermute | solution.py:223
  69.7 9.1 %copy-start.13 = (bf16[512,256]{1,0:T(8,128)(2,1)S(1)}, bf16[512,256]{1,0:T(8,128)(2,1)}, u32[]{:S(2)}) copy-start(bf16[512,256]{1,0:T(8,128)(2,1)} %copy-done.12) | copy-start | bytes 786436
  69.7 9.0 %collective-permute-start.2 = (bf16[48,512]{1,0:T(8,128)(2,1)S(1)}, bf16[48,512]{1,0:T(8,128)(2,1)S(1)}, u32[]{:S(2)}, u32[]{:S(2)}) collective-permute-start(bf16[48,512]{1,0:T(8,128)(2,1)S(1)} %get-tuple-element.43), channel_id=1, source_target_pairs={{4,0},{8,4},{12,8},{5,1},{9,5},{13,9},{6,2},{10,6},{14,10},{7,3},{... | collective-permute-start | bytes 147464 | tf_op jit(solution)/shard_map/ppermute | solution.py:218
  71.1 7.6 %collective-permute-start.3 = (bf16[48,512]{1,0:T(8,128)(2,1)S(1)}, bf16[48,512]{1,0:T(8,128)(2,1)S(1)}, u32[]{:S(2)}, u32[]{:S(2)}) collective-permute-start(bf16[48,512]{1,0:T(8,128)(2,1)S(1)} %get-tuple-element.44), channel_id=1, source_target_pairs={{0,4},{4,8},{8,12},{1,5},{5,9},{9,13},{2,6},{6,10},{10,14},{3,7},{... | collective-permute-start | bytes 147464 | tf_op jit(solution)/shard_map/ppermute | solution.py:218
  76.8 4.2 %collective-permute-start.11 = (f32[64,384]{1,0:T(8,128)S(1)}, f32[64,384]{1,0:T(8,128)S(1)}, u32[]{:S(2)}, u32[]{:S(2)}) collective-permute-start(f32[64,384]{1,0:T(8,128)S(1)} %get-tuple-element.51), channel_id=1, source_target_pairs={{0,1},{1,0},{2,3},{3,2},{4,5},{5,4},{6,7},{7,6},{8,9},{9,8},{10,11... | collective-permute-start | bytes 294920 | tf_op jit(solution)/shard_map/ppermute | solution.py:223
  (4 other events, 2.8 us)

commit v2 on v1

v2 whole, which is shorter than its diff:
```python
import functools
import math

import jax
import jax.numpy as jnp
import numpy as np
from jax import lax
from jax.experimental import pallas as pl
from jax.experimental.pallas import tpu as pltpu
from jax.sharding import PartitionSpec as P

HEADS = 8
HEAD = 64
TH = 16
TW = 32
HALO = 3
TOKENS = TH * TW
NEG = -1e30
LAST = (((1,), (1,)), ((), ()))
F32 = jnp.float32
BF16 = jnp.bfloat16
CHUNK = 256
ROWS = 64

vmem = functools.partial(pl.BlockSpec, memory_space=pltpu.VMEM)
smem = functools.partial(pl.BlockSpec, memory_space=pltpu.SMEM)


def params():
    return pltpu.CompilerParams(vmem_limit_bytes=24 * 1024 * 1024)


def dot(a, b):
    return jnp.dot(a, b, preferred_element_type=F32)


def dot_t(a, b):
    return lax.dot_general(a, b, LAST, preferred_element_type=F32)


def normalise(tok):
    tok = tok.astype(F32)
    centred = tok - jnp.mean(tok, axis=-1, keepdims=True)
    inv = lax.rsqrt(jnp.mean(centred * centred, axis=-1, keepdims=True) + 1e-05)
    return centred * inv, inv


def own_ids(cols):
    position = lax.axis_index("space")
    member = lax.axis_index("sample")
    return position, member, position // cols, position % cols


def live(row, col, margin_ref, rows, cols):
    return (
        (row >= margin_ref[0, 0])
        & (row < rows - margin_ref[0, 1])
        & (col >= margin_ref[0, 2])
        & (col < cols - margin_ref[0, 3])
    )


def permutation(feat, n_space, position, member):
    bits = (n_space - 1).bit_length()
    size = feat // (4 * n_space)
    row = lax.broadcasted_iota(jnp.int32, (feat, feat), 0)
    col = lax.broadcasted_iota(jnp.int32, (feat, feat), 1)
    relative = row // size
    space = jnp.zeros_like(row)
    for i in range(bits):
        space = space | (((relative >> (bits - 1 - i)) & 1) << i)
    space = space ^ position
    part = (relative >> bits) & 1
    half = (relative >> (bits + 1)) ^ (member & 1)
    source = ((space * 2 + half) * 2 + part) * size + row % size
    return jnp.where(col == source, 1.0, 0.0).astype(BF16)


def kernel_own(sizes, margin_ref, tok_ref, w_ref, q_ref, kv_ref, kvt_ref, nt_ref, bias_ref):
    n_space, grid_cols, plane_rows, plane_cols = sizes
    position, member, tile_row, tile_col = own_ids(grid_cols)
    feat = w_ref.shape[0]
    standard, _ = normalise(tok_ref[...])
    normed = standard.astype(BF16)
    scale = 1.0 / math.sqrt(HEAD)
    q_ref[...] = (dot(normed, w_ref[:, :feat]).astype(BF16).astype(F32) * scale).astype(BF16)
    for i in range(2):
        part = dot(normed, w_ref[:, (i + 1) * feat : (i + 2) * feat]).astype(BF16)
        kv_ref[:TOKENS, i * feat : (i + 1) * feat] = part
        kvt_ref[i * feat : (i + 1) * feat, :TOKENS] = part.T
    nt_ref[:, :TOKENS] = dot_t(permutation(feat, n_space, position, member), normed).astype(BF16)
    key = lax.broadcasted_iota(jnp.int32, (TOKENS, TOKENS), 0)
    query = lax.broadcasted_iota(jnp.int32, (TOKENS, TOKENS), 1)
    row = tile_row * TH + key // TW
    col = tile_col * TW + key % TW
    is_open = live(row, col, margin_ref, plane_rows, plane_cols) | (key == query)
    bias_ref[:TOKENS, :] = jnp.where(is_open, 0.0, NEG)


def kernel_attend(sizes, n_sample, spans, margin_ref, coord_ref, q_ref, cot_ref, w_ref, *refs):
    n_space, grid_cols, plane_rows, plane_cols = sizes
    count = len(spans)
    toks, refs = refs[:count], refs[count + 4 :]
    kv_ref, kvt_ref, nt_ref, bias_ref, att_ref, gq_ref, gkv_ref, keep_ref, send_ref = refs[:9]
    gnh_refs, refs = refs[9 : 9 + count], refs[9 + count :]
    s_s, g_s, pb_s, ds_s, cm_s, qm_s, att_s, dqt_s, gh_s = refs
    position, member, tile_row, tile_col = own_ids(grid_cols)
    feat = w_ref.shape[0]
    keys = kv_ref.shape[0]
    padded = keys - TOKENS
    scale = 1.0 / math.sqrt(HEAD)

    parts = [r[...].astype(F32) for r in toks]
    if spans[-1][1] < padded:
        parts.append(jnp.zeros((padded - spans[-1][1], feat), F32))
    standard, _ = normalise(jnp.concatenate(parts, axis=0))
    normed = standard.astype(BF16)
    for i in range(2):
        part = dot(normed, w_ref[:, (i + 1) * feat : (i + 2) * feat]).astype(BF16)
        kv_ref[TOKENS:, i * feat : (i + 1) * feat] = part
        kvt_ref[i * feat : (i + 1) * feat, TOKENS:] = part.T
    nt_ref[:, TOKENS:] = dot_t(permutation(feat, n_space, position, member), normed).astype(BF16)
    row = tile_row * TH + coord_ref[:, 0:1]
    col = tile_col * TW + coord_ref[:, 1:2]
    is_open = live(row, col, margin_ref, plane_rows, plane_cols) & (coord_ref[:, 2:3] > 0)
    is_open = is_open & (row >= 0) & (row < plane_rows) & (col >= 0) & (col < plane_cols)
    bias_ref[TOKENS:, :] = jnp.broadcast_to(jnp.where(is_open, 0.0, NEG), (padded, TOKENS))

    lane = lax.broadcasted_iota(jnp.int32, (TOKENS, 2 * HEAD), 1)
    step = 0
    for pair in range(HEADS // 2):
        base = pair * 2 * HEAD
        cols = slice(base, base + 2 * HEAD)
        vcols = slice(feat + base, feat + base + 2 * HEAD)
        q = q_ref[:, cols]
        cot = cot_ref[:, cols]
        zero = jnp.zeros_like(q)
        for odd in range(2):
            mine = (lane >= HEAD) if odd else (lane < HEAD)
            qm_s[odd * TOKENS : (odd + 1) * TOKENS, :] = jnp.where(mine, q, zero)
            cm_s[odd * TOKENS : (odd + 1) * TOKENS, :] = jnp.where(mine, cot, zero)
            krow = base + odd * HEAD
            vrow = feat + krow
            for c in range(TOKENS // CHUNK):
                slot = step % 2
                step += 1
                lanes = slice(c * CHUNK, (c + 1) * CHUNK)
                out = slice(odd * TOKENS + c * CHUNK, odd * TOKENS + (c + 1) * CHUNK)
                s_s[slot] = dot_t(kv_ref[:, cols], qm_s[out, :])
                g_s[slot] = dot_t(kv_ref[:, vcols], cm_s[out, :])
                top = jnp.full((8, CHUNK), NEG, F32)
                for r in range(0, keys, ROWS):
                    x = s_s[slot, r : r + ROWS, :] + bias_ref[r : r + ROWS, lanes]
                    top = jnp.maximum(top, jnp.max(x.reshape(ROWS // 8, 8, CHUNK), axis=0))
                top = jnp.max(top, axis=0, keepdims=True)
                total = jnp.zeros((8, CHUNK), F32)
                delta = jnp.zeros((8, CHUNK), F32)
                for r in range(0, keys, ROWS):
                    x = s_s[slot, r : r + ROWS, :] + bias_ref[r : r + ROWS, lanes]
                    e = jnp.exp(x - top)
                    s_s[slot, r : r + ROWS, :] = e
                    total = total + jnp.sum(e.reshape(ROWS // 8, 8, CHUNK), axis=0)
                    eg = e * g_s[slot, r : r + ROWS, :]
                    delta = delta + jnp.sum(eg.reshape(ROWS // 8, 8, CHUNK), axis=0)
                inv = 1.0 / jnp.sum(total, axis=0, keepdims=True)
                delta = jnp.sum(delta, axis=0, keepdims=True) * inv
                for r in range(0, keys, ROWS):
                    p = s_s[slot, r : r + ROWS, :] * inv
                    pb_s[r : r + ROWS, out] = p.astype(BF16)
                    ds_s[r : r + ROWS, out] = (p * (g_s[slot, r : r + ROWS, :] - delta)).astype(BF16)
                att_s[krow : krow + HEAD, lanes] = dot(kvt_ref[vrow : vrow + HEAD, :], pb_s[:, out])
                dqt_s[krow : krow + HEAD, lanes] = scale * dot(kvt_ref[krow : krow + HEAD, :], ds_s[:, out])
        for source, other, at in ((ds_s, qm_s, base), (pb_s, cm_s, feat + base)):
            grad = dot(source[...], other[...]).astype(BF16)
            gkv_ref[:, at : at + 2 * HEAD] = grad[:TOKENS]
            gh_s[:, at : at + 2 * HEAD] = grad[TOKENS:]

    block = 3 * feat // n_sample

    def store(value, at):
        for i in range(0, value.shape[1], 128):
            b, rest = (at + i) // block, (at + i) % block
            mine = pl.multiple_of((b ^ member) * block + rest, 128)
            theirs = pl.multiple_of((b ^ member ^ 1) * block + rest, 128)
            keep_ref[:, pl.ds(mine, 128)] = value[: feat // 2, i : i + 128]
            send_ref[:, pl.ds(theirs, 128)] = value[feat // 2 :, i : i + 128].astype(BF16)

    wide = 256
    for i in range(0, feat, wide):
        store(dot_t(nt_ref[:, :TOKENS], dqt_s[i : i + wide, :].astype(BF16)), i)
    for i in range(0, 2 * feat, wide):
        store(
            dot(nt_ref[:, :TOKENS], gkv_ref[:, i : i + wide]) + dot(nt_ref[:, TOKENS:], gh_s[:, i : i + wide]),
            feat + i,
        )
    gnh = dot_t(gh_s[...], w_ref[:, feat:])
    for (lo, hi), ref in zip(spans, gnh_refs):
        ref[...] = gnh[lo:hi, :].astype(BF16)
    gq_ref[...] = dqt_s[...].T.astype(BF16)
    att_ref[...] = att_s[...].T.astype(BF16)


def kernel_final(count, tok_ref, w_ref, index_ref, gq_ref, gkv_ref, *refs):
    arrived, out_ref = refs[:count], refs[count]
    feat = w_ref.shape[0]
    total = dot_t(gq_ref[...], w_ref[:, :feat]) + dot_t(gkv_ref[...], w_ref[:, feat:])
    padded = index_ref.shape[1]
    parts = [r[...].astype(F32) for r in arrived]
    have = sum(p.shape[0] for p in parts)
    if have < padded:
        parts.append(jnp.zeros((padded - have, feat), F32))
    rim = jnp.concatenate(parts, axis=0).astype(BF16)
    token = lax.broadcasted_iota(jnp.int32, (TOKENS, padded), 0)
    place = jnp.where(token == index_ref[...], 1.0, 0.0).astype(BF16)
    total = total + dot(place, rim)
    standard, inv = normalise(tok_ref[...])
    mean = jnp.mean(total, axis=-1, keepdims=True)
    cross = jnp.mean(total * standard, axis=-1, keepdims=True)
    out_ref[...] = ((total - mean - standard * cross) * inv).astype(BF16)


def shift(value, axis, steps):
    count = lax.axis_size(axis)
    first, last = max(0, -steps), min(count, count - steps)
    return lax.ppermute(value, axis, [(i, i + steps) for i in range(first, last)])


def swap(value, axis, bit):
    count = lax.axis_size(axis)
    return lax.ppermute(value, axis, [(i, i ^ (1 << bit)) for i in range(count)])


def span(step, length):
    if step < 0:
        return (length - HALO, length)
    if step > 0:
        return (0, HALO)
    return (0, length)


def window_span(step, length):
    if step < 0:
        return (-HALO, 0)
    if step > 0:
        return (length, length + HALO)
    return (0, length)


def struct(shape, dtype):
    return jax.ShapeDtypeStruct(shape, dtype)


def cost(flops, nbytes, exps=0):
    return pl.CostEstimate(flops=int(flops), bytes_accessed=int(nbytes), transcendentals=int(exps))


def halve(keep, send, axis, bit):
    return keep + swap(send.astype(BF16), axis, bit).astype(F32)


def local(tokens, cotangent, weight, margins):
    feat = weight.shape[0]
    tok, cot = tokens[0, 0], cotangent[0, 0]
    n_space, n_sample = lax.axis_size("space"), lax.axis_size("sample")
    grid_cols = min(8, n_space)
    grid_rows = n_space // grid_cols
    sizes = (n_space, grid_cols, grid_rows * TH, grid_cols * TW)
    member = lax.axis_index("sample")
    row_steps = (-1, 0, 1) if grid_rows > 1 else (0,)
    steps = [(r, c) for r in row_steps for c in (-1, 0, 1) if (r, c) != (0, 0)]
    counts, coords, sources = [], [], []
    for r, c in steps:
        rr, cc = np.meshgrid(
            np.arange(*window_span(r, TH)), np.arange(*window_span(c, TW)), indexing="ij"
        )
        coords.append(np.stack([rr.ravel(), cc.ravel(), np.ones(rr.size, np.int64)], axis=1))
        rr, cc = np.meshgrid(np.arange(*span(r, TH)), np.arange(*span(c, TW)), indexing="ij")
        sources.append((rr * TW + cc).ravel())
        counts.append(rr.size)
    halo = sum(counts)
    padded = -(-halo // 128) * 128
    keys = TOKENS + padded
    coords = np.concatenate([*coords, np.zeros((padded - halo, 3), np.int64)]).astype(np.int32)
    rim_index = np.concatenate([*sources, np.full(padded - halo, -1)]).astype(np.int32)[None, :]
    ends = np.cumsum([0, *counts])
    spans = [(int(a), int(b)) for a, b in zip(ends[:-1], ends[1:])]

    grid = tok.reshape(TH, TW, feat)
    halo_tokens = []
    for (r, c), n in zip(steps, counts):
        (r0, r1), (c0, c1) = span(r, TH), span(c, TW)
        piece = grid[r0:r1, c0:c1].reshape(n, feat)
        halo_tokens.append(shift(piece, "space", -(r * grid_cols + c)))

    q, *window = pl.pallas_call(
        functools.partial(kernel_own, sizes),
        out_shape=(
            struct((TOKENS, feat), BF16),
            struct((keys, 2 * feat), BF16),
            struct((2 * feat, keys), BF16),
            struct((feat, keys), BF16),
            struct((keys, TOKENS), F32),
        ),
        in_specs=[smem(), vmem(), vmem()],
        out_specs=[vmem()] * 5,
        compiler_params=params(),
        cost_estimate=cost(8 * TOKENS * feat * feat, 7e6),
        name="own",
    )(margins, tok, weight)

    outs = pl.pallas_call(
        functools.partial(kernel_attend, sizes, n_sample, spans),
        out_shape=(
            *[struct(a.shape, a.dtype) for a in window],
            struct((TOKENS, feat), BF16),
            struct((TOKENS, feat), BF16),
            struct((TOKENS, 2 * feat), BF16),
            struct((feat // 2, 3 * feat), F32),
            struct((feat // 2, 3 * feat), BF16),
            *[struct((n, feat), BF16) for n in counts],
        ),
        in_specs=[smem()] + [vmem()] * (4 + len(counts) + 4),
        out_specs=[vmem()] * (9 + len(counts)),
        input_output_aliases={5 + len(counts) + i: i for i in range(4)},
        scratch_shapes=[
            pltpu.VMEM((2, keys, CHUNK), F32),
            pltpu.VMEM((2, keys, CHUNK), F32),
            pltpu.VMEM((keys, 2 * TOKENS), BF16),
            pltpu.VMEM((keys, 2 * TOKENS), BF16),
            pltpu.VMEM((2 * TOKENS, 2 * HEAD), BF16),
            pltpu.VMEM((2 * TOKENS, 2 * HEAD), BF16),
            pltpu.VMEM((feat, TOKENS), F32),
            pltpu.VMEM((feat, TOKENS), F32),
            pltpu.VMEM((padded, 2 * feat), BF16),
        ],
        compiler_params=params(),
        cost_estimate=cost(48 * TOKENS * keys * feat, 6e6, TOKENS * keys * HEADS),
        name="attend",
    )(margins, jnp.asarray(coords), q, cot, weight, *halo_tokens, *window)
    attention, gq, gkv, keep, send = outs[4:9]
    rims = outs[9:]

    arrived = [shift(rim, "space", r * grid_cols + c) for (r, c), rim in zip(steps, rims)]

    total = keep + swap(send, "sample", 0).astype(F32)
    half = total.shape[0] // 2
    first, second = total[:half], total[half:]
    row_bits = range((n_space - 1).bit_length())
    col_bits = range((n_sample - 1).bit_length() - 1, 0, -1)

    def by_cols(value):
        for bit in col_bits:
            n = value.shape[1] // 2
            value = halve(value[:, :n], value[:, n:], "sample", bit)
        return value

    def by_rows(value):
        for bit in row_bits:
            n = value.shape[0] // 2
            value = halve(value[:n], value[n:], "space", bit)
        return value

    total = jnp.concatenate([by_rows(by_cols(first)), by_cols(by_rows(second))], axis=0)
    n = total.shape[1] // 2
    mine, got = total[:, :n], swap(total[:, n:], "sample", 0)
    weight_grad = jnp.where(
        (member & 1) == 1, jnp.concatenate([got, mine], axis=0), jnp.concatenate([mine, got], axis=0)
    )

    token_grad = pl.pallas_call(
        functools.partial(kernel_final, len(steps)),
        out_shape=struct((TOKENS, feat), BF16),
        in_specs=[vmem()] * (5 + len(steps)),
        out_specs=vmem(),
        compiler_params=params(),
        cost_estimate=cost(6 * TOKENS * feat * feat, 5e6),
        name="final",
    )(tok, weight, jnp.asarray(rim_index), gq, gkv, *arrived)
    return (attention[None, None], token_grad[None, None], weight_grad)


def solution(mesh):
    return jax.shard_map(
        local,
        mesh=mesh,
        in_specs=(
            P(("groups", "sample"), "space", None, None),
            P(("groups", "sample"), "space", None, None),
            P("groups", None),
            P(("groups", "sample"), None),
        ),
        out_specs=(
            P(("groups", "sample"), "space", None, None),
            P(("groups", "sample"), "space", None, None),
            P(("groups", "space"), "sample"),
        ),
        check_vma=False,
    )
```

time: 82.2 us -> 62.3 us (0.76)
  other arithmetic: 8.47 us -> 2.07 us
  local copies, waits for them, and re-layouts: 11.6 us -> 5.35 us
  Pallas kernels: 24.2 us -> 20.7 us
  waiting for transfers between devices: 12.4 us -> 8.91 us
  between operations: 2.21 us -> 0.9 us
  starting transfers between devices: 22.8 us -> 24 us
    broadcast_in_dim x2 -> x0, other arithmetic: 3.78 us -> none  [the longest x1 1.92 us: local(): jnp.broadcast_to(jnp.where(open_key, 0.0, NEG).astype(F32), (padded, TOKE...]
    pallas_call x5 -> x3, Pallas kernels: 24.2 us -> 20.7 us  [the longest x1 16.3 us: local(): pl.pallas_call(functools.partial(kernel_attend, sizes, n_sample, spans),...]
    ppermute x8, waiting for transfers between devices: 12.4 us -> 8.9 us  [swap(): return lax.ppermute(value, axis, [(i, i ^ 1 << bit) for i in range(count)])]
    unnamed x48 -> x20, local copies, waits for them, and re-layouts: 7.49 us -> 4.16 us
    add x7 -> x6, other arithmetic: 3.31 us -> 0.13 us  [halve(): return keep + swap(send.astype(BF16), axis, bit).astype(F32)]
    slice x7 -> x6, local copies, waits for them, and re-layouts: 1.56 us -> 0.07 us  [the longest x4 0.05 us: by_rows(): value = halve(value[:n], value[n:], 'space', bit)]
    ppermute x8, starting transfers between devices: 10.6 us -> 11.9 us  [swap(): return lax.ppermute(value, axis, [(i, i ^ 1 << bit) for i in range(count)])]
    another operation x1 -> x0, local copies, waits for them, and re-layouts: 1.3 us -> none  [local(): jnp.stack([me, tile_row * TH, tile_col * TW, margin[0], plane_rows - marg...]
  transfers between devices with their start and end apart: 12 -> 12, of which waited for: 4 -> 5; matrix products, arithmetic and copies ran while one was open for 12% -> 0% of each run, Pallas kernels for 5% -> 7%
where the time goes in v2:
time: 62.3 us; the launch traced here: 61.9 us
  starting transfers between devices  24 us (39%)
  Pallas kernels  20.7 us (33%)
  waiting for transfers between devices  8.91 us (14%)
  local copies, waits for them, and re-layouts  5.35 us (9%)
  other arithmetic  2.07 us (3%)
  between operations  0.9 us (1%)
    pallas_call x1, Pallas kernels, local(): pl.pallas_call(functools.partial(kernel_attend, sizes, n_sample, spans),...  16.3 us
    ppermute x4, starting transfers between devices, shift(): lax.ppermute(value, axis, [(i, i + steps) for i in range(first, last)])  12.1 us
    ppermute x8, starting transfers between devices, swap(): return lax.ppermute(value, axis, [(i, i ^ 1 << bit) for i in range(count)])  11.9 us
    ppermute x8, waiting for transfers between devices, swap(): return lax.ppermute(value, axis, [(i, i ^ 1 << bit) for i in range(count)])  8.9 us
    unnamed x20, local copies, waits for them, and re-layouts  4.16 us
    pallas_call x1, Pallas kernels, local(): pl.pallas_call(functools.partial(kernel_own, sizes), out_shape=(struct((T...  2.21 us
    pallas_call x1, Pallas kernels, local(): pl.pallas_call(functools.partial(kernel_final, len(steps)), out_shape=str...  2.15 us
    select_n x1, other arithmetic, local(): jnp.where(member & 1 == 1, jnp.concatenate([got, mine], axis=0), jnp.conc...  1.66 us
  transfers between devices with their start and end apart: 12, of which 5 were waited for; matrix products, arithmetic and copies ran while one was open for 0% of the time, Pallas kernels for 7%

profile of v2, /device:TPU:0, one launch (start us, length us, event | category | flops | bytes accessed | tf_op | source)
XLA Modules:
  0.0 61.9 jit_solution(6084465944573022896)
XLA Ops:
  0.6 1.0 %fusion.2 = (bf16[16,3,512]{2,1,0:T(4,128)(2,1)S(1)}, bf16[16,3,512]{2,1,0:T(4,128)(2,1)S(1)}) fusion(bf16[16,32,512]{2,1,0:T(8,128)(2,1)} %bitcast.5), kind=kLoop, calls=%fused_computation.17 | loop fusion | bytes 196608 | tf_op jit(solution)/shard_map/slice | solution.py:292
  1.7 4.9 %collective-permute-start = (bf16[48,512]{1,0:T(8,128)(2,1)S(1)}, bf16[48,512]{1,0:T(8,128)(2,1)S(1)}, u32[]{:S(2)}, u32[]{:S(2)}) collective-permute-start(bf16[48,512]{1,0:T(8,128)(2,1)S(1)} %reshape.12), channel_id=1, source_target_pairs={{0,4},{4,8},{8,12},{1,5},{5,9},{9,13},{2,6},{6,10},{10,14},{3,7},{... | collective-permute-start | bytes 147464 | tf_op jit(solution)/shard_map/ppermute | solution.py:225
  6.7 1.3 %collective-permute-start.1 = (bf16[48,512]{1,0:T(8,128)(2,1)S(1)}, bf16[48,512]{1,0:T(8,128)(2,1)S(1)}, u32[]{:S(2)}, u32[]{:S(2)}) collective-permute-start(bf16[48,512]{1,0:T(8,128)(2,1)S(1)} %reshape.13), channel_id=1, source_target_pairs={{4,0},{8,4},{12,8},{5,1},{9,5},{13,9},{6,2},{10,6},{14,10},{7,3},{... | collective-permute-start | bytes 147464 | tf_op jit(solution)/shard_map/ppermute | solution.py:225
  8.0 0.0 copy-start
  8.0 1.4 %copy-done = bf16[512,1536]{1,0:T(8,128)(2,1)S(1)} copy-done((bf16[512,1536]{1,0:T(8,128)(2,1)S(1)}, bf16[512,1536]{1,0:T(8,128)(2,1)}, u32[]{:S(2)}) %copy-start) | copy-done | bytes 1572888
  9.4 1.0 %copy-done.2 = bf16[1,1,512,512]{3,2,1,0:T(8,128)(2,1)S(1)} copy-done((bf16[1,1,512,512]{3,2,1,0:T(8,128)(2,1)S(1)}, bf16[1,1,512,512]{3,2,1,0:T(8,128)(2,1)}, u32[]{:S(2)}) %copy-start.2) | copy-done | bytes 524312
  10.4 0.7 %copy-done.8 = s32[1,4]{1,0:T(1,128)S(1)} copy-done((s32[1,4]{1,0:T(1,128)S(1)}, s32[1,4]{1,0:T(1,128)}, u32[]{:S(2)}) %copy-start.8) | copy-done | bytes 40
  11.1 2.2 %own.1 = (bf16[512,512]{1,0:T(8,128)(2,1)S(1)}, bf16[640,1024]{1,0:T(8,128)(2,1)S(1)}, bf16[1024,640]{1,0:T(8,128)(2,1)S(1)}, bf16[512,640]{1,0:T(8,128)(2,1)S(1)}, f32[640,512]{1,0:T(8,128)S(1)}) custom-call(s32[1,4]{1,0:T(1,128)S(1)} %copy-done.8, bf16[512,512]{1,0:T(8,128)(2,1)S(1)} %bitcast.6, bf16[512,1536]{1,0:T(8,128)(2,1)S(1)} %copy-done), custom_call_target="tpu_custom_call" | custom-call | flops 1073741824 | bytes 7000000 | tf_op jit(solution)/shard_map/own/pallas_call | solution.py:295
  13.3 0.0 collective-permute-done.refs_0_
  13.3 0.0 collective-permute-done.1.refs_1_
  13.4 16.3 %attend.1 = (bf16[640,1024]{1,0:T(8,128)(2,1)S(1)}, bf16[1024,640]{1,0:T(8,128)(2,1)S(1)}, bf16[512,640]{1,0:T(8,128)(2,1)S(1)}, f32[640,512]{1,0:T(8,128)S(1)},...) custom-call(s32[1,4]{1,0:T(1,128)S(1)} %copy-done.8, ...), custom_call_target="tpu_custom_call", output_to_operand_aliasing={{0}: (7, {}), {1}: (8, {}), {2}: (9, {}), {3}: (10, {})} | custom-call | flops 8053063680 | bytes 6000000 | tf_op jit(solution)/shard_map/attend/pallas_call | solution.py:311
  29.7 2.3 %collective-permute-done.4 = bf16[256,1536]{1,0:T(8,128)(2,1)S(1)} collective-permute-done((bf16[256,1536]{1,0:T(8,128)(2,1)S(1)}, bf16[256,1536]{1,0:T(8,128)(2,1)S(1)}, u32[]{:S(2)}, u32[]{:S(2)}) %collective-permute-start.4) | collective-permute-done | bytes 786464 | tf_op jit(solution)/shard_map/ppermute | solution.py:230
  32.0 0.3 fusion.1
  32.3 2.7 %collective-permute-start.8 = (bf16[64,1536]{1,0:T(8,128)(2,1)S(1)}, bf16[64,1536]{1,0:T(8,128)(2,1)S(1)}, u32[]{:S(2)}, u32[]{:S(2)}) collective-permute-start(bf16[64,1536]{1,0:T(8,128)(2,1)S(1)} %slice.85), channel_id=1, source_target_pairs={{0,4},{4,0},{8,12},{12,8},{1,5},{5,1},{9,13},{13,9},{2,6},{6,2},{1... | collective-permute-start | bytes 589832 | tf_op jit(solution)/shard_map/ppermute | solution.py:230
  35.0 1.3 %collective-permute-start.2 = (bf16[48,512]{1,0:T(8,128)(2,1)S(1)}, bf16[48,512]{1,0:T(8,128)(2,1)S(1)}, u32[]{:S(2)}, u32[]{:S(2)}) collective-permute-start(bf16[48,512]{1,0:T(8,128)(2,1)S(1)} %get-tuple-element.23), channel_id=1, source_target_pairs={{4,0},{8,4},{12,8},{5,1},{9,5},{13,9},{6,2},{10,6},{14,10},{7,3},{... | collective-permute-start | bytes 147464 | tf_op jit(solution)/shard_map/ppermute | solution.py:225
  36.3 4.5 %collective-permute-start.3 = (bf16[48,512]{1,0:T(8,128)(2,1)S(1)}, bf16[48,512]{1,0:T(8,128)(2,1)S(1)}, u32[]{:S(2)}, u32[]{:S(2)}) collective-permute-start(bf16[48,512]{1,0:T(8,128)(2,1)S(1)} %get-tuple-element.24), channel_id=1, source_target_pairs={{0,4},{4,8},{8,12},{1,5},{5,9},{9,13},{2,6},{6,10},{10,14},{3,7},{... | collective-permute-start | bytes 147464 | tf_op jit(solution)/shard_map/ppermute | solution.py:225
  40.9 1.6 %collective-permute-start.5 = (bf16[128,768]{1,0:T(8,128)(2,1)S(1)}, bf16[128,768]{1,0:T(8,128)(2,1)S(1)}, u32[]{:S(2)}, u32[]{:S(2)}) collective-permute-start(bf16[128,768]{1,0:T(8,128)(2,1)S(1)} %slice.79), channel_id=1, source_target_pairs={{0,2},{1,3},{2,0},{3,1},{4,6},{5,7},{6,4},{7,5},{8,10},{9,11},{10,... | collective-permute-start | bytes 589832 | tf_op jit(solution)/shard_map/ppermute | solution.py:230
  42.5 0.0 copy-start.3
  42.5 0.0 copy-start.6
  42.5 2.6 %collective-permute-start.9 = (bf16[32,1536]{1,0:T(8,128)(2,1)S(1)}, bf16[32,1536]{1,0:T(8,128)(2,1)S(1)}, u32[]{:S(2)}, u32[]{:S(2)}) collective-permute-start(bf16[32,1536]{1,0:T(8,128)(2,1)S(1)} %slice.108), channel_id=1, source_target_pairs={{0,8},{4,12},{8,0},{12,4},{1,9},{5,13},{9,1},{13,5},{2,10},{6,14},... | collective-permute-start | bytes 294920 | tf_op jit(solution)/shard_map/ppermute | solution.py:230
  45.2 1.9 %collective-permute-done.5 = bf16[128,768]{1,0:T(8,128)(2,1)S(1)} collective-permute-done((bf16[128,768]{1,0:T(8,128)(2,1)S(1)}, bf16[128,768]{1,0:T(8,128)(2,1)S(1)}, u32[]{:S(2)}, u32[]{:S(2)}) %collective-permute-start.5) | collective-permute-done | bytes 196640 | tf_op jit(solution)/shard_map/ppermute | solution.py:230
  47.1 1.5 %collective-permute-start.6 = (bf16[64,768]{1,0:T(8,128)(2,1)S(1)}, bf16[64,768]{1,0:T(8,128)(2,1)S(1)}, u32[]{:S(2)}, u32[]{:S(2)}) collective-permute-start(bf16[64,768]{1,0:T(8,128)(2,1)S(1)} %slice.109), channel_id=1, source_target_pairs={{0,4},{4,0},{8,12},{12,8},{1,5},{5,1},{9,13},{13,9},{2,6},{6,2},{1... | collective-permute-start | bytes 294920 | tf_op jit(solution)/shard_map/ppermute | solution.py:230
  48.6 0.8 %collective-permute-done.9 = bf16[32,1536]{1,0:T(8,128)(2,1)S(1)} collective-permute-done((bf16[32,1536]{1,0:T(8,128)(2,1)S(1)}, bf16[32,1536]{1,0:T(8,128)(2,1)S(1)}, u32[]{:S(2)}, u32[]{:S(2)}) %collective-permute-start.9) | collective-permute-done | bytes 98336 | tf_op jit(solution)/shard_map/ppermute | solution.py:230
  49.4 0.7 %collective-permute-start.10 = (bf16[32,768]{1,0:T(8,128)(2,1)S(1)}, bf16[32,768]{1,0:T(8,128)(2,1)S(1)}, u32[]{:S(2)}, u32[]{:S(2)}) collective-permute-start(bf16[32,768]{1,0:T(8,128)(2,1)S(1)} %slice.110), channel_id=1, source_target_pairs={{0,2},{1,3},{2,0},{3,1},{4,6},{5,7},{6,4},{7,5},{8,10},{9,11},{10,... | collective-permute-start | bytes 147464 | tf_op jit(solution)/shard_map/ppermute | solution.py:230
  50.2 1.6 %collective-permute-done.6 = bf16[64,768]{1,0:T(8,128)(2,1)S(1)} collective-permute-done((bf16[64,768]{1,0:T(8,128)(2,1)S(1)}, bf16[64,768]{1,0:T(8,128)(2,1)S(1)}, u32[]{:S(2)}, u32[]{:S(2)}) %collective-permute-start.6) | collective-permute-done | bytes 98336 | tf_op jit(solution)/shard_map/ppermute | solution.py:230
  51.8 2.7 %collective-permute-start.7 = (bf16[32,768]{1,0:T(8,128)(2,1)S(1)}, bf16[32,768]{1,0:T(8,128)(2,1)S(1)}, u32[]{:S(2)}, u32[]{:S(2)}) collective-permute-start(bf16[32,768]{1,0:T(8,128)(2,1)S(1)} %slice.111), channel_id=1, source_target_pairs={{0,8},{4,12},{8,0},{12,4},{1,9},{5,13},{9,1},{13,5},{2,10},{6,14},... | collective-permute-start | bytes 147464 | tf_op jit(solution)/shard_map/ppermute | solution.py:230
  54.5 2.3 %collective-permute-done.7 = bf16[32,768]{1,0:T(8,128)(2,1)S(1)} collective-permute-done((bf16[32,768]{1,0:T(8,128)(2,1)S(1)}, bf16[32,768]{1,0:T(8,128)(2,1)S(1)}, u32[]{:S(2)}, u32[]{:S(2)}) %collective-permute-start.7) | collective-permute-done | bytes 49184 | tf_op jit(solution)/shard_map/ppermute | solution.py:230
  56.9 0.1 collective-permute-start.11
  57.0 0.0 copy-start.5
  57.0 1.0 %copy-done.5 = bf16[512,512]{1,0:T(8,128)(2,1)S(1)} copy-done((bf16[512,512]{1,0:T(8,128)(2,1)S(1)}, bf16[512,512]{1,0:T(8,128)(2,1)}, u32[]{:S(2)}) %copy-start.5) | copy-done | bytes 524312
  58.1 2.1 %final.1 = bf16[512,512]{1,0:T(8,128)(2,1)} custom-call(bf16[512,512]{1,0:T(8,128)(2,1)S(1)} %bitcast.7, bf16[512,1536]{1,0:T(8,128)(2,1)S(1)} %copy-done.1, s32[1,128]{1,0:T(1,128)S(1)} %copy-done.6, bf16[512,512]{1,0:T(8,128)(2,1)S(1)} %copy-done.5, bf16[512,1024]{1,0:T(8,128)(2,1)S(1)} %get-tuple-element.22.gkv_ref, ...), custom_call_target="tpu_custom_call" | custom-call | flops 805306368 | bytes 5000000 | tf_op jit(solution)/shard_map/final/pallas_call | solution.py:370
  60.2 1.7 %maximum_select_fusion = f32[128,384]{1,0:T(8,128)} fusion(f32[64,384]{1,0:T(8,128)S(1)} %get-tuple-element.32, f32[64,384]{1,0:T(8,128)} %collective-permute-done.11, pred[]{:T(512)S(6)} %eq.3), kind=kLoop, calls=%fused_computation.9 | loop fusion | flops 147456 | bytes 393217 | tf_op jit(solution)/shard_map/jit(_where)/select_n | solution.py:366
  (33 shorter events, 0.3 us)
Async XLA Ops:
  1.7 11.6 %collective-permute-start = (bf16[48,512]{1,0:T(8,128)(2,1)S(1)}, bf16[48,512]{1,0:T(8,128)(2,1)S(1)}, u32[]{:S(2)}, u32[]{:S(2)}) collective-permute-start(bf16[48,512]{1,0:T(8,128)(2,1)S(1)} %reshape.12), channel_id=1, source_target_pairs={{0,4},{4,8},{8,12},{1,5},{5,9},{9,13},{2,6},{6,10},{10,14},{3,7},{... | collective-permute-start | bytes 147464 | tf_op jit(solution)/shard_map/ppermute | solution.py:225
  6.7 6.6 %collective-permute-start.1 = (bf16[48,512]{1,0:T(8,128)(2,1)S(1)}, bf16[48,512]{1,0:T(8,128)(2,1)S(1)}, u32[]{:S(2)}, u32[]{:S(2)}) collective-permute-start(bf16[48,512]{1,0:T(8,128)(2,1)S(1)} %reshape.13), channel_id=1, source_target_pairs={{4,0},{8,4},{12,8},{5,1},{9,5},{13,9},{6,2},{10,6},{14,10},{7,3},{... | collective-permute-start | bytes 147464 | tf_op jit(solution)/shard_map/ppermute | solution.py:225
  8.0 1.4 %copy-start = (bf16[512,1536]{1,0:T(8,128)(2,1)S(1)}, bf16[512,1536]{1,0:T(8,128)(2,1)}, u32[]{:S(2)}) copy-start(bf16[512,1536]{1,0:T(8,128)(2,1)} %w_ref.5) | copy-start | bytes 4718596
  9.4 1.0 %copy-start.2 = (bf16[1,1,512,512]{3,2,1,0:T(8,128)(2,1)S(1)}, bf16[1,1,512,512]{3,2,1,0:T(8,128)(2,1)}, u32[]{:S(2)}) copy-start(bf16[1,1,512,512]{3,2,1,0:T(8,128)(2,1)} %param.6) | copy-start | bytes 1572868
  10.4 0.7 %copy-start.8 = (s32[1,4]{1,0:T(1,128)S(1)}, s32[1,4]{1,0:T(1,128)}, u32[]{:S(2)}) copy-start(s32[1,4]{1,0:T(1,128)} %margin_ref.3) | copy-start | bytes 52
  11.1 2.2 %copy-start.1 = (bf16[512,1536]{1,0:T(8,128)(2,1)S(1)}, bf16[512,1536]{1,0:T(8,128)(2,1)}, u32[]{:S(2)}) copy-start(bf16[512,1536]{1,0:T(8,128)(2,1)} %w_ref.5) | copy-start | bytes 4718596
  11.1 2.3 %copy-start.7 = (bf16[1,1,512,512]{3,2,1,0:T(8,128)(2,1)S(1)}, bf16[1,1,512,512]{3,2,1,0:T(8,128)(2,1)}, u32[]{:S(2)}) copy-start(bf16[1,1,512,512]{3,2,1,0:T(8,128)(2,1)} %param.7) | copy-start | bytes 1572868
  11.1 2.3 %copy-start.9 = (s32[128,3]{1,0:T(8,128)S(1)}, s32[128,3]{1,0:T(8,128)}, u32[]{:S(2)}) copy-start(s32[128,3]{1,0:T(8,128)} %constant.10.clone.coord_ref) | copy-start | bytes 4612
  29.7 2.6 %copy-start.4 = (bf16[512,512]{1,0:T(8,128)(2,1)}, bf16[512,512]{1,0:T(8,128)(2,1)S(1)}, u32[]{:S(2)}) copy-start(bf16[512,512]{1,0:T(8,128)(2,1)S(1)} %get-tuple-element.21.gq_ref) | copy-start | bytes 1572868
  29.7 2.3 %collective-permute-start.4 = (bf16[256,1536]{1,0:T(8,128)(2,1)S(1)}, bf16[256,1536]{1,0:T(8,128)(2,1)S(1)}, u32[]{:S(2)}, u32[]{:S(2)}) collective-permute-start(bf16[256,1536]{1,0:T(8,128)(2,1)S(1)} %get-tuple-element.26), channel_id=1, source_target_pairs={{0,1},{1,0},{2,3},{3,2},{4,5},{5,4},{6,7},{7,6},{8,9},{9,8},{10,11... | collective-permute-start | bytes 2359304 | tf_op jit(solution)/shard_map/ppermute | solution.py:230
  32.3 10.1 %collective-permute-start.8 = (bf16[64,1536]{1,0:T(8,128)(2,1)S(1)}, bf16[64,1536]{1,0:T(8,128)(2,1)S(1)}, u32[]{:S(2)}, u32[]{:S(2)}) collective-permute-start(bf16[64,1536]{1,0:T(8,128)(2,1)S(1)} %slice.85), channel_id=1, source_target_pairs={{0,4},{4,0},{8,12},{12,8},{1,5},{5,1},{9,13},{13,9},{2,6},{6,2},{1... | collective-permute-start | bytes 589832 | tf_op jit(solution)/shard_map/ppermute | solution.py:230
  35.0 22.0 %collective-permute-start.2 = (bf16[48,512]{1,0:T(8,128)(2,1)S(1)}, bf16[48,512]{1,0:T(8,128)(2,1)S(1)}, u32[]{:S(2)}, u32[]{:S(2)}) collective-permute-start(bf16[48,512]{1,0:T(8,128)(2,1)S(1)} %get-tuple-element.23), channel_id=1, source_target_pairs={{4,0},{8,4},{12,8},{5,1},{9,5},{13,9},{6,2},{10,6},{14,10},{7,3},{... | collective-permute-start | bytes 147464 | tf_op jit(solution)/shard_map/ppermute | solution.py:225
  36.3 20.7 %collective-permute-start.3 = (bf16[48,512]{1,0:T(8,128)(2,1)S(1)}, bf16[48,512]{1,0:T(8,128)(2,1)S(1)}, u32[]{:S(2)}, u32[]{:S(2)}) collective-permute-start(bf16[48,512]{1,0:T(8,128)(2,1)S(1)} %get-tuple-element.24), channel_id=1, source_target_pairs={{0,4},{4,8},{8,12},{1,5},{5,9},{9,13},{2,6},{6,10},{10,14},{3,7},{... | collective-permute-start | bytes 147464 | tf_op jit(solution)/shard_map/ppermute | solution.py:225
  40.9 6.2 %collective-permute-start.5 = (bf16[128,768]{1,0:T(8,128)(2,1)S(1)}, bf16[128,768]{1,0:T(8,128)(2,1)S(1)}, u32[]{:S(2)}, u32[]{:S(2)}) collective-permute-start(bf16[128,768]{1,0:T(8,128)(2,1)S(1)} %slice.79), channel_id=1, source_target_pairs={{0,2},{1,3},{2,0},{3,1},{4,6},{5,7},{6,4},{7,5},{8,10},{9,11},{10,... | collective-permute-start | bytes 589832 | tf_op jit(solution)/shard_map/ppermute | solution.py:230
  42.5 14.5 %copy-start.3 = (bf16[1,1,512,512]{3,2,1,0:T(8,128)(2,1)S(1)}, bf16[1,1,512,512]{3,2,1,0:T(8,128)(2,1)}, u32[]{:S(2)}) copy-start(bf16[1,1,512,512]{3,2,1,0:T(8,128)(2,1)} %param.6) | copy-start | bytes 1572868
  42.5 14.5 %copy-start.6 = (s32[1,128]{1,0:T(1,128)S(1)}, s32[1,128]{1,0:T(1,128)}, u32[]{:S(2)}) copy-start(s32[1,128]{1,0:T(1,128)} %constant.11.clone.index_ref) | copy-start | bytes 1540
  42.5 6.9 %collective-permute-start.9 = (bf16[32,1536]{1,0:T(8,128)(2,1)S(1)}, bf16[32,1536]{1,0:T(8,128)(2,1)S(1)}, u32[]{:S(2)}, u32[]{:S(2)}) collective-permute-start(bf16[32,1536]{1,0:T(8,128)(2,1)S(1)} %slice.108), channel_id=1, source_target_pairs={{0,8},{4,12},{8,0},{12,4},{1,9},{5,13},{9,1},{13,5},{2,10},{6,14},... | collective-permute-start | bytes 294920 | tf_op jit(solution)/shard_map/ppermute | solution.py:230
  47.1 4.7 %collective-permute-start.6 = (bf16[64,768]{1,0:T(8,128)(2,1)S(1)}, bf16[64,768]{1,0:T(8,128)(2,1)S(1)}, u32[]{:S(2)}, u32[]{:S(2)}) collective-permute-start(bf16[64,768]{1,0:T(8,128)(2,1)S(1)} %slice.109), channel_id=1, source_target_pairs={{0,4},{4,0},{8,12},{12,8},{1,5},{5,1},{9,13},{13,9},{2,6},{6,2},{1... | collective-permute-start | bytes 294920 | tf_op jit(solution)/shard_map/ppermute | solution.py:230
  49.4 5.1 %collective-permute-start.10 = (bf16[32,768]{1,0:T(8,128)(2,1)S(1)}, bf16[32,768]{1,0:T(8,128)(2,1)S(1)}, u32[]{:S(2)}, u32[]{:S(2)}) collective-permute-start(bf16[32,768]{1,0:T(8,128)(2,1)S(1)} %slice.110), channel_id=1, source_target_pairs={{0,2},{1,3},{2,0},{3,1},{4,6},{5,7},{6,4},{7,5},{8,10},{9,11},{10,... | collective-permute-start | bytes 147464 | tf_op jit(solution)/shard_map/ppermute | solution.py:230
  51.8 5.1 %collective-permute-start.7 = (bf16[32,768]{1,0:T(8,128)(2,1)S(1)}, bf16[32,768]{1,0:T(8,128)(2,1)S(1)}, u32[]{:S(2)}, u32[]{:S(2)}) collective-permute-start(bf16[32,768]{1,0:T(8,128)(2,1)S(1)} %slice.111), channel_id=1, source_target_pairs={{0,8},{4,12},{8,0},{12,4},{1,9},{5,13},{9,1},{13,5},{2,10},{6,14},... | collective-permute-start | bytes 147464 | tf_op jit(solution)/shard_map/ppermute | solution.py:230
  56.9 3.3 %collective-permute-start.11 = (f32[64,384]{1,0:T(8,128)S(1)}, f32[64,384]{1,0:T(8,128)}, u32[]{:S(2)}, u32[]{:S(2)}) collective-permute-start(f32[64,384]{1,0:T(8,128)S(1)} %get-tuple-element.31), channel_id=1, source_target_pairs={{0,1},{1,0},{2,3},{3,2},{4,5},{5,4},{6,7},{7,6},{8,9},{9,8},{10,11... | collective-permute-start | bytes 294920 | tf_op jit(solution)/shard_map/ppermute | solution.py:230
  57.0 1.0 %copy-start.5 = (bf16[512,512]{1,0:T(8,128)(2,1)S(1)}, bf16[512,512]{1,0:T(8,128)(2,1)}, u32[]{:S(2)}) copy-start(bf16[512,512]{1,0:T(8,128)(2,1)} %copy-done.4) | copy-start | bytes 1572868

commit v3 on v2

v3 whole, which is shorter than its diff:
```python
import functools
import math

import jax
import jax.numpy as jnp
import numpy as np
from jax import lax
from jax.experimental import pallas as pl
from jax.experimental.pallas import tpu as pltpu
from jax.sharding import PartitionSpec as P

HEADS = 8
HEAD = 64
TH = 16
TW = 32
HALO = 3
TOKENS = TH * TW
NEG = -1e30
LAST = (((1,), (1,)), ((), ()))
F32 = jnp.float32
BF16 = jnp.bfloat16
CHUNK = 512
ROWS = 64

vmem = functools.partial(pl.BlockSpec, memory_space=pltpu.VMEM)
hbm = functools.partial(pl.BlockSpec, memory_space=pltpu.HBM)


def params():
    return pltpu.CompilerParams(vmem_limit_bytes=24 * 1024 * 1024)


def dot(a, b):
    return jnp.dot(a, b, preferred_element_type=F32)


def dot_t(a, b):
    return lax.dot_general(a, b, LAST, preferred_element_type=F32)


def normalise(tok):
    tok = tok.astype(F32)
    centred = tok - jnp.mean(tok, axis=-1, keepdims=True)
    inv = lax.rsqrt(jnp.mean(centred * centred, axis=-1, keepdims=True) + 1e-05)
    return centred * inv, inv


def own_ids(cols):
    position = lax.axis_index("space")
    member = lax.axis_index("sample")
    return position, member, position // cols, position % cols


def live(row, col, margin_ref, rows, cols):
    return (
        (row >= margin_ref[0, 0])
        & (row < rows - margin_ref[0, 1])
        & (col >= margin_ref[0, 2])
        & (col < cols - margin_ref[0, 3])
    )


def row_masks(sizes):
    bits = (sizes[0] - 1).bit_length()
    one_row = sizes[1] == sizes[0]
    return [((2 << i) - 1) if one_row else (1 << i) for i in range(bits)]


def paired(sizes):
    return sizes[1] == sizes[0] and sizes[0] in (2, 4)


def permutation(feat, sizes, position):
    masks = row_masks(sizes)
    bits = len(masks)
    size = feat // (2 * sizes[0])
    row = lax.broadcasted_iota(jnp.int32, (feat, feat), 0)
    col = lax.broadcasted_iota(jnp.int32, (feat, feat), 1)
    relative = row // size
    space = jnp.zeros_like(row) + position
    for i, mask in enumerate(masks):
        space = space ^ (((relative >> (bits - 1 - i)) & 1) * mask)
    part = (relative >> bits) & 1
    source = (space * 2 + part) * size + row % size
    return jnp.where(col == source, 1.0, 0.0).astype(BF16)


def kernel_own(
    sizes, pieces, margin_hbm, tok_hbm, w_hbm, q_ref, kv_ref, kvt_ref, nt_ref, bias_ref, margin_ref, tok_s, w_s, sems
):
    n_space, grid_cols, plane_rows, plane_cols = sizes
    feat = w_hbm.shape[0]
    copies = [pltpu.make_async_copy(tok_hbm, tok_s, sems.at[0])]
    for i in range(3):
        cols = pl.ds(i * feat, feat)
        copies.append(pltpu.make_async_copy(w_hbm.at[:, cols], w_s.at[:, cols], sems.at[1 + i]))
    copies.append(pltpu.make_async_copy(margin_hbm, margin_ref, sems.at[4]))
    for copy in copies:
        copy.start()
    position, member, tile_row, tile_col = own_ids(grid_cols)
    copies[4].wait()
    key = lax.broadcasted_iota(jnp.int32, (TOKENS, TOKENS), 0)
    query = lax.broadcasted_iota(jnp.int32, (TOKENS, TOKENS), 1)
    row = tile_row * TH + key // TW
    col = tile_col * TW + key % TW
    is_open = live(row, col, margin_ref, plane_rows, plane_cols) | (key == query)
    bias_ref[:TOKENS, :] = jnp.where(is_open, 0.0, NEG)
    padded = bias_ref.shape[0] - TOKENS
    index = lax.broadcasted_iota(jnp.int32, (padded, TOKENS), 0)
    row = jnp.full((padded, TOKENS), -1, jnp.int32)
    col = row
    for start, count, r0, c0, wide in pieces:
        at = index - start
        down = (at * 171) >> 9 if wide == 3 else at // wide
        here = (at >= 0) & (at < count)
        row = jnp.where(here, tile_row * TH + r0 + down, row)
        col = jnp.where(here, tile_col * TW + c0 + at - down * wide, col)
    is_open = live(row, col, margin_ref, plane_rows, plane_cols)
    is_open = is_open & (row >= 0) & (row < plane_rows) & (col >= 0) & (col < plane_cols)
    bias_ref[TOKENS:, :] = jnp.where(is_open, 0.0, NEG)
    place = permutation(feat, sizes, position)
    copies[0].wait()
    standard, _ = normalise(tok_s[...])
    normed = standard.astype(BF16)
    nt_ref[:, :TOKENS] = dot_t(place, normed).astype(BF16)
    scale = 1.0 / math.sqrt(HEAD)
    copies[1].wait()
    q_ref[...] = (dot(normed, w_s[:, :feat]).astype(BF16).astype(F32) * scale).astype(BF16)
    for i in range(2):
        copies[2 + i].wait()
        part = dot(normed, w_s[:, (i + 1) * feat : (i + 2) * feat]).astype(BF16)
        kv_ref[:TOKENS, i * feat : (i + 1) * feat] = part
        kvt_ref[i * feat : (i + 1) * feat, :TOKENS] = part.T


def kernel_attend(sizes, n_sample, spans, q_ref, cot_ref, w_ref, bias_ref, *refs):
    n_space, grid_cols, plane_rows, plane_cols = sizes
    count = len(spans)
    toks, refs = refs[:count], refs[count + 3 :]
    kv_ref, kvt_ref, nt_ref, att_ref, grad_ref, keep_ref, send_ref = refs[:7]
    rim_refs, refs = refs[7 : 7 + count], refs[7 + count :]
    s_s, g_s, pb_s, ds_s, cm_s, qm_s, att_s, dqt_s = refs
    position, member, tile_row, tile_col = own_ids(grid_cols)
    feat = w_ref.shape[0]
    keys = kv_ref.shape[0]
    padded = keys - TOKENS
    scale = 1.0 / math.sqrt(HEAD)

    parts = [r[...].astype(F32) for r in toks]
    even = (position & 1) == 0
    if paired(sizes):
        parts = [jnp.where(even, parts[1], parts[0]), jnp.where(even, parts[0], parts[1])]
    if spans[-1][1] < padded:
        parts.append(jnp.zeros((padded - spans[-1][1], feat), F32))
    standard, _ = normalise(jnp.concatenate(parts, axis=0))
    normed = standard.astype(BF16)
    for i in range(2):
        part = dot(normed, w_ref[:, (i + 1) * feat : (i + 2) * feat]).astype(BF16)
        kv_ref[TOKENS:, i * feat : (i + 1) * feat] = part
        kvt_ref[i * feat : (i + 1) * feat, TOKENS:] = part.T
    nt_ref[:, TOKENS:] = dot_t(permutation(feat, sizes, position), normed).astype(BF16)
    lane = lax.broadcasted_iota(jnp.int32, (TOKENS, 2 * HEAD), 1)
    step = 0
    for pair in range(HEADS // 2):
        base = pair * 2 * HEAD
        cols = slice(base, base + 2 * HEAD)
        vcols = slice(feat + base, feat + base + 2 * HEAD)
        q = q_ref[:, cols]
        cot = cot_ref[:, cols]
        zero = jnp.zeros_like(q)
        for odd in range(2):
            mine = (lane >= HEAD) if odd else (lane < HEAD)
            qm_s[odd * TOKENS : (odd + 1) * TOKENS, :] = jnp.where(mine, q, zero)
            cm_s[odd * TOKENS : (odd + 1) * TOKENS, :] = jnp.where(mine, cot, zero)
            krow = base + odd * HEAD
            vrow = feat + krow
            for c in range(TOKENS // CHUNK):
                slot = step % 2
                step += 1
                lanes = slice(c * CHUNK, (c + 1) * CHUNK)
                out = slice(odd * TOKENS + c * CHUNK, odd * TOKENS + (c + 1) * CHUNK)
                s_s[slot] = dot_t(kv_ref[:, cols], qm_s[out, :])
                g_s[slot] = dot_t(kv_ref[:, vcols], cm_s[out, :])
                top = jnp.full((8, CHUNK), NEG, F32)
                for r in range(0, keys, ROWS):
                    x = s_s[slot, r : r + ROWS, :] + bias_ref[r : r + ROWS, lanes]
                    top = jnp.maximum(top, jnp.max(x.reshape(ROWS // 8, 8, CHUNK), axis=0))
                top = jnp.max(top, axis=0, keepdims=True)
                total = jnp.zeros((8, CHUNK), F32)
                delta = jnp.zeros((8, CHUNK), F32)
                for r in range(0, keys, ROWS):
                    x = s_s[slot, r : r + ROWS, :] + bias_ref[r : r + ROWS, lanes]
                    e = jnp.exp(x - top)
                    s_s[slot, r : r + ROWS, :] = e
                    total = total + jnp.sum(e.reshape(ROWS // 8, 8, CHUNK), axis=0)
                    eg = e * g_s[slot, r : r + ROWS, :]
                    delta = delta + jnp.sum(eg.reshape(ROWS // 8, 8, CHUNK), axis=0)
                inv = 1.0 / jnp.sum(total, axis=0, keepdims=True)
                delta = jnp.sum(delta, axis=0, keepdims=True) * inv
                for r in range(0, keys, ROWS):
                    p = s_s[slot, r : r + ROWS, :] * inv
                    pb_s[r : r + ROWS, out] = p.astype(BF16)
                    ds_s[r : r + ROWS, out] = (p * (g_s[slot, r : r + ROWS, :] - delta)).astype(BF16)
                att_s[krow : krow + HEAD, lanes] = dot(kvt_ref[vrow : vrow + HEAD, :], pb_s[:, out])
                dqt_s[krow : krow + HEAD, lanes] = scale * dot(kvt_ref[krow : krow + HEAD, :], ds_s[:, out])
        for source, other, at in ((ds_s, qm_s, feat + base), (pb_s, cm_s, 2 * feat + base)):
            grad_ref[:, at : at + 2 * HEAD] = dot(source[...], other[...]).astype(BF16)
    grad_ref[:TOKENS, :feat] = dqt_s[...].T.astype(BF16)
    grad_ref[TOKENS:, :feat] = jnp.zeros((padded, feat), BF16)

    block = 3 * feat // n_sample
    for j in range(n_sample // 2):
        for target, other in ((keep_ref, 2 * j), (send_ref, 2 * j + 1)):
            cols = pl.ds(pl.multiple_of((member ^ other) * block, 128), block)
            value = dot(nt_ref[...], grad_ref[:, cols])
            target[:, j * block : (j + 1) * block] = value.astype(target.dtype)
    rim = dot_t(grad_ref[TOKENS:, feat:], w_ref[:, feat:])
    if paired(sizes):
        rows = rim_refs[0].shape[0]
        left, right = (rim[lo:hi, :] for lo, hi in spans)
        for ref, value in zip(rim_refs, (jnp.where(even, right, left), jnp.where(even, left, right))):
            wide = feat // 2
            value = jnp.concatenate([value[:, :wide], value[:, wide:]], axis=0).astype(BF16)
            for i in range(3):
                ref[:, i * wide : (i + 1) * wide] = value[i * rows : (i + 1) * rows]
    else:
        for (lo, hi), ref in zip(spans, rim_refs):
            ref[...] = rim[lo:hi, :].astype(BF16)
    att_ref[...] = att_s[...].T.astype(BF16)


def kernel_final(sizes, count, tok_ref, w_ref, index_ref, grad_ref, *refs):
    arrived, out_ref = refs[:count], refs[count]
    feat = w_ref.shape[0]
    total = dot_t(grad_ref[:TOKENS, :], w_ref[...])
    padded = index_ref.shape[1]
    parts = [r[...].astype(F32) for r in arrived]
    if paired(sizes):
        even = (lax.axis_index("space") & 1) == 0
        wide = feat // 2
        parts = [jnp.concatenate([p[:, i * wide : (i + 1) * wide] for i in range(3)], axis=0) for p in parts]
        parts = [jnp.concatenate([p[: p.shape[0] // 2], p[p.shape[0] // 2 :]], axis=1) for p in parts]
        parts = [jnp.where(even, parts[1], parts[0]), jnp.where(even, parts[0], parts[1])]
    have = sum(p.shape[0] for p in parts)
    if have < padded:
        parts.append(jnp.zeros((padded - have, feat), F32))
    rim = jnp.concatenate(parts, axis=0).astype(BF16)
    token = lax.broadcasted_iota(jnp.int32, (TOKENS, padded), 0)
    place = jnp.where(token == index_ref[...], 1.0, 0.0).astype(BF16)
    total = total + dot(place, rim)
    standard, inv = normalise(tok_ref[...])
    mean = jnp.mean(total, axis=-1, keepdims=True)
    cross = jnp.mean(total * standard, axis=-1, keepdims=True)
    out_ref[...] = ((total - mean - standard * cross) * inv).astype(BF16)


def shift(value, axis, steps):
    count = lax.axis_size(axis)
    first, last = max(0, -steps), min(count, count - steps)
    return lax.ppermute(value, axis, [(i, i + steps) for i in range(first, last)])


def span(step, length):
    if step < 0:
        return (length - HALO, length)
    if step > 0:
        return (0, HALO)
    return (0, length)


def window_span(step, length):
    if step < 0:
        return (-HALO, 0)
    if step > 0:
        return (length, length + HALO)
    return (0, length)


def struct(shape, dtype):
    return jax.ShapeDtypeStruct(shape, dtype)


def cost(flops, nbytes, exps=0):
    return pl.CostEstimate(flops=int(flops), bytes_accessed=int(nbytes), transcendentals=int(exps))


def exchange(value, axis, mask):
    count = lax.axis_size(axis)
    return lax.ppermute(value, axis, [(i, i ^ mask) for i in range(count)])


def local(tokens, cotangent, weight, margins):
    feat = weight.shape[0]
    tok, cot = tokens[0, 0], cotangent[0, 0]
    n_space, n_sample = lax.axis_size("space"), lax.axis_size("sample")
    grid_cols = min(8, n_space)
    grid_rows = n_space // grid_cols
    sizes = (n_space, grid_cols, grid_rows * TH, grid_cols * TW)
    masks = row_masks(sizes)
    row_steps = (-1, 0, 1) if grid_rows > 1 else (0,)
    steps = [(r, c) for r in row_steps for c in (-1, 0, 1) if (r, c) != (0, 0)]
    counts, pieces, sources = [], [], []
    way = -1 if paired(sizes) else 1
    for r, c in steps:
        (r0, r1), (c0, c1) = window_span(r, TH), window_span(c, TW)
        pieces.append((sum(counts), (r1 - r0) * (c1 - c0), r0, c0, c1 - c0))
        rr, cc = np.meshgrid(np.arange(*span(way * r, TH)), np.arange(*span(way * c, TW)), indexing="ij")
        sources.append((rr * TW + cc).ravel())
        counts.append(pieces[-1][1])
    halo = sum(counts)
    padded = -(-halo // 128) * 128
    keys = TOKENS + padded
    rim_index = np.concatenate([*sources, np.full(padded - halo, -1)]).astype(np.int32)[None, :]
    ends = np.cumsum([0, *counts])
    spans = [(int(a), int(b)) for a, b in zip(ends[:-1], ends[1:])]

    grid = tok.reshape(TH, TW, feat)
    even = (lax.axis_index("space") & 1) == 0
    rims = []
    for r, c in steps:
        (r0, r1), (c0, c1) = span(r, TH), span(c, TW)
        rims.append(grid[r0:r1, c0:c1].reshape(-1, feat))
    if paired(sizes):
        sent = (jnp.where(even, rims[0], rims[1]), jnp.where(even, rims[1], rims[0]))
        halo_tokens = [exchange(v, "space", m) for v, m in zip(sent, masks)]
        halo_tokens += [jnp.zeros_like(rims[0])] * (2 - len(masks))
    else:
        halo_tokens = [shift(v, "space", -(r * grid_cols + c)) for v, (r, c) in zip(rims, steps)]

    q, kv, kvt, nt, bias = pl.pallas_call(
        functools.partial(kernel_own, sizes, pieces),
        out_shape=(
            struct((TOKENS, feat), BF16),
            struct((keys, 2 * feat), BF16),
            struct((2 * feat, keys), BF16),
            struct((feat, keys), BF16),
            struct((keys, TOKENS), F32),
        ),
        in_specs=[hbm()] * 3,
        out_specs=[vmem()] * 5,
        scratch_shapes=[
            pltpu.SMEM(margins.shape, jnp.int32),
            pltpu.VMEM(tok.shape, BF16),
            pltpu.VMEM(weight.shape, BF16),
            pltpu.SemaphoreType.DMA((5,)),
        ],
        compiler_params=params(),
        cost_estimate=cost(8 * TOKENS * feat * feat, 7e6),
        name="own",
    )(margins, tok, weight)

    rim_shape = (2 * counts[0] // 3, 3 * feat // 2)
    outs = pl.pallas_call(
        functools.partial(kernel_attend, sizes, n_sample, spans),
        out_shape=(
            *[struct(a.shape, a.dtype) for a in (kv, kvt, nt)],
            struct((TOKENS, feat), BF16),
            struct((keys, 3 * feat), BF16),
            struct((feat, 3 * feat // 2), F32),
            struct((feat, 3 * feat // 2), BF16),
            *[struct(rim_shape if paired(sizes) else (n, feat), BF16) for n in counts],
        ),
        in_specs=[vmem()] * (4 + len(counts) + 3),
        out_specs=[vmem()] * (7 + len(counts)),
        input_output_aliases={4 + len(counts) + i: i for i in range(3)},
        scratch_shapes=[
            pltpu.VMEM((2, keys, CHUNK), F32),
            pltpu.VMEM((2, keys, CHUNK), F32),
            pltpu.VMEM((keys, 2 * TOKENS), BF16),
            pltpu.VMEM((keys, 2 * TOKENS), BF16),
            pltpu.VMEM((2 * TOKENS, 2 * HEAD), BF16),
            pltpu.VMEM((2 * TOKENS, 2 * HEAD), BF16),
            pltpu.VMEM((feat, TOKENS), F32),
            pltpu.VMEM((feat, TOKENS), F32),
        ],
        compiler_params=params(),
        cost_estimate=cost(48 * TOKENS * keys * feat, 6e6, TOKENS * keys * HEADS),
        name="attend",
    )(q, cot, weight, bias, *halo_tokens, kv, kvt, nt)
    attention, grads, keep, send = outs[3:7]
    rims = list(outs[7:])

    total = keep + exchange(send, "sample", 1).astype(F32)
    half = feat // 2
    first, second = total[:half], total[half:]
    col_masks = [1 << bit for bit in range((n_sample - 1).bit_length() - 1, 0, -1)]
    arrived = []
    if not paired(sizes):
        arrived = [shift(rim, "space", r * grid_cols + c) for (r, c), rim in zip(steps, rims)]

    def by_cols(value):
        for mask in col_masks:
            n = value.shape[1] // 2
            got = exchange(value[:, n:].astype(BF16), "sample", mask)
            value = value[:, :n] + got.astype(F32)
        return value

    def by_rows(value, riders):
        for i, mask in enumerate(masks):
            n = value.shape[0] // 2
            out = value[n:].astype(BF16)
            if riders:
                out = jnp.concatenate([out, riders[i]], axis=0)
            got = exchange(out, "space", mask)
            if riders:
                arrived.append(got[n:])
            value = value[:n] + got[:n].astype(F32)
        return value

    upper = by_rows(by_cols(first), [])
    lower = by_cols(by_rows(second, rims if paired(sizes) else []))
    weight_grad = jnp.concatenate([upper, lower], axis=0)
    arrived += [jnp.zeros_like(rim) for rim in rims[len(arrived) :]]

    token_grad = pl.pallas_call(
        functools.partial(kernel_final, sizes, len(steps)),
        out_shape=struct((TOKENS, feat), BF16),
        in_specs=[vmem()] * (4 + len(steps)),
        out_specs=vmem(),
        compiler_params=params(),
        cost_estimate=cost(6 * TOKENS * feat * feat, 5e6),
        name="final",
    )(tok, weight, jnp.asarray(rim_index), grads, *arrived)
    return (attention[None, None], token_grad[None, None], weight_grad)


def solution(mesh):
    return jax.shard_map(
        local,
        mesh=mesh,
        in_specs=(
            P(("groups", "sample"), "space", None, None),
            P(("groups", "sample"), "space", None, None),
            P("groups", None),
            P(("groups", "sample"), None),
        ),
        out_specs=(
            P(("groups", "sample"), "space", None, None),
            P(("groups", "sample"), "space", None, None),
            P(("groups", "space"), "sample"),
        ),
        check_vma=False,
    )
```

time: 62.3 us -> 55.7 us (0.89)
  starting transfers between devices: 24 us -> 14.3 us
  waiting for transfers between devices: 8.91 us -> 15.8 us
  local copies, waits for them, and re-layouts: 5.35 us -> 3.3 us
  Pallas kernels: 20.7 us -> 19.3 us
    ppermute x12 -> x9, starting transfers between devices: 24 us -> 14.3 us  [exchange(): return lax.ppermute(value, axis, [(i, i ^ mask) for i in range(count)])]
    ppermute x12 -> x9, waiting for transfers between devices: 8.91 us -> 15.8 us  [exchange(): return lax.ppermute(value, axis, [(i, i ^ mask) for i in range(count)])]
    pallas_call x1, Pallas kernels: 16.3 us -> 13.9 us  [local(): pl.pallas_call(functools.partial(kernel_attend, sizes, n_sample, spans),...]
    pallas_call x2, Pallas kernels: 4.36 us -> 5.41 us  [the longest x1 3.28 us: local(): pl.pallas_call(functools.partial(kernel_own, sizes, pieces), out_shape=(s...]
    unnamed x20 -> x14, local copies, waits for them, and re-layouts: 4.16 us -> 3.12 us
    slice x7 -> x8, local copies, waits for them, and re-layouts: 1.1 us -> 0.09 us  [the longest x4 0.05 us: by_rows(): out = value[n:].astype(BF16)]
    concatenate x1 -> x3, other arithmetic: 0.02 us -> 0.72 us  [the longest x1 0.69 us: local(): weight_grad = jnp.concatenate([upper, lower], axis=0)]
  transfers between devices with their start and end apart: 12 -> 9, of which waited for: 5 -> 7; matrix products, arithmetic and copies ran while one was open for 0% -> 0% of each run, Pallas kernels for 7% -> 10%
where the time goes in v3:
time: 55.7 us; the launch traced here: 55.5 us
  Pallas kernels  19.3 us (35%)
  waiting for transfers between devices  15.8 us (28%)
  starting transfers between devices  14.3 us (26%)
  local copies, waits for them, and re-layouts  3.3 us (6%)
  other arithmetic  2.08 us (4%)
  between operations  0.79 us (1%)
    ppermute x9, waiting for transfers between devices, exchange(): return lax.ppermute(value, axis, [(i, i ^ mask) for i in range(count)])  15.8 us
    ppermute x9, starting transfers between devices, exchange(): return lax.ppermute(value, axis, [(i, i ^ mask) for i in range(count)])  14.3 us
    pallas_call x1, Pallas kernels, local(): pl.pallas_call(functools.partial(kernel_attend, sizes, n_sample, spans),...  13.9 us
    pallas_call x1, Pallas kernels, local(): pl.pallas_call(functools.partial(kernel_own, sizes, pieces), out_shape=(s...  3.28 us
    unnamed x14, local copies, waits for them, and re-layouts  3.12 us
    pallas_call x1, Pallas kernels, local(): pl.pallas_call(functools.partial(kernel_final, sizes, len(steps)), out_sh...  2.13 us
  transfers between devices with their start and end apart: 9, of which 7 were waited for; matrix products, arithmetic and copies ran while one was open for 0% of the time, Pallas kernels for 10%

profile of v3, /device:TPU:0, one launch (start us, length us, event | category | flops | bytes accessed | tf_op | source)
XLA Modules:
  0.0 55.5 jit_solution(17606254820982984375)
XLA Ops:
  0.6 1.0 %broadcast_select_fusion = (bf16[16,3,512]{2,1,0:T(4,128)(2,1)S(1)}, bf16[16,3,512]{2,1,0:T(4,128)(2,1)S(1)}) fusion(pred[]{:T(512)S(6)} %eq.3, bf16[16,32,512]{2,1,0:T(8,128)(2,1)} %bitcast.5), kind=kLoop, calls=%fused_computation.14 | loop fusion | flops 49152 | bytes 196609 | tf_op jit(solution)/shard_map/jit(_where)/select_n | solution.py:324
  1.7 3.1 %collective-permute-start = (bf16[48,512]{1,0:T(8,128)(2,1)S(1)}, bf16[48,512]{1,0:T(8,128)(2,1)S(1)}, u32[]{:S(2)}, u32[]{:S(2)}) collective-permute-start(bf16[48,512]{1,0:T(8,128)(2,1)S(1)} %select_n.20), channel_id=1, source_target_pairs={{0,4},{4,0},{8,12},{12,8},{1,5},{5,1},{9,13},{13,9},{2,6},{6,2},{1... | collective-permute-start | bytes 147464 | tf_op jit(solution)/shard_map/ppermute | solution.py:289
  4.9 2.5 %collective-permute-start.1 = (bf16[48,512]{1,0:T(8,128)(2,1)S(1)}, bf16[48,512]{1,0:T(8,128)(2,1)S(1)}, u32[]{:S(2)}, u32[]{:S(2)}) collective-permute-start(bf16[48,512]{1,0:T(8,128)(2,1)S(1)} %select_n.22), channel_id=1, source_target_pairs={{0,12},{4,8},{8,4},{12,0},{1,13},{5,9},{9,5},{13,1},{2,14},{6,10},... | collective-permute-start | bytes 147464 | tf_op jit(solution)/shard_map/ppermute | solution.py:289
  7.4 1.4 %copy-done = bf16[512,1536]{1,0:T(8,128)(2,1)S(1)} copy-done((bf16[512,1536]{1,0:T(8,128)(2,1)S(1)}, bf16[512,1536]{1,0:T(8,128)(2,1)}, u32[]{:S(2)}) %copy-start) | copy-done | bytes 1572888
  8.8 1.0 %copy-done.2 = bf16[1,1,512,512]{3,2,1,0:T(8,128)(2,1)S(1)} copy-done((bf16[1,1,512,512]{3,2,1,0:T(8,128)(2,1)S(1)}, bf16[1,1,512,512]{3,2,1,0:T(8,128)(2,1)}, u32[]{:S(2)}) %copy-start.2) | copy-done | bytes 524312
  9.9 0.7 %copy-done.6 = s32[1,4]{1,0:T(1,128)S(1)} copy-done((s32[1,4]{1,0:T(1,128)S(1)}, s32[1,4]{1,0:T(1,128)}, u32[]{:S(2)}) %copy-start.6) | copy-done | bytes 40
  10.5 3.3 %own.1 = (bf16[512,512]{1,0:T(8,128)(2,1)S(1)}, bf16[640,1024]{1,0:T(8,128)(2,1)S(1)}, bf16[1024,640]{1,0:T(8,128)(2,1)S(1)}, bf16[512,640]{1,0:T(8,128)(2,1)S(1)}, f32[640,512]{1,0:T(8,128)S(1)}) custom-call(s32[1,4]{1,0:T(1,128)S(1)} %copy-done.6, bf16[512,512]{1,0:T(8,128)(2,1)S(1)} %bitcast.6, bf16[512,1536]{1,0:T(8,128)(2,1)S(1)} %copy-done), custom_call_target="tpu_custom_call" | custom-call | flops 1073741824 | bytes 7000000 | tf_op jit(solution)/shard_map/own/pallas_call | solution.py:330
  13.8 0.0 collective-permute-done.refs_0_
  13.8 0.0 collective-permute-done.1.refs_1_
  13.8 0.0 copy-done.1
  13.8 0.0 copy-done.5
  13.8 13.9 %attend.1 = (bf16[640,1024]{1,0:T(8,128)(2,1)S(1)}, bf16[1024,640]{1,0:T(8,128)(2,1)S(1)}, bf16[512,640]{1,0:T(8,128)(2,1)S(1)}, bf16[512,512]{1,0:T(8,128)(2,1)...) custom-call(bf16[512,512]{1,0:T(8,128)(2,1)S(1)} %get-tuple-element., ...), custom_call_target="tpu_custom_call", output_to_operand_aliasing={{0}: (6, {}), {1}: (7, {}), {2}: (8, {})} | custom-call | flops 8053063680 | bytes 6000000 | tf_op jit(solution)/shard_map/attend/pallas_call | solution.py:353
  27.7 0.0 collective-permute-start.2
  27.7 2.3 %collective-permute-done.2 = bf16[512,768]{1,0:T(8,128)(2,1)S(1)} collective-permute-done((bf16[512,768]{1,0:T(8,128)(2,1)S(1)}, bf16[512,768]{1,0:T(8,128)(2,1)S(1)}, u32[]{:S(2)}, u32[]{:S(2)}) %collective-permute-start.2) | collective-permute-done | bytes 786464 | tf_op jit(solution)/shard_map/ppermute | solution.py:289
  30.0 0.2 fusion
  30.2 1.6 %collective-permute-start.5 = (bf16[256,384]{1,0:T(8,128)(2,1)S(1)}, bf16[256,384]{1,0:T(8,128)(2,1)S(1)}, u32[]{:S(2)}, u32[]{:S(2)}) collective-permute-start(bf16[256,384]{1,0:T(8,128)(2,1)S(1)} %slice.93), channel_id=1, source_target_pairs={{0,2},{1,3},{2,0},{3,1},{4,6},{5,7},{6,4},{7,5},{8,10},{9,11},{10,... | collective-permute-start | bytes 589832 | tf_op jit(solution)/shard_map/ppermute | solution.py:289
  31.9 0.7 %collective-permute-start.3 = (bf16[160,768]{1,0:T(8,128)(2,1)S(1)}, bf16[160,768]{1,0:T(8,128)(2,1)S(1)}, u32[]{:S(2)}, u32[]{:S(2)}) collective-permute-start(bf16[160,768]{1,0:T(8,128)(2,1)S(1)} %pad_maximum_fusion), channel_id=1, source_target_pairs={{0,4},{4,0},{8,12},{12,8},{1,5},{5,1},{9,13},{13,9},{2,6},{6,2},{1... | collective-permute-start | bytes 737288 | tf_op jit(solution)/shard_map/ppermute | solution.py:289
  32.6 4.6 %collective-permute-done.5 = bf16[256,384]{1,0:T(8,128)(2,1)S(1)} collective-permute-done((bf16[256,384]{1,0:T(8,128)(2,1)S(1)}, bf16[256,384]{1,0:T(8,128)(2,1)S(1)}, u32[]{:S(2)}, u32[]{:S(2)}) %collective-permute-start.5) | collective-permute-done | bytes 196640 | tf_op jit(solution)/shard_map/ppermute | solution.py:289
  37.3 0.0 copy-start.3
  37.3 0.0 copy-start.4
  37.3 0.7 %collective-permute-start.6 = (bf16[128,384]{1,0:T(8,128)(2,1)S(1)}, bf16[128,384]{1,0:T(8,128)(2,1)S(1)}, u32[]{:S(2)}, u32[]{:S(2)}) collective-permute-start(bf16[128,384]{1,0:T(8,128)(2,1)S(1)} %slice.118), channel_id=1, source_target_pairs={{0,4},{4,0},{8,12},{12,8},{1,5},{5,1},{9,13},{13,9},{2,6},{6,2},{1... | collective-permute-start | bytes 294920 | tf_op jit(solution)/shard_map/ppermute | solution.py:289
  38.1 1.9 %collective-permute-done.3 = bf16[160,768]{1,0:T(8,128)(2,1)S(1)} collective-permute-done((bf16[160,768]{1,0:T(8,128)(2,1)S(1)}, bf16[160,768]{1,0:T(8,128)(2,1)S(1)}, u32[]{:S(2)}, u32[]{:S(2)}) %collective-permute-start.3) | collective-permute-done | bytes 245792 | tf_op jit(solution)/shard_map/ppermute | solution.py:289
  40.0 2.0 %collective-permute-done.6 = bf16[128,384]{1,0:T(8,128)(2,1)S(1)} collective-permute-done((bf16[128,384]{1,0:T(8,128)(2,1)S(1)}, bf16[128,384]{1,0:T(8,128)(2,1)S(1)}, u32[]{:S(2)}, u32[]{:S(2)}) %collective-permute-start.6) | collective-permute-done | bytes 98336 | tf_op jit(solution)/shard_map/ppermute | solution.py:289
  42.0 1.4 %collective-permute-start.7 = (bf16[64,384]{1,0:T(8,128)(2,1)S(1)}, bf16[64,384]{1,0:T(8,128)(2,1)S(1)}, u32[]{:S(2)}, u32[]{:S(2)}) collective-permute-start(bf16[64,384]{1,0:T(8,128)(2,1)S(1)} %slice.121), channel_id=1, source_target_pairs={{0,12},{4,8},{8,4},{12,0},{1,13},{5,9},{9,5},{13,1},{2,14},{6,10},... | collective-permute-start | bytes 147464 | tf_op jit(solution)/shard_map/ppermute | solution.py:289
  43.5 2.5 %collective-permute-start.4 = (bf16[96,768]{1,0:T(8,128)(2,1)S(1)}, bf16[96,768]{1,0:T(8,128)(2,1)S(1)}, u32[]{:S(2)}, u32[]{:S(2)}) collective-permute-start(bf16[96,768]{1,0:T(8,128)(2,1)S(1)} %pad_maximum_fusion.2), channel_id=1, source_target_pairs={{0,12},{4,8},{8,4},{12,0},{1,13},{5,9},{9,5},{13,1},{2,14},{6,10},... | collective-permute-start | bytes 442376 | tf_op jit(solution)/shard_map/ppermute | solution.py:289
  46.0 2.4 %collective-permute-done.7 = bf16[64,384]{1,0:T(8,128)(2,1)S(1)} collective-permute-done((bf16[64,384]{1,0:T(8,128)(2,1)S(1)}, bf16[64,384]{1,0:T(8,128)(2,1)S(1)}, u32[]{:S(2)}, u32[]{:S(2)}) %collective-permute-start.7) | collective-permute-done | bytes 49184 | tf_op jit(solution)/shard_map/ppermute | solution.py:289
  48.4 2.2 %collective-permute-done.4 = bf16[96,768]{1,0:T(8,128)(2,1)S(1)} collective-permute-done((bf16[96,768]{1,0:T(8,128)(2,1)S(1)}, bf16[96,768]{1,0:T(8,128)(2,1)S(1)}, u32[]{:S(2)}, u32[]{:S(2)}) %collective-permute-start.4) | collective-permute-done | bytes 147488 | tf_op jit(solution)/shard_map/ppermute | solution.py:289
  50.6 1.6 %collective-permute-start.8 = (bf16[64,384]{1,0:T(8,128)(2,1)S(1)}, bf16[64,384]{1,0:T(8,128)(2,1)S(1)}, u32[]{:S(2)}, u32[]{:S(2)}) collective-permute-start(bf16[64,384]{1,0:T(8,128)(2,1)S(1)} %slice.120), channel_id=1, source_target_pairs={{0,2},{1,3},{2,0},{3,1},{4,6},{5,7},{6,4},{7,5},{8,10},{9,11},{10,... | collective-permute-start | bytes 147464 | tf_op jit(solution)/shard_map/ppermute | solution.py:289
  52.2 0.0 copy-done.4
  52.2 2.1 %final.1 = bf16[512,512]{1,0:T(8,128)(2,1)} custom-call(bf16[512,512]{1,0:T(8,128)(2,1)S(1)} %bitcast.7, bf16[512,1536]{1,0:T(8,128)(2,1)S(1)} %copy-done.1, s32[1,128]{1,0:T(1,128)S(1)} %copy-done.4, bf16[640,1536]{1,0:T(8,128)(2,1)S(1)} %get-tuple-element.20.grad_ref, bf16[32,768]{1,0:T(8,128)(2,1)S(1)} %slice.87.refs_0_, bf16[32,768]{1,0:T(8,128)(2,1)S(1)} %slice.91.refs_1_), custom_call_target="tpu_custom_call" | custom-call | flops 805306368 | bytes 5000000 | tf_op jit(solution)/shard_map/final/pallas_call | solution.py:415
  54.4 0.4 collective-permute-done.8
  54.8 0.7 %pad_maximum_fusion.1 = f32[128,384]{1,0:T(8,128)} fusion(f32[64,384]{1,0:T(8,128)S(1)} %slice_add_fusion.4, f32[64,384]{1,0:T(8,128)S(1)} %slice_add_fusion.5), kind=kLoop, calls=%fused_computation.8 | loop fusion | flops 49152 | bytes 393216 | tf_op jit(solution)/shard_map/concatenate | solution.py:412
  (24 shorter events, 0.4 us)
Async XLA Ops:
  1.7 12.1 %collective-permute-start = (bf16[48,512]{1,0:T(8,128)(2,1)S(1)}, bf16[48,512]{1,0:T(8,128)(2,1)S(1)}, u32[]{:S(2)}, u32[]{:S(2)}) collective-permute-start(bf16[48,512]{1,0:T(8,128)(2,1)S(1)} %select_n.20), channel_id=1, source_target_pairs={{0,4},{4,0},{8,12},{12,8},{1,5},{5,1},{9,13},{13,9},{2,6},{6,2},{1... | collective-permute-start | bytes 147464 | tf_op jit(solution)/shard_map/ppermute | solution.py:289
  4.9 8.9 %collective-permute-start.1 = (bf16[48,512]{1,0:T(8,128)(2,1)S(1)}, bf16[48,512]{1,0:T(8,128)(2,1)S(1)}, u32[]{:S(2)}, u32[]{:S(2)}) collective-permute-start(bf16[48,512]{1,0:T(8,128)(2,1)S(1)} %select_n.22), channel_id=1, source_target_pairs={{0,12},{4,8},{8,4},{12,0},{1,13},{5,9},{9,5},{13,1},{2,14},{6,10},... | collective-permute-start | bytes 147464 | tf_op jit(solution)/shard_map/ppermute | solution.py:289
  7.4 1.4 %copy-start = (bf16[512,1536]{1,0:T(8,128)(2,1)S(1)}, bf16[512,1536]{1,0:T(8,128)(2,1)}, u32[]{:S(2)}) copy-start(bf16[512,1536]{1,0:T(8,128)(2,1)} %w_ref.3) | copy-start | bytes 4718596
  8.8 1.0 %copy-start.2 = (bf16[1,1,512,512]{3,2,1,0:T(8,128)(2,1)S(1)}, bf16[1,1,512,512]{3,2,1,0:T(8,128)(2,1)}, u32[]{:S(2)}) copy-start(bf16[1,1,512,512]{3,2,1,0:T(8,128)(2,1)} %param.5) | copy-start | bytes 1572868
  9.9 0.7 %copy-start.6 = (s32[1,4]{1,0:T(1,128)S(1)}, s32[1,4]{1,0:T(1,128)}, u32[]{:S(2)}) copy-start(s32[1,4]{1,0:T(1,128)} %margin_hbm.1) | copy-start | bytes 52
  10.5 3.3 %copy-start.1 = (bf16[512,1536]{1,0:T(8,128)(2,1)S(1)}, bf16[512,1536]{1,0:T(8,128)(2,1)}, u32[]{:S(2)}) copy-start(bf16[512,1536]{1,0:T(8,128)(2,1)} %w_ref.3) | copy-start | bytes 4718596
  10.5 3.3 %copy-start.5 = (bf16[1,1,512,512]{3,2,1,0:T(8,128)(2,1)S(1)}, bf16[1,1,512,512]{3,2,1,0:T(8,128)(2,1)}, u32[]{:S(2)}) copy-start(bf16[1,1,512,512]{3,2,1,0:T(8,128)(2,1)} %param.6) | copy-start | bytes 1572868
  27.7 2.3 %collective-permute-start.2 = (bf16[512,768]{1,0:T(8,128)(2,1)S(1)}, bf16[512,768]{1,0:T(8,128)(2,1)S(1)}, u32[]{:S(2)}, u32[]{:S(2)}) collective-permute-start(bf16[512,768]{1,0:T(8,128)(2,1)S(1)} %get-tuple-element.22), channel_id=1, source_target_pairs={{0,1},{1,0},{2,3},{3,2},{4,5},{5,4},{6,7},{7,6},{8,9},{9,8},{10,11... | collective-permute-start | bytes 2359304 | tf_op jit(solution)/shard_map/ppermute | solution.py:289
  30.2 7.0 %collective-permute-start.5 = (bf16[256,384]{1,0:T(8,128)(2,1)S(1)}, bf16[256,384]{1,0:T(8,128)(2,1)S(1)}, u32[]{:S(2)}, u32[]{:S(2)}) collective-permute-start(bf16[256,384]{1,0:T(8,128)(2,1)S(1)} %slice.93), channel_id=1, source_target_pairs={{0,2},{1,3},{2,0},{3,1},{4,6},{5,7},{6,4},{7,5},{8,10},{9,11},{10,... | collective-permute-start | bytes 589832 | tf_op jit(solution)/shard_map/ppermute | solution.py:289
  31.9 8.1 %collective-permute-start.3 = (bf16[160,768]{1,0:T(8,128)(2,1)S(1)}, bf16[160,768]{1,0:T(8,128)(2,1)S(1)}, u32[]{:S(2)}, u32[]{:S(2)}) collective-permute-start(bf16[160,768]{1,0:T(8,128)(2,1)S(1)} %pad_maximum_fusion), channel_id=1, source_target_pairs={{0,4},{4,0},{8,12},{12,8},{1,5},{5,1},{9,13},{13,9},{2,6},{6,2},{1... | collective-permute-start | bytes 737288 | tf_op jit(solution)/shard_map/ppermute | solution.py:289
  37.3 14.9 %copy-start.3 = (bf16[1,1,512,512]{3,2,1,0:T(8,128)(2,1)S(1)}, bf16[1,1,512,512]{3,2,1,0:T(8,128)(2,1)}, u32[]{:S(2)}) copy-start(bf16[1,1,512,512]{3,2,1,0:T(8,128)(2,1)} %param.5) | copy-start | bytes 1572868
  37.3 14.9 %copy-start.4 = (s32[1,128]{1,0:T(1,128)S(1)}, s32[1,128]{1,0:T(1,128)}, u32[]{:S(2)}) copy-start(s32[1,128]{1,0:T(1,128)} %constant.11.clone.index_ref) | copy-start | bytes 1540
  37.3 4.7 %collective-permute-start.6 = (bf16[128,384]{1,0:T(8,128)(2,1)S(1)}, bf16[128,384]{1,0:T(8,128)(2,1)S(1)}, u32[]{:S(2)}, u32[]{:S(2)}) collective-permute-start(bf16[128,384]{1,0:T(8,128)(2,1)S(1)} %slice.118), channel_id=1, source_target_pairs={{0,4},{4,0},{8,12},{12,8},{1,5},{5,1},{9,13},{13,9},{2,6},{6,2},{1... | collective-permute-start | bytes 294920 | tf_op jit(solution)/shard_map/ppermute | solution.py:289
  42.0 6.3 %collective-permute-start.7 = (bf16[64,384]{1,0:T(8,128)(2,1)S(1)}, bf16[64,384]{1,0:T(8,128)(2,1)S(1)}, u32[]{:S(2)}, u32[]{:S(2)}) collective-permute-start(bf16[64,384]{1,0:T(8,128)(2,1)S(1)} %slice.121), channel_id=1, source_target_pairs={{0,12},{4,8},{8,4},{12,0},{1,13},{5,9},{9,5},{13,1},{2,14},{6,10},... | collective-permute-start | bytes 147464 | tf_op jit(solution)/shard_map/ppermute | solution.py:289
  43.5 7.1 %collective-permute-start.4 = (bf16[96,768]{1,0:T(8,128)(2,1)S(1)}, bf16[96,768]{1,0:T(8,128)(2,1)S(1)}, u32[]{:S(2)}, u32[]{:S(2)}) collective-permute-start(bf16[96,768]{1,0:T(8,128)(2,1)S(1)} %pad_maximum_fusion.2), channel_id=1, source_target_pairs={{0,12},{4,8},{8,4},{12,0},{1,13},{5,9},{9,5},{13,1},{2,14},{6,10},... | collective-permute-start | bytes 442376 | tf_op jit(solution)/shard_map/ppermute | solution.py:289
  50.6 4.2 %collective-permute-start.8 = (bf16[64,384]{1,0:T(8,128)(2,1)S(1)}, bf16[64,384]{1,0:T(8,128)(2,1)S(1)}, u32[]{:S(2)}, u32[]{:S(2)}) collective-permute-start(bf16[64,384]{1,0:T(8,128)(2,1)S(1)} %slice.120), channel_id=1, source_target_pairs={{0,2},{1,3},{2,0},{3,1},{4,6},{5,7},{6,4},{7,5},{8,10},{9,11},{10,... | collective-permute-start | bytes 147464 | tf_op jit(solution)/shard_map/ppermute | solution.py:289

commit v4 on v3

v4 whole, which is shorter than its diff:
```python
import functools
import math

import jax
import jax.numpy as jnp
import numpy as np
from jax import lax
from jax.experimental import pallas as pl
from jax.experimental.pallas import tpu as pltpu
from jax.sharding import PartitionSpec as P

HEADS = 8
HEAD = 64
TH = 16
TW = 32
HALO = 3
TOKENS = TH * TW
NEG = -1e30
LAST = (((1,), (1,)), ((), ()))
F32 = jnp.float32
BF16 = jnp.bfloat16
PACK = 1e6
OWN = 24
ROWS = 64

vmem = functools.partial(pl.BlockSpec, memory_space=pltpu.VMEM)
hbm = functools.partial(pl.BlockSpec, memory_space=pltpu.HBM)


def params(mib=24):
    return pltpu.CompilerParams(vmem_limit_bytes=mib * 1024 * 1024)


def dot(a, b):
    return jnp.dot(a, b, preferred_element_type=F32)


def dot_t(a, b):
    return lax.dot_general(a, b, LAST, preferred_element_type=F32)


def normalise(tok):
    tok = tok.astype(F32)
    centred = tok - jnp.mean(tok, axis=-1, keepdims=True)
    inv = lax.rsqrt(jnp.mean(centred * centred, axis=-1, keepdims=True) + 1e-05)
    return centred * inv, inv


def own_ids(cols):
    position = lax.axis_index("space")
    member = lax.axis_index("sample")
    return position, member, position // cols, position % cols


def live(row, col, margin_ref, rows, cols):
    return (
        (row >= margin_ref[0, 0])
        & (row < rows - margin_ref[0, 1])
        & (col >= margin_ref[0, 2])
        & (col < cols - margin_ref[0, 3])
    )


def row_masks(sizes):
    bits = (sizes[0] - 1).bit_length()
    one_row = sizes[1] == sizes[0]
    return [((2 << i) - 1) if one_row else (1 << i) for i in range(bits)]


def paired(sizes):
    return sizes[1] == sizes[0] and sizes[0] in (2, 4)


def row_split(feat, n_space):
    size = feat // n_space
    return size * 5 // 8 // 16 * 16 if size >= 64 else size // 2


def permutation(feat, sizes, position):
    masks = row_masks(sizes)
    size = feat // sizes[0]
    upper = row_split(feat, sizes[0])
    row = lax.broadcasted_iota(jnp.int32, (feat, 128), 0)
    below = row >= upper * sizes[0]
    at = jnp.where(below, row - upper * sizes[0], row)
    relative = jnp.where(below, at // (size - upper), at // upper)
    rest = at - relative * jnp.where(below, size - upper, upper)
    space = jnp.zeros_like(row) + position
    for i, mask in enumerate(masks):
        space = space ^ (((relative >> (len(masks) - 1 - i)) & 1) * mask)
    source = space * size + jnp.where(below, upper, 0) + rest
    col = lax.broadcasted_iota(jnp.int32, (feat, 128), 1)
    return jnp.concatenate(
        [jnp.where(col + i == source, 1.0, 0.0).astype(BF16) for i in range(0, feat, 128)], axis=1
    )


def kernel_pack(sizes, pieces, tok_hbm, *refs):
    rim_refs, (tok_ref, sem) = refs[: len(pieces)], refs[len(pieces) :]
    copy = pltpu.make_async_copy(tok_hbm, tok_ref, sem)
    copy.start()
    even = (lax.axis_index("space") & 1) == 0
    total = sum(p[1] for p in pieces)
    rows = -(-total // 16) * 16
    index = lax.broadcasted_iota(jnp.int32, (rows, TOKENS), 0)
    token = lax.broadcasted_iota(jnp.int32, (rows, TOKENS), 1)
    wanted = jnp.full((rows, TOKENS), -1, jnp.int32)
    for i, (start, count, _, _, wide, r0, c0) in enumerate(pieces):
        at = index - start
        down = (at * 171) >> 9 if wide == 3 else at // wide
        source = (r0 + down) * TW + c0 + at - down * wide
        if paired(sizes):
            source = source + jnp.where(even, 0, pieces[1 - i][6] - c0)
        wanted = jnp.where((at >= 0) & (at < count), source, wanted)
    select = jnp.where(wanted == token, 1.0, 0.0).astype(BF16)
    copy.wait()
    rims = dot(select, tok_ref[...])
    for (start, count, *_), ref in zip(pieces, rim_refs):
        ref[...] = rims[start : start + count].astype(BF16)


def kernel_own(
    sizes, pieces, margin_hbm, tok_hbm, w_hbm, q_ref, kv_ref, kvt_ref, nt_ref, bias_ref, place_ref, margin_ref, tok_ref, w_ref, sems
):
    feat = w_hbm.shape[0]
    copies = [pltpu.make_async_copy(tok_hbm, tok_ref, sems.at[0])]
    for i in range(3):
        cols = pl.ds(i * feat, feat)
        copies.append(pltpu.make_async_copy(w_hbm.at[:, cols], w_ref.at[:, cols], sems.at[1 + i]))
    copies.append(pltpu.make_async_copy(margin_hbm, margin_ref, sems.at[4]))
    for copy in copies:
        copy.start()
    n_space, grid_cols, plane_rows, plane_cols = sizes
    position, member, tile_row, tile_col = own_ids(grid_cols)
    place = permutation(feat, sizes, position)
    place_ref[...] = place
    copies[0].wait()
    standard, _ = normalise(tok_ref[...])
    normed = standard.astype(BF16)
    nt_ref[:, :TOKENS] = dot_t(place, normed).astype(BF16)
    scale = 1.0 / math.sqrt(HEAD)
    copies[1].wait()
    q_ref[...] = (dot(normed, w_ref[:, :feat]).astype(BF16).astype(F32) * scale).astype(BF16)
    for i in range(2):
        copies[2 + i].wait()
        part = dot(normed, w_ref[:, (i + 1) * feat : (i + 2) * feat]).astype(BF16)
        kv_ref[:TOKENS, i * feat : (i + 1) * feat] = part
        kvt_ref[i * feat : (i + 1) * feat, :TOKENS] = part.T
    copies[4].wait()
    key = lax.broadcasted_iota(jnp.int32, (TOKENS, 128), 0)
    query = lax.broadcasted_iota(jnp.int32, (TOKENS, 128), 1)
    row = tile_row * TH + key // TW
    col = tile_col * TW + key % TW
    bias = jnp.where(live(row, col, margin_ref, plane_rows, plane_cols), 0.0, NEG)
    for i in range(0, TOKENS, 128):
        bias_ref[:TOKENS, i : i + 128] = jnp.where(key == query + i, 0.0, bias)
    padded = bias_ref.shape[0] - TOKENS
    index = lax.broadcasted_iota(jnp.int32, (padded, 128), 0)
    row = jnp.full((padded, 128), -1, jnp.int32)
    col = row
    for start, count, r0, c0, wide, *_ in pieces:
        at = index - start
        down = (at * 171) >> 9 if wide == 3 else at // wide
        here = (at >= 0) & (at < count)
        row = jnp.where(here, tile_row * TH + r0 + down, row)
        col = jnp.where(here, tile_col * TW + c0 + at - down * wide, col)
    is_open = live(row, col, margin_ref, plane_rows, plane_cols)
    is_open = is_open & (row >= 0) & (row < plane_rows) & (col >= 0) & (col < plane_cols)
    bias = jnp.where(is_open, 0.0, NEG)
    for i in range(0, TOKENS, 128):
        bias_ref[TOKENS:, i : i + 128] = bias


def kernel_attend(sizes, n_sample, spans, q_ref, cot_ref, w_ref, bias_ref, place_ref, *refs):
    n_space, grid_cols, plane_rows, plane_cols = sizes
    count = len(spans)
    toks, refs = refs[:count], refs[count + 3 :]
    kv_ref, kvt_ref, nt_ref, pb_ref, grad_ref, keep_ref, send_ref = refs[:7]
    rim_refs, refs = refs[7 : 7 + count], refs[7 + count :]
    s_s, g_s, ds_s, cm_s, qm_s, dqt_s = refs
    position, member, _, _ = own_ids(grid_cols)
    feat = w_ref.shape[0]
    keys = kv_ref.shape[0]
    padded = keys - TOKENS
    scale = 1.0 / math.sqrt(HEAD)

    parts = [r[...].astype(F32) for r in toks]
    even = (position & 1) == 0
    if paired(sizes):
        parts = [jnp.where(even, parts[1], parts[0]), jnp.where(even, parts[0], parts[1])]
    if spans[-1][1] < padded:
        parts.append(jnp.zeros((padded - spans[-1][1], feat), F32))
    standard, _ = normalise(jnp.concatenate(parts, axis=0))
    normed = standard.astype(BF16)
    for i in range(2):
        part = dot(normed, w_ref[:, (i + 1) * feat : (i + 2) * feat]).astype(BF16)
        kv_ref[TOKENS:, i * feat : (i + 1) * feat] = part
        kvt_ref[i * feat : (i + 1) * feat, TOKENS:] = part.T
    nt_ref[:, TOKENS:] = dot_t(place_ref[...], normed).astype(BF16)
    lane = lax.broadcasted_iota(jnp.int32, (TOKENS, 2 * HEAD), 1)

    def scores(head):
        slot, base = head % 2, head // 2 * 2 * HEAD
        cols = slice(base, base + 2 * HEAD)
        vcols = slice(feat + base, feat + base + 2 * HEAD)
        mine = (lane >= HEAD) if slot else (lane < HEAD)
        out = slice((head % 4) * TOKENS, (head % 4 + 1) * TOKENS)
        q, cot = q_ref[:, cols], cot_ref[:, cols]
        qm_s[out, :] = jnp.where(mine, q, jnp.zeros_like(q))
        cm_s[out, :] = jnp.where(mine, cot, jnp.zeros_like(cot))
        s_s[slot] = dot_t(kv_ref[:, cols], qm_s[out, :])
        g_s[slot] = dot_t(kv_ref[:, vcols], cm_s[out, :])

    def softmax(head):
        slot = head % 2
        out = slice(slot * TOKENS, (slot + 1) * TOKENS)
        top = jnp.full((8, TOKENS), NEG, F32)
        for r in range(0, keys, ROWS):
            x = s_s[slot, r : r + ROWS, :] + bias_ref[r : r + ROWS, :]
            top = jnp.maximum(top, jnp.max(x.reshape(ROWS // 8, 8, TOKENS), axis=0))
        top = jnp.max(top, axis=0, keepdims=True)
        total = jnp.zeros((8, TOKENS), F32)
        delta = jnp.zeros((8, TOKENS), F32)
        for r in range(0, keys, ROWS):
            x = s_s[slot, r : r + ROWS, :] + bias_ref[r : r + ROWS, :]
            e = jnp.exp(x - top)
            s_s[slot, r : r + ROWS, :] = e
            total = total + jnp.sum(e.reshape(ROWS // 8, 8, TOKENS), axis=0)
            eg = e * g_s[slot, r : r + ROWS, :]
            delta = delta + jnp.sum(eg.reshape(ROWS // 8, 8, TOKENS), axis=0)
        inv = 1.0 / jnp.sum(total, axis=0, keepdims=True)
        delta = jnp.sum(delta, axis=0, keepdims=True) * inv
        for r in range(0, keys, ROWS):
            p = s_s[slot, r : r + ROWS, :] * inv
            pb_ref[head // 2, r : r + ROWS, out] = p.astype(BF16)
            ds_s[r : r + ROWS, out] = (p * (g_s[slot, r : r + ROWS, :] - delta)).astype(BF16)

    def products(head):
        row = head * HEAD
        out = slice((head % 2) * TOKENS, (head % 2 + 1) * TOKENS)
        dqt_s[row : row + HEAD, :] = scale * dot(kvt_ref[row : row + HEAD, :], ds_s[:, out])
        if head % 2:
            base = head // 2 * 2 * HEAD
            both = slice((head % 4 - 1) * TOKENS, (head % 4 + 1) * TOKENS)
            grad_ref[:, feat + base : feat + base + 2 * HEAD] = dot(ds_s[...], qm_s[both, :]).astype(BF16)
            grad_ref[:, 2 * feat + base : 2 * feat + base + 2 * HEAD] = dot(
                pb_ref[head // 2], cm_s[both, :]
            ).astype(BF16)

    scores(0)
    for head in range(HEADS):
        if head + 1 < HEADS:
            scores(head + 1)
        softmax(head)
        products(head)
    grad_ref[:TOKENS, :feat] = dqt_s[...].T.astype(BF16)
    grad_ref[TOKENS:, :feat] = jnp.zeros((padded, feat), BF16)

    block = 3 * feat // n_sample
    for j in range(n_sample // 2):
        for target, other in ((keep_ref, 2 * j), (send_ref, 2 * j + 1)):
            cols = pl.ds(pl.multiple_of((member ^ other) * block, 128), block)
            value = dot(nt_ref[...], grad_ref[:, cols])
            target[:, j * block : (j + 1) * block] = value.astype(target.dtype)
    rim = dot_t(grad_ref[TOKENS:, feat:], w_ref[:, feat:])
    if paired(sizes):
        rows = rim_refs[0].shape[0]
        left, right = (rim[lo:hi, :] for lo, hi in spans)
        for ref, value in zip(rim_refs, (jnp.where(even, right, left), jnp.where(even, left, right))):
            wide = feat // 2
            value = jnp.concatenate([value[:, :wide], value[:, wide:]], axis=0).astype(BF16)
            for i in range(3):
                ref[:, i * wide : (i + 1) * wide] = value[i * rows : (i + 1) * rows]
    else:
        for (lo, hi), ref in zip(spans, rim_refs):
            ref[...] = rim[lo:hi, :].astype(BF16)


def kernel_mix(kvt_ref, pb_ref, att_ref, att_s):
    feat = att_ref.shape[1]
    for head in range(HEADS):
        row = head * HEAD
        out = slice((head % 2) * TOKENS, (head % 2 + 1) * TOKENS)
        att_s[row : row + HEAD, :] = dot(kvt_ref[feat + row : feat + row + HEAD, :], pb_ref[head // 2, :, out])
    att_ref[...] = att_s[...].T.astype(BF16)


def kernel_final(sizes, count, tok_ref, w_ref, index_ref, grad_ref, *refs):
    arrived, out_ref = refs[:count], refs[count]
    feat = w_ref.shape[0]
    total = dot_t(grad_ref[:TOKENS, :], w_ref[...])
    padded = index_ref.shape[1]
    parts = [r[...].astype(F32) for r in arrived]
    if paired(sizes):
        even = (lax.axis_index("space") & 1) == 0
        wide = feat // 2
        parts = [jnp.concatenate([p[:, i * wide : (i + 1) * wide] for i in range(3)], axis=0) for p in parts]
        parts = [jnp.concatenate([p[: p.shape[0] // 2], p[p.shape[0] // 2 :]], axis=1) for p in parts]
        parts = [jnp.where(even, parts[1], parts[0]), jnp.where(even, parts[0], parts[1])]
    have = sum(p.shape[0] for p in parts)
    if have < padded:
        parts.append(jnp.zeros((padded - have, feat), F32))
    rim = jnp.concatenate(parts, axis=0).astype(BF16)
    token = lax.broadcasted_iota(jnp.int32, (TOKENS, padded), 0)
    place = jnp.where(token == index_ref[...], 1.0, 0.0).astype(BF16)
    total = total + dot(place, rim)
    standard, inv = normalise(tok_ref[...])
    mean = jnp.mean(total, axis=-1, keepdims=True)
    cross = jnp.mean(total * standard, axis=-1, keepdims=True)
    out_ref[...] = ((total - mean - standard * cross) * inv).astype(BF16)


def shift(value, axis, steps):
    count = lax.axis_size(axis)
    first, last = max(0, -steps), min(count, count - steps)
    return lax.ppermute(value, axis, [(i, i + steps) for i in range(first, last)])


def span(step, length):
    if step < 0:
        return (length - HALO, length)
    if step > 0:
        return (0, HALO)
    return (0, length)


def window_span(step, length):
    if step < 0:
        return (-HALO, 0)
    if step > 0:
        return (length, length + HALO)
    return (0, length)


def struct(shape, dtype):
    return jax.ShapeDtypeStruct(shape, dtype)


def pinned(value):
    return pltpu.with_memory_space_constraint(value, pltpu.HBM)


def cost(flops, nbytes, exps=0):
    return pl.CostEstimate(flops=int(flops), bytes_accessed=int(nbytes), transcendentals=int(exps))


def exchange(value, axis, mask):
    count = lax.axis_size(axis)
    return lax.ppermute(value, axis, [(i, i ^ mask) for i in range(count)])


def local(tokens, cotangent, weight, margins):
    feat = weight.shape[0]
    tok, cot = tokens[0, 0], cotangent[0, 0]
    n_space, n_sample = lax.axis_size("space"), lax.axis_size("sample")
    grid_cols = min(8, n_space)
    grid_rows = n_space // grid_cols
    sizes = (n_space, grid_cols, grid_rows * TH, grid_cols * TW)
    masks = row_masks(sizes)
    row_steps = (-1, 0, 1) if grid_rows > 1 else (0,)
    steps = [(r, c) for r in row_steps for c in (-1, 0, 1) if (r, c) != (0, 0)]
    counts, pieces, sources = [], [], []
    way = -1 if paired(sizes) else 1
    for r, c in steps:
        (r0, r1), (c0, c1) = window_span(r, TH), window_span(c, TW)
        pieces.append((sum(counts), (r1 - r0) * (c1 - c0), r0, c0, c1 - c0, span(r, TH)[0], span(c, TW)[0]))
        rr, cc = np.meshgrid(np.arange(*span(way * r, TH)), np.arange(*span(way * c, TW)), indexing="ij")
        sources.append((rr * TW + cc).ravel())
        counts.append(pieces[-1][1])
    halo = sum(counts)
    padded = -(-halo // 128) * 128
    keys = TOKENS + padded
    rim_index = np.concatenate([*sources, np.full(padded - halo, -1)]).astype(np.int32)[None, :]
    ends = np.cumsum([0, *counts])
    spans = [(int(a), int(b)) for a, b in zip(ends[:-1], ends[1:])]

    rims = pl.pallas_call(
        functools.partial(kernel_pack, sizes, pieces),
        out_shape=[struct((n, feat), BF16) for n in counts],
        in_specs=[hbm()],
        out_specs=[vmem()] * len(counts),
        scratch_shapes=[pltpu.VMEM(tok.shape, BF16), pltpu.SemaphoreType.DMA],
        compiler_params=params(16),
        cost_estimate=cost(2 * halo * TOKENS * feat, PACK),
        name="pack",
    )(pinned(tok))
    if paired(sizes):
        halo_tokens = [exchange(v, "space", m) for v, m in zip(rims, masks)]
        halo_tokens += [jnp.zeros_like(rims[0])] * (2 - len(masks))
    else:
        halo_tokens = [shift(v, "space", -(r * grid_cols + c)) for v, (r, c) in zip(rims, steps)]

    q, kv, kvt, nt, bias, place = pl.pallas_call(
        functools.partial(kernel_own, sizes, pieces),
        out_shape=(
            struct((TOKENS, feat), BF16),
            struct((keys, 2 * feat), BF16),
            struct((2 * feat, keys), BF16),
            struct((feat, keys), BF16),
            struct((keys, TOKENS), F32),
            struct((feat, feat), BF16),
        ),
        in_specs=[hbm()] * 3,
        out_specs=[vmem()] * 6,
        scratch_shapes=[
            pltpu.SMEM(margins.shape, jnp.int32),
            pltpu.VMEM(tok.shape, BF16),
            pltpu.VMEM(weight.shape, BF16),
            pltpu.SemaphoreType.DMA((5,)),
        ],
        compiler_params=params(OWN),
        cost_estimate=cost(8 * TOKENS * feat * feat, 7e6),
        name="own",
    )(*(pinned(a) for a in (margins, tok, weight)))

    rim_shape = (2 * counts[0] // 3, 3 * feat // 2)
    outs = pl.pallas_call(
        functools.partial(kernel_attend, sizes, n_sample, spans),
        out_shape=(
            *[struct(a.shape, a.dtype) for a in (kv, kvt, nt)],
            struct((HEADS // 2, keys, 2 * TOKENS), BF16),
            struct((keys, 3 * feat), BF16),
            struct((feat, 3 * feat // 2), F32),
            struct((feat, 3 * feat // 2), BF16),
            *[struct(rim_shape if paired(sizes) else (n, feat), BF16) for n in counts],
        ),
        in_specs=[vmem()] * (5 + len(counts) + 3),
        out_specs=[vmem()] * (7 + len(counts)),
        input_output_aliases={5 + len(counts) + i: i for i in range(3)},
        scratch_shapes=[
            pltpu.VMEM((2, keys, TOKENS), F32),
            pltpu.VMEM((2, keys, TOKENS), F32),
            pltpu.VMEM((keys, 2 * TOKENS), BF16),
            pltpu.VMEM((4 * TOKENS, 2 * HEAD), BF16),
            pltpu.VMEM((4 * TOKENS, 2 * HEAD), BF16),
            pltpu.VMEM((feat, TOKENS), F32),
        ],
        compiler_params=params(),
        cost_estimate=cost(48 * TOKENS * keys * feat, 6e6, TOKENS * keys * HEADS),
        name="attend",
    )(q, cot, weight, bias, place, *halo_tokens, kv, kvt, nt)
    kvt, prob = outs[1], outs[3]
    grads, keep, send = outs[4:7]
    rims = list(outs[7:])

    total = keep + exchange(send, "sample", 1).astype(F32)
    half = row_split(feat, n_space) * n_space
    first, second = total[:half], total[half:]
    col_masks = [1 << bit for bit in range((n_sample - 1).bit_length() - 1, 0, -1)]
    arrived = []
    if not paired(sizes):
        arrived = [shift(rim, "space", r * grid_cols + c) for (r, c), rim in zip(steps, rims)]

    def by_cols(value):
        for mask in col_masks:
            n = value.shape[1] // 2
            got = exchange(value[:, n:].astype(BF16), "sample", mask)
            value = value[:, :n] + got.astype(F32)
        return value

    def by_rows(value, riders):
        for i, mask in enumerate(masks):
            n = value.shape[0] // 2
            out = value[n:].astype(BF16)
            if riders:
                out = jnp.concatenate([out, riders[i]], axis=0)
            got = exchange(out, "space", mask)
            if riders:
                arrived.append(got[n:])
            value = value[:n] + got[:n].astype(F32)
        return value

    upper = by_rows(by_cols(first), [])
    lower = by_cols(by_rows(second, rims if paired(sizes) else []))
    weight_grad = jnp.concatenate([upper, lower], axis=0)

    attention = pl.pallas_call(
        kernel_mix,
        out_shape=struct((TOKENS, feat), BF16),
        in_specs=[vmem()] * 2,
        out_specs=vmem(),
        scratch_shapes=[pltpu.VMEM((feat, TOKENS), F32)],
        compiler_params=params(8),
        cost_estimate=cost(8 * TOKENS * keys * feat, 6e6),
        name="mix",
    )(kvt, prob)
    arrived += [jnp.zeros_like(rim) for rim in rims[len(arrived) :]]

    token_grad = pl.pallas_call(
        functools.partial(kernel_final, sizes, len(steps)),
        out_shape=struct((TOKENS, feat), BF16),
        in_specs=[vmem()] * (4 + len(steps)),
        out_specs=vmem(),
        compiler_params=params(16),
        cost_estimate=cost(6 * TOKENS * feat * feat, 5e6),
        name="final",
    )(tok, weight, jnp.asarray(rim_index), grads, *arrived)
    return (attention[None, None], token_grad[None, None], weight_grad)


def solution(mesh):
    return jax.shard_map(
        local,
        mesh=mesh,
        in_specs=(
            P(("groups", "sample"), "space", None, None),
            P(("groups", "sample"), "space", None, None),
            P("groups", None),
            P(("groups", "sample"), None),
        ),
        out_specs=(
            P(("groups", "sample"), "space", None, None),
            P(("groups", "sample"), "space", None, None),
            P(("groups", "space"), "sample"),
        ),
        check_vma=False,
    )
```

time: 55.7 us -> 49.8 us (0.89)
  waiting for transfers between devices: 15.8 us -> 10.7 us
  local copies, waits for them, and re-layouts: 3.3 us -> 0.1 us
  starting transfers between devices: 14.3 us -> 16.7 us
  other arithmetic: 2.08 us -> 1.07 us
  Pallas kernels: 19.3 us -> 20.3 us
    ppermute x9, waiting for transfers between devices: 15.8 us -> 10.7 us  [exchange(): return lax.ppermute(value, axis, [(i, i ^ mask) for i in range(count)])]
    pallas_call x0 -> x2, Pallas kernels: none -> 3.18 us  [the longest x1 1.9 us: local(): pl.pallas_call(kernel_mix, out_shape=struct((TOKENS, feat), BF16), in_spe...]
    unnamed x14 -> x8, local copies, waits for them, and re-layouts: 3.12 us -> 0.01 us
    ppermute x9, starting transfers between devices: 14.3 us -> 16.7 us  [exchange(): return lax.ppermute(value, axis, [(i, i ^ mask) for i in range(count)])]
    pallas_call x1, Pallas kernels: 13.9 us -> 11.5 us  [local(): pl.pallas_call(functools.partial(kernel_attend, sizes, n_sample, spans),...]
    select_n x1 -> x0, other arithmetic: 1.05 us -> none  [local(): jnp.where(even, rims[1], rims[0])]
  transfers between devices with their start and end apart: 9 -> 9, of which waited for: 7 -> 5; matrix products, arithmetic and copies ran while one was open for 0% -> 0% of each run, Pallas kernels for 10% -> 15%
where the time goes in v4:
time: 49.8 us; the launch traced here: 49.7 us
  Pallas kernels  20.3 us (41%)
  starting transfers between devices  16.7 us (34%)
  waiting for transfers between devices  10.7 us (21%)
  other arithmetic  1.07 us (2%)
  between operations  0.79 us (2%)
    ppermute x9, starting transfers between devices, exchange(): return lax.ppermute(value, axis, [(i, i ^ mask) for i in range(count)])  16.7 us
    pallas_call x1, Pallas kernels, local(): pl.pallas_call(functools.partial(kernel_attend, sizes, n_sample, spans),...  11.5 us
    ppermute x9, waiting for transfers between devices, exchange(): return lax.ppermute(value, axis, [(i, i ^ mask) for i in range(count)])  10.7 us
    pallas_call x1, Pallas kernels, local(): pl.pallas_call(functools.partial(kernel_own, sizes, pieces), out_shape=(s...  3.46 us
    pallas_call x1, Pallas kernels, local(): pl.pallas_call(functools.partial(kernel_final, sizes, len(steps)), out_sh...  2.12 us
    pallas_call x1, Pallas kernels, local(): pl.pallas_call(kernel_mix, out_shape=struct((TOKENS, feat), BF16), in_spe...  1.9 us
    pallas_call x1, Pallas kernels, local(): pl.pallas_call(functools.partial(kernel_pack, sizes, pieces), out_shape=[...  1.28 us
  transfers between devices with their start and end apart: 9, of which 5 were waited for; matrix products, arithmetic and copies ran while one was open for 0% of the time, Pallas kernels for 15%

profile of v4, /device:TPU:0, one launch (start us, length us, event | category | flops | bytes accessed | tf_op | source)
XLA Modules:
  0.0 49.7 jit_solution(6284144037318587645)
XLA Ops:
  0.6 1.3 %pack.1 = (bf16[48,512]{1,0:T(8,128)(2,1)S(1)}, bf16[48,512]{1,0:T(8,128)(2,1)S(1)}) custom-call(bf16[512,512]{1,0:T(8,128)(2,1)} %bitcast.4), custom_call_target="tpu_custom_call" | custom-call | flops 50331648 | bytes 1000000 | tf_op jit(solution)/shard_map/pack/pallas_call | solution.py:377
  1.9 3.1 %collective-permute-start = (bf16[48,512]{1,0:T(8,128)(2,1)S(1)}, bf16[48,512]{1,0:T(8,128)(2,1)S(1)}, u32[]{:S(2)}, u32[]{:S(2)}) collective-permute-start(bf16[48,512]{1,0:T(8,128)(2,1)S(1)} %get-tuple-element.21), channel_id=1, source_target_pairs={{0,4},{4,0},{8,12},{12,8},{1,5},{5,1},{9,13},{13,9},{2,6},{6,2},{1... | collective-permute-start | bytes 147464 | tf_op jit(solution)/shard_map/ppermute | solution.py:349
  5.0 0.0 copy-start.1
  5.0 0.0 copy-start.3
  5.0 2.5 %collective-permute-start.1 = (bf16[48,512]{1,0:T(8,128)(2,1)S(1)}, bf16[48,512]{1,0:T(8,128)(2,1)S(1)}, u32[]{:S(2)}, u32[]{:S(2)}) collective-permute-start(bf16[48,512]{1,0:T(8,128)(2,1)S(1)} %get-tuple-element.22), channel_id=1, source_target_pairs={{0,12},{4,8},{8,4},{12,0},{1,13},{5,9},{9,5},{13,1},{2,14},{6,10},... | collective-permute-start | bytes 147464 | tf_op jit(solution)/shard_map/ppermute | solution.py:349
  7.5 3.5 %own.1 = (bf16[512,512]{1,0:T(8,128)(2,1)S(1)}, bf16[640,1024]{1,0:T(8,128)(2,1)S(1)}, bf16[1024,640]{1,0:T(8,128)(2,1)S(1)}, bf16[512,640]{1,0:T(8,128)(2,1)S(1...) custom-call(s32[1,4]{1,0:T(1,128)} %margin_hbm.1, bf16[512,512]{1,0:T(8,128)(2,1)} %bitcast.5, ...), custom_call_target="tpu_custom_call" | custom-call | flops 1073741824 | bytes 7000000 | tf_op jit(solution)/shard_map/own/pallas_call | solution.py:393
  11.0 0.0 collective-permute-done.refs_0_
  11.0 0.0 collective-permute-done.1.refs_1_
  11.0 0.0 copy-done.1
  11.0 0.0 copy-done.3
  11.0 11.5 %attend.1 = (bf16[640,1024]{1,0:T(8,128)(2,1)S(1)}, bf16[1024,640]{1,0:T(8,128)(2,1)S(1)}, bf16[512,640]{1,0:T(8,128)(2,1)S(1)}, bf16[4,640,1024]{2,1,0:T(8,128)...) custom-call(bf16[512,512]{1,0:T(8,128)(2,1)S(1)} %get-tuple-element., ...), custom_call_target="tpu_custom_call", output_to_operand_aliasing={{0}: (7, {}), {1}: (8, {}), {2}: (9, {})} | custom-call | flops 8053063680 | bytes 6000000 | tf_op jit(solution)/shard_map/attend/pallas_call | solution.py:417
  22.5 0.1 collective-permute-start.2
  22.6 2.3 %collective-permute-done.2 = bf16[512,768]{1,0:T(8,128)(2,1)S(1)} collective-permute-done((bf16[512,768]{1,0:T(8,128)(2,1)S(1)}, bf16[512,768]{1,0:T(8,128)(2,1)S(1)}, u32[]{:S(2)}, u32[]{:S(2)}) %collective-permute-start.2) | collective-permute-done | bytes 786464 | tf_op jit(solution)/shard_map/ppermute | solution.py:349
  24.9 0.2 fusion
  25.1 0.8 %collective-permute-start.3 = (bf16[128,768]{1,0:T(8,128)(2,1)S(1)}, bf16[128,768]{1,0:T(8,128)(2,1)S(1)}, u32[]{:S(2)}, u32[]{:S(2)}) collective-permute-start(bf16[128,768]{1,0:T(8,128)(2,1)S(1)} %pad_maximum_fusion), channel_id=1, source_target_pairs={{0,4},{4,0},{8,12},{12,8},{1,5},{5,1},{9,13},{13,9},{2,6},{6,2},{1... | collective-permute-start | bytes 589832 | tf_op jit(solution)/shard_map/ppermute | solution.py:349
  25.9 1.9 %mix.1 = bf16[512,512]{1,0:T(8,128)(2,1)} custom-call(bf16[1024,640]{1,0:T(8,128)(2,1)S(1)} %get-tuple-element.26.kvt_ref, bf16[4,640,1024]{2,1,0:T(8,128)(2,1)S(1)} %get-tuple-element.27.pb_ref), custom_call_target="tpu_custom_call" | custom-call | flops 1342177280 | bytes 6000000 | tf_op jit(solution)/shard_map/mix/pallas_call | solution.py:477
  27.8 1.6 %collective-permute-start.5 = (bf16[320,384]{1,0:T(8,128)(2,1)S(1)}, bf16[320,384]{1,0:T(8,128)(2,1)S(1)}, u32[]{:S(2)}, u32[]{:S(2)}) collective-permute-start(bf16[320,384]{1,0:T(8,128)(2,1)S(1)} %slice.83), channel_id=1, source_target_pairs={{0,2},{1,3},{2,0},{3,1},{4,6},{5,7},{6,4},{7,5},{8,10},{9,11},{10,... | collective-permute-start | bytes 737288 | tf_op jit(solution)/shard_map/ppermute | solution.py:349
  29.4 2.8 %collective-permute-done.3 = bf16[128,768]{1,0:T(8,128)(2,1)S(1)} collective-permute-done((bf16[128,768]{1,0:T(8,128)(2,1)S(1)}, bf16[128,768]{1,0:T(8,128)(2,1)S(1)}, u32[]{:S(2)}, u32[]{:S(2)}) %collective-permute-start.3) | collective-permute-done | bytes 196640 | tf_op jit(solution)/shard_map/ppermute | solution.py:349
  32.2 2.4 %collective-permute-start.4 = (bf16[80,768]{1,0:T(8,128)(2,1)S(1)}, bf16[80,768]{1,0:T(8,128)(2,1)S(1)}, u32[]{:S(2)}, u32[]{:S(2)}) collective-permute-start(bf16[80,768]{1,0:T(8,128)(2,1)S(1)} %pad_maximum_fusion.2), channel_id=1, source_target_pairs={{0,12},{4,8},{8,4},{12,0},{1,13},{5,9},{9,5},{13,1},{2,14},{6,10},... | collective-permute-start | bytes 368648 | tf_op jit(solution)/shard_map/ppermute | solution.py:349
  34.7 0.9 %collective-permute-done.5 = bf16[320,384]{1,0:T(8,128)(2,1)S(1)} collective-permute-done((bf16[320,384]{1,0:T(8,128)(2,1)S(1)}, bf16[320,384]{1,0:T(8,128)(2,1)S(1)}, u32[]{:S(2)}, u32[]{:S(2)}) %collective-permute-start.5) | collective-permute-done | bytes 245792 | tf_op jit(solution)/shard_map/ppermute | solution.py:349
  35.6 0.1 slice_add_fusion
  35.7 1.4 %collective-permute-start.6 = (bf16[160,384]{1,0:T(8,128)(2,1)S(1)}, bf16[160,384]{1,0:T(8,128)(2,1)S(1)}, u32[]{:S(2)}, u32[]{:S(2)}) collective-permute-start(bf16[160,384]{1,0:T(8,128)(2,1)S(1)} %slice.104), channel_id=1, source_target_pairs={{0,4},{4,0},{8,12},{12,8},{1,5},{5,1},{9,13},{13,9},{2,6},{6,2},{1... | collective-permute-start | bytes 368648 | tf_op jit(solution)/shard_map/ppermute | solution.py:349
  37.1 2.0 %collective-permute-done.4 = bf16[80,768]{1,0:T(8,128)(2,1)S(1)} collective-permute-done((bf16[80,768]{1,0:T(8,128)(2,1)S(1)}, bf16[80,768]{1,0:T(8,128)(2,1)S(1)}, u32[]{:S(2)}, u32[]{:S(2)}) %collective-permute-start.4) | collective-permute-done | bytes 122912 | tf_op jit(solution)/shard_map/ppermute | solution.py:349
  39.1 1.6 %collective-permute-start.8 = (bf16[48,384]{1,0:T(8,128)(2,1)S(1)}, bf16[48,384]{1,0:T(8,128)(2,1)S(1)}, u32[]{:S(2)}, u32[]{:S(2)}) collective-permute-start(bf16[48,384]{1,0:T(8,128)(2,1)S(1)} %slice.107), channel_id=1, source_target_pairs={{0,2},{1,3},{2,0},{3,1},{4,6},{5,7},{6,4},{7,5},{8,10},{9,11},{10,... | collective-permute-start | bytes 110600 | tf_op jit(solution)/shard_map/ppermute | solution.py:349
  40.7 0.0 copy-done
  40.7 0.0 copy-done.2
  40.7 2.1 %final.1 = bf16[512,512]{1,0:T(8,128)(2,1)} custom-call(bf16[512,512]{1,0:T(8,128)(2,1)S(1)} %bitcast.6, bf16[512,1536]{1,0:T(8,128)(2,1)S(1)} %copy-done.1, s32[1,128]{1,0:T(1,128)S(1)} %copy-done.2, bf16[640,1536]{1,0:T(8,128)(2,1)S(1)} %get-tuple-element.28.grad_ref, bf16[32,768]{1,0:T(8,128)(2,1)S(1)} %slice.77.refs_0_, bf16[32,768]{1,0:T(8,128)(2,1)S(1)} %slice.81.refs_1_), custom_call_target="tpu_custom_call" | custom-call | flops 805306368 | bytes 5000000 | tf_op jit(solution)/shard_map/final/pallas_call | solution.py:489
  42.8 0.0 collective-permute-done.6
  42.9 3.3 %collective-permute-start.7 = (bf16[80,384]{1,0:T(8,128)(2,1)S(1)}, bf16[80,384]{1,0:T(8,128)(2,1)S(1)}, u32[]{:S(2)}, u32[]{:S(2)}) collective-permute-start(bf16[80,384]{1,0:T(8,128)(2,1)S(1)} %slice.106), channel_id=1, source_target_pairs={{0,12},{4,8},{8,4},{12,0},{1,13},{5,9},{9,5},{13,1},{2,14},{6,10},... | collective-permute-start | bytes 184328 | tf_op jit(solution)/shard_map/ppermute | solution.py:349
  46.2 0.0 collective-permute-done.8
  46.2 2.8 %collective-permute-done.7 = bf16[80,384]{1,0:T(8,128)(2,1)S(1)} collective-permute-done((bf16[80,384]{1,0:T(8,128)(2,1)S(1)}, bf16[80,384]{1,0:T(8,128)(2,1)S(1)}, u32[]{:S(2)}, u32[]{:S(2)}) %collective-permute-start.7) | collective-permute-done | bytes 61472 | tf_op jit(solution)/shard_map/ppermute | solution.py:349
  49.0 0.7 %pad_maximum_fusion.1 = f32[128,384]{1,0:T(8,128)} fusion(f32[48,384]{1,0:T(8,128)S(1)} %slice_add_fusion.5, f32[80,384]{1,0:T(8,128)S(1)} %slice_add_fusion.4), kind=kLoop, calls=%fused_computation.6 | loop fusion | flops 49152 | bytes 393216 | tf_op jit(solution)/shard_map/concatenate | solution.py:475
  (17 shorter events, 0.2 us)
Async XLA Ops:
  1.9 9.0 %collective-permute-start = (bf16[48,512]{1,0:T(8,128)(2,1)S(1)}, bf16[48,512]{1,0:T(8,128)(2,1)S(1)}, u32[]{:S(2)}, u32[]{:S(2)}) collective-permute-start(bf16[48,512]{1,0:T(8,128)(2,1)S(1)} %get-tuple-element.21), channel_id=1, source_target_pairs={{0,4},{4,0},{8,12},{12,8},{1,5},{5,1},{9,13},{13,9},{2,6},{6,2},{1... | collective-permute-start | bytes 147464 | tf_op jit(solution)/shard_map/ppermute | solution.py:349
  5.0 6.0 %copy-start.1 = (bf16[512,1536]{1,0:T(8,128)(2,1)S(1)}, bf16[512,1536]{1,0:T(8,128)(2,1)}, u32[]{:S(2)}) copy-start(bf16[512,1536]{1,0:T(8,128)(2,1)} %w_ref.3) | copy-start | bytes 4718596
  5.0 6.0 %copy-start.3 = (bf16[1,1,512,512]{3,2,1,0:T(8,128)(2,1)S(1)}, bf16[1,1,512,512]{3,2,1,0:T(8,128)(2,1)}, u32[]{:S(2)}) copy-start(bf16[1,1,512,512]{3,2,1,0:T(8,128)(2,1)} %param.6) | copy-start | bytes 1572868
  5.0 6.0 %collective-permute-start.1 = (bf16[48,512]{1,0:T(8,128)(2,1)S(1)}, bf16[48,512]{1,0:T(8,128)(2,1)S(1)}, u32[]{:S(2)}, u32[]{:S(2)}) collective-permute-start(bf16[48,512]{1,0:T(8,128)(2,1)S(1)} %get-tuple-element.22), channel_id=1, source_target_pairs={{0,12},{4,8},{8,4},{12,0},{1,13},{5,9},{9,5},{13,1},{2,14},{6,10},... | collective-permute-start | bytes 147464 | tf_op jit(solution)/shard_map/ppermute | solution.py:349
  22.5 2.4 %collective-permute-start.2 = (bf16[512,768]{1,0:T(8,128)(2,1)S(1)}, bf16[512,768]{1,0:T(8,128)(2,1)S(1)}, u32[]{:S(2)}, u32[]{:S(2)}) collective-permute-start(bf16[512,768]{1,0:T(8,128)(2,1)S(1)} %get-tuple-element.30), channel_id=1, source_target_pairs={{0,1},{1,0},{2,3},{3,2},{4,5},{5,4},{6,7},{7,6},{8,9},{9,8},{10,11... | collective-permute-start | bytes 2359304 | tf_op jit(solution)/shard_map/ppermute | solution.py:349
  25.1 7.0 %collective-permute-start.3 = (bf16[128,768]{1,0:T(8,128)(2,1)S(1)}, bf16[128,768]{1,0:T(8,128)(2,1)S(1)}, u32[]{:S(2)}, u32[]{:S(2)}) collective-permute-start(bf16[128,768]{1,0:T(8,128)(2,1)S(1)} %pad_maximum_fusion), channel_id=1, source_target_pairs={{0,4},{4,0},{8,12},{12,8},{1,5},{5,1},{9,13},{13,9},{2,6},{6,2},{1... | collective-permute-start | bytes 589832 | tf_op jit(solution)/shard_map/ppermute | solution.py:349
  27.8 7.8 %collective-permute-start.5 = (bf16[320,384]{1,0:T(8,128)(2,1)S(1)}, bf16[320,384]{1,0:T(8,128)(2,1)S(1)}, u32[]{:S(2)}, u32[]{:S(2)}) collective-permute-start(bf16[320,384]{1,0:T(8,128)(2,1)S(1)} %slice.83), channel_id=1, source_target_pairs={{0,2},{1,3},{2,0},{3,1},{4,6},{5,7},{6,4},{7,5},{8,10},{9,11},{10,... | collective-permute-start | bytes 737288 | tf_op jit(solution)/shard_map/ppermute | solution.py:349
  32.1 8.5 %copy-start = (bf16[1,1,512,512]{3,2,1,0:T(8,128)(2,1)S(1)}, bf16[1,1,512,512]{3,2,1,0:T(8,128)(2,1)}, u32[]{:S(2)}) copy-start(bf16[1,1,512,512]{3,2,1,0:T(8,128)(2,1)} %param.5) | copy-start | bytes 1572868
  32.1 8.5 %copy-start.2 = (s32[1,128]{1,0:T(1,128)S(1)}, s32[1,128]{1,0:T(1,128)}, u32[]{:S(2)}) copy-start(s32[1,128]{1,0:T(1,128)} %constant.2.clone.index_ref) | copy-start | bytes 1540
  32.2 6.9 %collective-permute-start.4 = (bf16[80,768]{1,0:T(8,128)(2,1)S(1)}, bf16[80,768]{1,0:T(8,128)(2,1)S(1)}, u32[]{:S(2)}, u32[]{:S(2)}) collective-permute-start(bf16[80,768]{1,0:T(8,128)(2,1)S(1)} %pad_maximum_fusion.2), channel_id=1, source_target_pairs={{0,12},{4,8},{8,4},{12,0},{1,13},{5,9},{9,5},{13,1},{2,14},{6,10},... | collective-permute-start | bytes 368648 | tf_op jit(solution)/shard_map/ppermute | solution.py:349
  35.7 7.1 %collective-permute-start.6 = (bf16[160,384]{1,0:T(8,128)(2,1)S(1)}, bf16[160,384]{1,0:T(8,128)(2,1)S(1)}, u32[]{:S(2)}, u32[]{:S(2)}) collective-permute-start(bf16[160,384]{1,0:T(8,128)(2,1)S(1)} %slice.104), channel_id=1, source_target_pairs={{0,4},{4,0},{8,12},{12,8},{1,5},{5,1},{9,13},{13,9},{2,6},{6,2},{1... | collective-permute-start | bytes 368648 | tf_op jit(solution)/shard_map/ppermute | solution.py:349
  39.1 7.1 %collective-permute-start.8 = (bf16[48,384]{1,0:T(8,128)(2,1)S(1)}, bf16[48,384]{1,0:T(8,128)(2,1)S(1)}, u32[]{:S(2)}, u32[]{:S(2)}) collective-permute-start(bf16[48,384]{1,0:T(8,128)(2,1)S(1)} %slice.107), channel_id=1, source_target_pairs={{0,2},{1,3},{2,0},{3,1},{4,6},{5,7},{6,4},{7,5},{8,10},{9,11},{10,... | collective-permute-start | bytes 110600 | tf_op jit(solution)/shard_map/ppermute | solution.py:349
  42.9 6.1 %collective-permute-start.7 = (bf16[80,384]{1,0:T(8,128)(2,1)S(1)}, bf16[80,384]{1,0:T(8,128)(2,1)S(1)}, u32[]{:S(2)}, u32[]{:S(2)}) collective-permute-start(bf16[80,384]{1,0:T(8,128)(2,1)S(1)} %slice.106), channel_id=1, source_target_pairs={{0,12},{4,8},{8,4},{12,0},{1,13},{5,9},{9,5},{13,1},{2,14},{6,10},... | collective-permute-start | bytes 184328 | tf_op jit(solution)/shard_map/ppermute | solution.py:349

commit v5 on v4

--- a/solution.py
+++ b/solution.py
@@ -16,14 +16,14 @@
 HALO = 3
 TOKENS = TH * TW
 NEG = -1e30
+TIES = (0,)
 LAST = (((1,), (1,)), ((), ()))
 F32 = jnp.float32
 BF16 = jnp.bfloat16
-PACK = 1e6
-OWN = 24
 ROWS = 64
 
 vmem = functools.partial(pl.BlockSpec, memory_space=pltpu.VMEM)
+anywhere = functools.partial(pl.BlockSpec, memory_space=pl.ANY)
 hbm = functools.partial(pl.BlockSpec, memory_space=pltpu.HBM)
 
 
@@ -73,7 +73,7 @@
 
 def row_split(feat, n_space):
     size = feat // n_space
-    return size * 5 // 8 // 16 * 16 if size >= 64 else size // 2
+    return size // 2 // 16 * 16 if size >= 64 else size // 2
 
 
 def permutation(feat, sizes, position):
@@ -120,33 +120,32 @@
 
 
 def kernel_own(
-    sizes, pieces, margin_hbm, tok_hbm, w_hbm, q_ref, kv_ref, kvt_ref, nt_ref, bias_ref, place_ref, margin_ref, tok_ref, w_ref, sems
+    sizes, pieces, margin_hbm, tok_ref, w_hbm, q_ref, kv_ref, kvt_ref, nt_ref, bias_ref, place_ref, margin_ref, w_ref, sems
 ):
     feat = w_hbm.shape[0]
-    copies = [pltpu.make_async_copy(tok_hbm, tok_ref, sems.at[0])]
+    copies = []
     for i in range(3):
         cols = pl.ds(i * feat, feat)
-        copies.append(pltpu.make_async_copy(w_hbm.at[:, cols], w_ref.at[:, cols], sems.at[1 + i]))
-    copies.append(pltpu.make_async_copy(margin_hbm, margin_ref, sems.at[4]))
+        copies.append(pltpu.make_async_copy(w_hbm.at[:, cols], w_ref.at[:, cols], sems.at[i]))
+    copies.append(pltpu.make_async_copy(margin_hbm, margin_ref, sems.at[3]))
     for copy in copies:
         copy.start()
     n_space, grid_cols, plane_rows, plane_cols = sizes
     position, member, tile_row, tile_col = own_ids(grid_cols)
     place = permutation(feat, sizes, position)
     place_ref[...] = place
-    copies[0].wait()
     standard, _ = normalise(tok_ref[...])
     normed = standard.astype(BF16)
     nt_ref[:, :TOKENS] = dot_t(place, normed).astype(BF16)
     scale = 1.0 / math.sqrt(HEAD)
-    copies[1].wait()
+    copies[0].wait()
     q_ref[...] = (dot(normed, w_ref[:, :feat]).astype(BF16).astype(F32) * scale).astype(BF16)
     for i in range(2):
-        copies[2 + i].wait()
+        copies[1 + i].wait()
         part = dot(normed, w_ref[:, (i + 1) * feat : (i + 2) * feat]).astype(BF16)
         kv_ref[:TOKENS, i * feat : (i + 1) * feat] = part
         kvt_ref[i * feat : (i + 1) * feat, :TOKENS] = part.T
-    copies[4].wait()
+    copies[3].wait()
     key = lax.broadcasted_iota(jnp.int32, (TOKENS, 128), 0)
     query = lax.broadcasted_iota(jnp.int32, (TOKENS, 128), 1)
     row = tile_row * TH + key // TW
@@ -175,8 +174,7 @@
     n_space, grid_cols, plane_rows, plane_cols = sizes
     count = len(spans)
     toks, refs = refs[:count], refs[count + 3 :]
-    kv_ref, kvt_ref, nt_ref, pb_ref, grad_ref, keep_ref, send_ref = refs[:7]
-    rim_refs, refs = refs[7 : 7 + count], refs[7 + count :]
+    kv_ref, kvt_ref, nt_ref, pb_ref, grad_ref, keep_ref, send_ref, *refs = refs
     s_s, g_s, ds_s, cm_s, qm_s, dqt_s = refs
     position, member, _, _ = own_ids(grid_cols)
     feat = w_ref.shape[0]
@@ -262,6 +260,12 @@
             cols = pl.ds(pl.multiple_of((member ^ other) * block, 128), block)
             value = dot(nt_ref[...], grad_ref[:, cols])
             target[:, j * block : (j + 1) * block] = value.astype(target.dtype)
+
+
+def kernel_mix(sizes, spans, kvt_ref, pb_ref, grad_ref, w_ref, att_ref, *refs):
+    rim_refs, att_s = refs[:-1], refs[-1]
+    feat = att_ref.shape[1]
+    even = (lax.axis_index("space") & 1) == 0
     rim = dot_t(grad_ref[TOKENS:, feat:], w_ref[:, feat:])
     if paired(sizes):
         rows = rim_refs[0].shape[0]
@@ -274,10 +278,6 @@
     else:
         for (lo, hi), ref in zip(spans, rim_refs):
             ref[...] = rim[lo:hi, :].astype(BF16)
-
-
-def kernel_mix(kvt_ref, pb_ref, att_ref, att_s):
-    feat = att_ref.shape[1]
     for head in range(HEADS):
         row = head * HEAD
         out = slice((head % 2) * TOKENS, (head % 2 + 1) * TOKENS)
@@ -286,7 +286,7 @@
 
 
 def kernel_final(sizes, count, tok_ref, w_ref, index_ref, grad_ref, *refs):
-    arrived, out_ref = refs[:count], refs[count]
+    arrived, out_ref = refs[:count], refs[-1]
     feat = w_ref.shape[0]
     total = dot_t(grad_ref[:TOKENS, :], w_ref[...])
     padded = index_ref.shape[1]
@@ -374,14 +374,14 @@
     ends = np.cumsum([0, *counts])
     spans = [(int(a), int(b)) for a, b in zip(ends[:-1], ends[1:])]
 
-    rims = pl.pallas_call(
+    *rims, tok_near = pl.pallas_call(
         functools.partial(kernel_pack, sizes, pieces),
-        out_shape=[struct((n, feat), BF16) for n in counts],
+        out_shape=[*[struct((n, feat), BF16) for n in counts], struct(tok.shape, BF16)],
         in_specs=[hbm()],
-        out_specs=[vmem()] * len(counts),
-        scratch_shapes=[pltpu.VMEM(tok.shape, BF16), pltpu.SemaphoreType.DMA],
+        out_specs=[vmem()] * (len(counts) + 1),
+        scratch_shapes=[pltpu.SemaphoreType.DMA],
         compiler_params=params(16),
-        cost_estimate=cost(2 * halo * TOKENS * feat, PACK),
+        cost_estimate=cost(2 * halo * TOKENS * feat, 1e6),
         name="pack",
     )(pinned(tok))
     if paired(sizes):
@@ -400,18 +400,17 @@
             struct((keys, TOKENS), F32),
             struct((feat, feat), BF16),
         ),
-        in_specs=[hbm()] * 3,
+        in_specs=[hbm(), vmem(), hbm()],
         out_specs=[vmem()] * 6,
         scratch_shapes=[
             pltpu.SMEM(margins.shape, jnp.int32),
-            pltpu.VMEM(tok.shape, BF16),
             pltpu.VMEM(weight.shape, BF16),
-            pltpu.SemaphoreType.DMA((5,)),
+            pltpu.SemaphoreType.DMA((4,)),
         ],
-        compiler_params=params(OWN),
+        compiler_params=params(),
         cost_estimate=cost(8 * TOKENS * feat * feat, 7e6),
         name="own",
-    )(*(pinned(a) for a in (margins, tok, weight)))
+    )(pinned(margins), tok_near, pinned(weight))
 
     rim_shape = (2 * counts[0] // 3, 3 * feat // 2)
     outs = pl.pallas_call(
@@ -422,10 +421,9 @@
             struct((keys, 3 * feat), BF16),
             struct((feat, 3 * feat // 2), F32),
             struct((feat, 3 * feat // 2), BF16),
-            *[struct(rim_shape if paired(sizes) else (n, feat), BF16) for n in counts],
         ),
         in_specs=[vmem()] * (5 + len(counts) + 3),
-        out_specs=[vmem()] * (7 + len(counts)),
+        out_specs=[vmem()] * 7,
         input_output_aliases={5 + len(counts) + i: i for i in range(3)},
         scratch_shapes=[
             pltpu.VMEM((2, keys, TOKENS), F32),
@@ -439,9 +437,21 @@
         cost_estimate=cost(48 * TOKENS * keys * feat, 6e6, TOKENS * keys * HEADS),
         name="attend",
     )(q, cot, weight, bias, place, *halo_tokens, kv, kvt, nt)
-    kvt, prob = outs[1], outs[3]
-    grads, keep, send = outs[4:7]
-    rims = list(outs[7:])
+    kvt, prob, grads, keep, send = outs[1], *outs[3:]
+
+    attention, *rims = pl.pallas_call(
+        functools.partial(kernel_mix, sizes, spans),
+        out_shape=(
+            struct((TOKENS, feat), BF16),
+            *[struct(rim_shape if paired(sizes) else (n, feat), BF16) for n in counts],
+        ),
+        in_specs=[vmem()] * 4,
+        out_specs=[vmem()] * (1 + len(counts)),
+        scratch_shapes=[pltpu.VMEM((feat, TOKENS), F32)],
+        compiler_params=params(12),
+        cost_estimate=cost(8 * TOKENS * keys * feat, 6e6),
+        name="mix",
+    )(kvt, prob, grads, weight)
 
     total = keep + exchange(send, "sample", 1).astype(F32)
     half = row_split(feat, n_space) * n_space
@@ -451,50 +461,43 @@
     if not paired(sizes):
         arrived = [shift(rim, "space", r * grid_cols + c) for (r, c), rim in zip(steps, rims)]
 
-    def by_cols(value):
-        for mask in col_masks:
-            n = value.shape[1] // 2
-            got = exchange(value[:, n:].astype(BF16), "sample", mask)
-            value = value[:, :n] + got.astype(F32)
-        return value
-
-    def by_rows(value, riders):
-        for i, mask in enumerate(masks):
-            n = value.shape[0] // 2
-            out = value[n:].astype(BF16)
-            if riders:
-                out = jnp.concatenate([out, riders[i]], axis=0)
-            got = exchange(out, "space", mask)
-            if riders:
-                arrived.append(got[n:])
-            value = value[:n] + got[:n].astype(F32)
-        return value
-
-    upper = by_rows(by_cols(first), [])
-    lower = by_cols(by_rows(second, rims if paired(sizes) else []))
+    def cut(value, axis):
+        dim = 0 if axis == "space" else 1
+        return jnp.split(value, 2, axis=dim)
+
+    upper, lower = first, second
+    over_rows = [("space", mask) for mask in masks]
+    over_cols = [("sample", mask) for mask in col_masks]
+    after, step = [], 0
+    for one, two in zip(over_cols + over_rows, over_rows + over_cols):
+        upper, out = cut(upper, one[0])
+        got = exchange(out.astype(BF16), *one)
+        lower, out = cut(lower, two[0])
+        out = out.astype(BF16)
+        ride = paired(sizes) and two[0] == "space"
+        if ride:
+            out = jnp.concatenate([out, rims[step]], axis=0)
+        other = exchange(out, *two)
+        if step in TIES:
+            got, other = lax.optimization_barrier((got, other))
+        if ride:
+            arrived.append(other[lower.shape[0] :])
+        if step == len(over_cols):
+            after.append(got)
+        upper = upper + got.astype(F32)
+        lower = lower + other[: lower.shape[0]].astype(F32)
+        step += 1
     weight_grad = jnp.concatenate([upper, lower], axis=0)
-
-    attention = pl.pallas_call(
-        kernel_mix,
-        out_shape=struct((TOKENS, feat), BF16),
-        in_specs=[vmem()] * 2,
-        out_specs=vmem(),
-        scratch_shapes=[pltpu.VMEM((feat, TOKENS), F32)],
-        compiler_params=params(8),
-        cost_estimate=cost(8 * TOKENS * keys * feat, 6e6),
-        name="mix",
-    )(kvt, prob)
-    arrived += [jnp.zeros_like(rim) for rim in rims[len(arrived) :]]
 
     token_grad = pl.pallas_call(
         functools.partial(kernel_final, sizes, len(steps)),
         out_shape=struct((TOKENS, feat), BF16),
-        in_specs=[vmem()] * (4 + len(steps)),
+        in_specs=[vmem()] * (4 + len(steps)) + [anywhere()] * len(after),
         out_specs=vmem(),
         compiler_params=params(16),
         cost_estimate=cost(6 * TOKENS * feat * feat, 5e6),
         name="final",
-    )(tok, weight, jnp.asarray(rim_index), grads, *arrived)
+    )(tok_near, weight, jnp.asarray(rim_index), grads, *arrived, *after)
     return (attention[None, None], token_grad[None, None], weight_grad)
 
 

time: 49.8 us -> 47.6 us (0.956)
  starting transfers between devices: 16.7 us -> 14.9 us
    ppermute x9, starting transfers between devices: 16.7 us -> 14.9 us  [exchange(): return lax.ppermute(value, axis, [(i, i ^ mask) for i in range(count)])]
  transfers between devices with their start and end apart: 9 -> 9, of which waited for: 5 -> 6; matrix products, arithmetic and copies ran while one was open for 0% -> 0% of each run, Pallas kernels for 15% -> 16%
where the time goes in v5:
time: 47.6 us; the launch traced here: 47.4 us
  Pallas kernels  20 us (42%)
  starting transfers between devices  14.9 us (31%)
  waiting for transfers between devices  10.6 us (22%)
  other arithmetic  1.09 us (2%)
  between operations  0.76 us (2%)
    ppermute x9, starting transfers between devices, exchange(): return lax.ppermute(value, axis, [(i, i ^ mask) for i in range(count)])  14.9 us
    pallas_call x1, Pallas kernels, local(): pl.pallas_call(functools.partial(kernel_attend, sizes, n_sample, spans),...  11.2 us
    ppermute x9, waiting for transfers between devices, exchange(): return lax.ppermute(value, axis, [(i, i ^ mask) for i in range(count)])  10.6 us
    pallas_call x1, Pallas kernels, local(): pl.pallas_call(functools.partial(kernel_own, sizes, pieces), out_shape=(s...  3.13 us
    pallas_call x1, Pallas kernels, local(): pl.pallas_call(functools.partial(kernel_mix, sizes, spans), out_shape=(st...  2.23 us
    pallas_call x1, Pallas kernels, local(): pl.pallas_call(functools.partial(kernel_final, sizes, len(steps)), out_sh...  2.12 us
    pallas_call x1, Pallas kernels, local(): pl.pallas_call(functools.partial(kernel_pack, sizes, pieces), out_shape=[...  1.27 us
  transfers between devices with their start and end apart: 9, of which 6 were waited for; matrix products, arithmetic and copies ran while one was open for 0% of the time, Pallas kernels for 16%

profile of v5, /device:TPU:0, one launch (start us, length us, event | category | flops | bytes accessed | tf_op | source)
XLA Modules:
  0.0 47.4 jit_solution(9934794643018237480)
XLA Ops:
  0.6 1.3 %pack.1 = (bf16[48,512]{1,0:T(8,128)(2,1)S(1)}, bf16[48,512]{1,0:T(8,128)(2,1)S(1)}, bf16[512,512]{1,0:T(8,128)(2,1)S(1)}) custom-call(bf16[512,512]{1,0:T(8,128)(2,1)} %bitcast.6), custom_call_target="tpu_custom_call" | custom-call | flops 50331648 | bytes 1000000 | tf_op jit(solution)/shard_map/pack/pallas_call | solution.py:377
  1.9 3.1 %collective-permute-start = (bf16[48,512]{1,0:T(8,128)(2,1)S(1)}, bf16[48,512]{1,0:T(8,128)(2,1)S(1)}, u32[]{:S(2)}, u32[]{:S(2)}) collective-permute-start(bf16[48,512]{1,0:T(8,128)(2,1)S(1)} %get-tuple-element.26), channel_id=1, source_target_pairs={{0,4},{4,0},{8,12},{12,8},{1,5},{5,1},{9,13},{13,9},{2,6},{6,2},{1... | collective-permute-start | bytes 147464 | tf_op jit(solution)/shard_map/ppermute | solution.py:349
  5.0 2.5 %collective-permute-start.1 = (bf16[48,512]{1,0:T(8,128)(2,1)S(1)}, bf16[48,512]{1,0:T(8,128)(2,1)S(1)}, u32[]{:S(2)}, u32[]{:S(2)}) collective-permute-start(bf16[48,512]{1,0:T(8,128)(2,1)S(1)} %get-tuple-element.27), channel_id=1, source_target_pairs={{0,12},{4,8},{8,4},{12,0},{1,13},{5,9},{9,5},{13,1},{2,14},{6,10},... | collective-permute-start | bytes 147464 | tf_op jit(solution)/shard_map/ppermute | solution.py:349
  7.5 0.0 copy-start
  7.5 0.0 copy-start.2
  7.5 3.1 %own.1 = (bf16[512,512]{1,0:T(8,128)(2,1)S(1)}, bf16[640,1024]{1,0:T(8,128)(2,1)S(1)}, bf16[1024,640]{1,0:T(8,128)(2,1)S(1)}, bf16[512,640]{1,0:T(8,128)(2,1)S(1...) custom-call(s32[1,4]{1,0:T(1,128)} %margin_hbm.1, bf16[512,512]{1,0:T(8,128)(2,1)S(1)} %get-tuple-element.22.tok_ref, ...), custom_call_target="tpu_custom_call" | custom-call | flops 1073741824 | bytes 7000000 | tf_op jit(solution)/shard_map/own/pallas_call | solution.py:393
  10.6 0.0 collective-permute-done.refs_0_
  10.6 0.3 collective-permute-done.1.refs_1_
  10.9 0.0 copy-done
  10.9 0.0 copy-done.2
  10.9 11.2 %attend.1 = (bf16[640,1024]{1,0:T(8,128)(2,1)S(1)}, bf16[1024,640]{1,0:T(8,128)(2,1)S(1)}, bf16[512,640]{1,0:T(8,128)(2,1)S(1)}, bf16[4,640,1024]{2,1,0:T(8,128)...) custom-call(bf16[512,512]{1,0:T(8,128)(2,1)S(1)} %get-tuple-element., ...), custom_call_target="tpu_custom_call", output_to_operand_aliasing={{0}: (7, {}), {1}: (8, {}), {2}: (9, {})} | custom-call | flops 8053063680 | bytes 6000000 | tf_op jit(solution)/shard_map/attend/pallas_call | solution.py:416
  22.1 0.1 collective-permute-start.2
  22.2 2.2 %mix.1 = (bf16[512,512]{1,0:T(8,128)(2,1)}, bf16[32,768]{1,0:T(8,128)(2,1)S(1)}, bf16[32,768]{1,0:T(8,128)(2,1)S(1)}) custom-call(bf16[1024,640]{1,0:T(8,128)(2,1)S(1)} %get-tuple-element.31.kvt_ref, bf16[4,640,1024]{2,1,0:T(8,128)(2,1)S(1)} %get-tuple-element.32.pb_ref, bf16[640,1536]{1,0:T(8,128)(2,1)S(1)} %get-tuple-element.33.grad_ref, ...), custom_call_target="tpu_custom_call" | custom-call | flops 1342177280 | bytes 6000000 | tf_op jit(solution)/shard_map/mix/pallas_call | solution.py:442
  24.5 0.0 collective-permute-done.2
  24.5 0.2 fusion
  24.8 0.5 %collective-permute-start.4 = (bf16[160,768]{1,0:T(8,128)(2,1)S(1)}, bf16[160,768]{1,0:T(8,128)(2,1)S(1)}, u32[]{:S(2)}, u32[]{:S(2)}) collective-permute-start(bf16[160,768]{1,0:T(8,128)(2,1)S(1)} %pad_maximum_fusion), channel_id=1, source_target_pairs={{0,4},{4,0},{8,12},{12,8},{1,5},{5,1},{9,13},{13,9},{2,6},{6,2},{1... | collective-permute-start | bytes 737288 | tf_op jit(solution)/shard_map/ppermute | solution.py:349
  25.3 1.6 %collective-permute-start.3 = (bf16[256,384]{1,0:T(8,128)(2,1)S(1)}, bf16[256,384]{1,0:T(8,128)(2,1)S(1)}, u32[]{:S(2)}, u32[]{:S(2)}) collective-permute-start(bf16[256,384]{1,0:T(8,128)(2,1)S(1)} %split.54), channel_id=1, source_target_pairs={{0,2},{1,3},{2,0},{3,1},{4,6},{5,7},{6,4},{7,5},{8,10},{9,11},{10,... | collective-permute-start | bytes 589832 | tf_op jit(solution)/shard_map/ppermute | solution.py:349
  26.9 5.5 %collective-permute-done.3 = bf16[256,384]{1,0:T(8,128)(2,1)S(1)} collective-permute-done((bf16[256,384]{1,0:T(8,128)(2,1)S(1)}, bf16[256,384]{1,0:T(8,128)(2,1)S(1)}, u32[]{:S(2)}, u32[]{:S(2)}) %collective-permute-start.3) | collective-permute-done | bytes 196640 | tf_op jit(solution)/shard_map/ppermute | solution.py:349
  32.3 0.8 %collective-permute-done.4 = bf16[160,768]{1,0:T(8,128)(2,1)S(1)} collective-permute-done((bf16[160,768]{1,0:T(8,128)(2,1)S(1)}, bf16[160,768]{1,0:T(8,128)(2,1)S(1)}, u32[]{:S(2)}, u32[]{:S(2)}) %collective-permute-start.4) | collective-permute-done | bytes 245792 | tf_op jit(solution)/shard_map/ppermute | solution.py:349
  33.2 0.0 copy-start.1
  33.3 0.9 %collective-permute-start.6 = (bf16[128,384]{1,0:T(8,128)(2,1)S(1)}, bf16[128,384]{1,0:T(8,128)(2,1)S(1)}, u32[]{:S(2)}, u32[]{:S(2)}) collective-permute-start(bf16[128,384]{1,0:T(8,128)(2,1)S(1)} %split.76), channel_id=1, source_target_pairs={{0,4},{4,0},{8,12},{12,8},{1,5},{5,1},{9,13},{13,9},{2,6},{6,2},{1... | collective-permute-start | bytes 294920 | tf_op jit(solution)/shard_map/ppermute | solution.py:349
  34.2 2.5 %collective-permute-start.5 = (bf16[96,768]{1,0:T(8,128)(2,1)S(1)}, bf16[96,768]{1,0:T(8,128)(2,1)S(1)}, u32[]{:S(2)}, u32[]{:S(2)}) collective-permute-start(bf16[96,768]{1,0:T(8,128)(2,1)S(1)} %pad_maximum_fusion.2), channel_id=1, source_target_pairs={{0,12},{4,8},{8,4},{12,0},{1,13},{5,9},{9,5},{13,1},{2,14},{6,10},... | collective-permute-start | bytes 442376 | tf_op jit(solution)/shard_map/ppermute | solution.py:349
  36.7 1.9 %collective-permute-done.6.refs_2_ = bf16[128,384]{1,0:T(8,128)(2,1)S(1)} collective-permute-done((bf16[128,384]{1,0:T(8,128)(2,1)S(1)}, bf16[128,384]{1,0:T(8,128)(2,1)S(1)}, u32[]{:S(2)}, u32[]{:S(2)}) %collective-permute-start.6) | collective-permute-done | bytes 98336 | tf_op jit(solution)/shard_map/ppermute | solution.py:349
  38.7 2.2 %collective-permute-start.7 = (bf16[64,384]{1,0:T(8,128)(2,1)S(1)}, bf16[64,384]{1,0:T(8,128)(2,1)S(1)}, u32[]{:S(2)}, u32[]{:S(2)}) collective-permute-start(bf16[64,384]{1,0:T(8,128)(2,1)S(1)} %split.79), channel_id=1, source_target_pairs={{0,12},{4,8},{8,4},{12,0},{1,13},{5,9},{9,5},{13,1},{2,14},{6,10},... | collective-permute-start | bytes 147464 | tf_op jit(solution)/shard_map/ppermute | solution.py:349
  40.9 1.6 %collective-permute-done.5 = bf16[96,768]{1,0:T(8,128)(2,1)S(1)} collective-permute-done((bf16[96,768]{1,0:T(8,128)(2,1)S(1)}, bf16[96,768]{1,0:T(8,128)(2,1)S(1)}, u32[]{:S(2)}, u32[]{:S(2)}) %collective-permute-start.5) | collective-permute-done | bytes 147488 | tf_op jit(solution)/shard_map/ppermute | solution.py:349
  42.5 1.6 %collective-permute-start.8 = (bf16[64,384]{1,0:T(8,128)(2,1)S(1)}, bf16[64,384]{1,0:T(8,128)(2,1)S(1)}, u32[]{:S(2)}, u32[]{:S(2)}) collective-permute-start(bf16[64,384]{1,0:T(8,128)(2,1)S(1)} %split.78), channel_id=1, source_target_pairs={{0,2},{1,3},{2,0},{3,1},{4,6},{5,7},{6,4},{7,5},{8,10},{9,11},{10,... | collective-permute-start | bytes 147464 | tf_op jit(solution)/shard_map/ppermute | solution.py:349
  44.1 0.0 copy-done.1
  44.1 2.1 %final.1 = bf16[512,512]{1,0:T(8,128)(2,1)} custom-call(bf16[512,512]{1,0:T(8,128)(2,1)S(1)} %get-tuple-element.22.tok_ref, bf16[512,1536]{1,0:T(8,128)(2,1)S(1)} %copy-done, s32[1,128]{1,0:T(1,128)S(1)} %copy-done.1, bf16[640,1536]{1,0:T(8,128)(2,1)S(1)} %get-tuple-element.33.grad_ref, bf16[32,768]{1,0:T(8,128)(2,1)S(1)} %slice.18.refs_0_, ...), custom_call_target="tpu_custom_call" | custom-call | flops 805306368 | bytes 5000000 | tf_op jit(solution)/shard_map/final/pallas_call | solution.py:492
  46.2 0.0 collective-permute-done.7
  46.2 0.5 collective-permute-done.8
  46.7 0.7 %pad_maximum_fusion.1 = f32[128,384]{1,0:T(8,128)} fusion(f32[64,384]{1,0:T(8,128)S(1)} %slice_add_fusion.4, f32[64,384]{1,0:T(8,128)S(1)} %slice_add_fusion.5), kind=kLoop, calls=%fused_computation.8 | loop fusion | flops 49152 | bytes 393216 | tf_op jit(solution)/shard_map/concatenate | solution.py:490
  (16 shorter events, 0.3 us)
Async XLA Ops:
  1.9 8.7 %collective-permute-start = (bf16[48,512]{1,0:T(8,128)(2,1)S(1)}, bf16[48,512]{1,0:T(8,128)(2,1)S(1)}, u32[]{:S(2)}, u32[]{:S(2)}) collective-permute-start(bf16[48,512]{1,0:T(8,128)(2,1)S(1)} %get-tuple-element.26), channel_id=1, source_target_pairs={{0,4},{4,0},{8,12},{12,8},{1,5},{5,1},{9,13},{13,9},{2,6},{6,2},{1... | collective-permute-start | bytes 147464 | tf_op jit(solution)/shard_map/ppermute | solution.py:349
  5.0 5.9 %collective-permute-start.1 = (bf16[48,512]{1,0:T(8,128)(2,1)S(1)}, bf16[48,512]{1,0:T(8,128)(2,1)S(1)}, u32[]{:S(2)}, u32[]{:S(2)}) collective-permute-start(bf16[48,512]{1,0:T(8,128)(2,1)S(1)} %get-tuple-element.27), channel_id=1, source_target_pairs={{0,12},{4,8},{8,4},{12,0},{1,13},{5,9},{9,5},{13,1},{2,14},{6,10},... | collective-permute-start | bytes 147464 | tf_op jit(solution)/shard_map/ppermute | solution.py:349
  7.5 3.4 %copy-start = (bf16[512,1536]{1,0:T(8,128)(2,1)S(1)}, bf16[512,1536]{1,0:T(8,128)(2,1)}, u32[]{:S(2)}) copy-start(bf16[512,1536]{1,0:T(8,128)(2,1)} %w_ref.5) | copy-start | bytes 4718596
  7.5 3.4 %copy-start.2 = (bf16[1,1,512,512]{3,2,1,0:T(8,128)(2,1)S(1)}, bf16[1,1,512,512]{3,2,1,0:T(8,128)(2,1)}, u32[]{:S(2)}) copy-start(bf16[1,1,512,512]{3,2,1,0:T(8,128)(2,1)} %param.6) | copy-start | bytes 1572868
  22.1 2.4 %collective-permute-start.2 = (bf16[512,768]{1,0:T(8,128)(2,1)S(1)}, bf16[512,768]{1,0:T(8,128)(2,1)S(1)}, u32[]{:S(2)}, u32[]{:S(2)}) collective-permute-start(bf16[512,768]{1,0:T(8,128)(2,1)S(1)} %get-tuple-element.36), channel_id=1, source_target_pairs={{0,1},{1,0},{2,3},{3,2},{4,5},{5,4},{6,7},{7,6},{8,9},{9,8},{10,11... | collective-permute-start | bytes 2359304 | tf_op jit(solution)/shard_map/ppermute | solution.py:349
  24.8 8.4 %collective-permute-start.4 = (bf16[160,768]{1,0:T(8,128)(2,1)S(1)}, bf16[160,768]{1,0:T(8,128)(2,1)S(1)}, u32[]{:S(2)}, u32[]{:S(2)}) collective-permute-start(bf16[160,768]{1,0:T(8,128)(2,1)S(1)} %pad_maximum_fusion), channel_id=1, source_target_pairs={{0,4},{4,0},{8,12},{12,8},{1,5},{5,1},{9,13},{13,9},{2,6},{6,2},{1... | collective-permute-start | bytes 737288 | tf_op jit(solution)/shard_map/ppermute | solution.py:349
  25.3 7.0 %collective-permute-start.3 = (bf16[256,384]{1,0:T(8,128)(2,1)S(1)}, bf16[256,384]{1,0:T(8,128)(2,1)S(1)}, u32[]{:S(2)}, u32[]{:S(2)}) collective-permute-start(bf16[256,384]{1,0:T(8,128)(2,1)S(1)} %split.54), channel_id=1, source_target_pairs={{0,2},{1,3},{2,0},{3,1},{4,6},{5,7},{6,4},{7,5},{8,10},{9,11},{10,... | collective-permute-start | bytes 589832 | tf_op jit(solution)/shard_map/ppermute | solution.py:349
  33.2 10.9 %copy-start.1 = (s32[1,128]{1,0:T(1,128)S(1)}, s32[1,128]{1,0:T(1,128)}, u32[]{:S(2)}) copy-start(s32[1,128]{1,0:T(1,128)} %constant.2.clone.index_ref) | copy-start | bytes 1540
  33.3 5.3 %collective-permute-start.6 = (bf16[128,384]{1,0:T(8,128)(2,1)S(1)}, bf16[128,384]{1,0:T(8,128)(2,1)S(1)}, u32[]{:S(2)}, u32[]{:S(2)}) collective-permute-start(bf16[128,384]{1,0:T(8,128)(2,1)S(1)} %split.76), channel_id=1, source_target_pairs={{0,4},{4,0},{8,12},{12,8},{1,5},{5,1},{9,13},{13,9},{2,6},{6,2},{1... | collective-permute-start | bytes 294920 | tf_op jit(solution)/shard_map/ppermute | solution.py:349
  34.2 8.3 %collective-permute-start.5 = (bf16[96,768]{1,0:T(8,128)(2,1)S(1)}, bf16[96,768]{1,0:T(8,128)(2,1)S(1)}, u32[]{:S(2)}, u32[]{:S(2)}) collective-permute-start(bf16[96,768]{1,0:T(8,128)(2,1)S(1)} %pad_maximum_fusion.2), channel_id=1, source_target_pairs={{0,12},{4,8},{8,4},{12,0},{1,13},{5,9},{9,5},{13,1},{2,14},{6,10},... | collective-permute-start | bytes 442376 | tf_op jit(solution)/shard_map/ppermute | solution.py:349
  38.7 7.5 %collective-permute-start.7 = (bf16[64,384]{1,0:T(8,128)(2,1)S(1)}, bf16[64,384]{1,0:T(8,128)(2,1)S(1)}, u32[]{:S(2)}, u32[]{:S(2)}) collective-permute-start(bf16[64,384]{1,0:T(8,128)(2,1)S(1)} %split.79), channel_id=1, source_target_pairs={{0,12},{4,8},{8,4},{12,0},{1,13},{5,9},{9,5},{13,1},{2,14},{6,10},... | collective-permute-start | bytes 147464 | tf_op jit(solution)/shard_map/ppermute | solution.py:349
  42.5 4.2 %collective-permute-start.8 = (bf16[64,384]{1,0:T(8,128)(2,1)S(1)}, bf16[64,384]{1,0:T(8,128)(2,1)S(1)}, u32[]{:S(2)}, u32[]{:S(2)}) collective-permute-start(bf16[64,384]{1,0:T(8,128)(2,1)S(1)} %split.78), channel_id=1, source_target_pairs={{0,2},{1,3},{2,0},{3,1},{4,6},{5,7},{6,4},{7,5},{8,10},{9,11},{10,... | collective-permute-start | bytes 147464 | tf_op jit(solution)/shard_map/ppermute | solution.py:349

commit v6 on v5

--- a/solution.py
+++ b/solution.py
@@ -120,7 +120,7 @@
 
 
 def kernel_own(
-    sizes, pieces, margin_hbm, tok_ref, w_hbm, q_ref, kv_ref, kvt_ref, nt_ref, bias_ref, place_ref, margin_ref, w_ref, sems
+    sizes, pieces, margin_hbm, tok_ref, w_hbm, q_ref, kv_ref, kvt_ref, nt_ref, bias_ref, place_ref, w_ref, margin_ref, sems
 ):
     feat = w_hbm.shape[0]
     copies = []
@@ -285,10 +285,16 @@
     att_ref[...] = att_s[...].T.astype(BF16)
 
 
-def kernel_final(sizes, count, tok_ref, w_ref, index_ref, grad_ref, *refs):
+def kernel_own_grad(tok_ref, w_ref, grad_ref, total_ref, standard_ref, inv_ref):
+    standard, inv = normalise(tok_ref[...])
+    standard_ref[...] = standard
+    inv_ref[...] = jnp.broadcast_to(inv, inv_ref.shape)
+    total_ref[...] = dot_t(grad_ref[:TOKENS, :], w_ref[...])
+
+
+def kernel_final(sizes, count, total_ref, standard_ref, inv_ref, index_ref, *refs):
     arrived, out_ref = refs[:count], refs[-1]
-    feat = w_ref.shape[0]
-    total = dot_t(grad_ref[:TOKENS, :], w_ref[...])
+    feat = total_ref.shape[1]
     padded = index_ref.shape[1]
     parts = [r[...].astype(F32) for r in arrived]
     if paired(sizes):
@@ -303,11 +309,11 @@
     rim = jnp.concatenate(parts, axis=0).astype(BF16)
     token = lax.broadcasted_iota(jnp.int32, (TOKENS, padded), 0)
     place = jnp.where(token == index_ref[...], 1.0, 0.0).astype(BF16)
-    total = total + dot(place, rim)
-    standard, inv = normalise(tok_ref[...])
+    total = total_ref[...] + dot(place, rim)
+    standard = standard_ref[...]
     mean = jnp.mean(total, axis=-1, keepdims=True)
     cross = jnp.mean(total * standard, axis=-1, keepdims=True)
-    out_ref[...] = ((total - mean - standard * cross) * inv).astype(BF16)
+    out_ref[...] = ((total - mean - standard * cross) * inv_ref[:, 0:1]).astype(BF16)
 
 
 def shift(value, axis, steps):
@@ -390,7 +396,7 @@
     else:
         halo_tokens = [shift(v, "space", -(r * grid_cols + c)) for v, (r, c) in zip(rims, steps)]
 
-    q, kv, kvt, nt, bias, place = pl.pallas_call(
+    q, kv, kvt, nt, bias, place, weight = pl.pallas_call(
         functools.partial(kernel_own, sizes, pieces),
         out_shape=(
             struct((TOKENS, feat), BF16),
@@ -399,12 +405,12 @@
             struct((feat, keys), BF16),
             struct((keys, TOKENS), F32),
             struct((feat, feat), BF16),
+            struct(weight.shape, BF16),
         ),
         in_specs=[hbm(), vmem(), hbm()],
-        out_specs=[vmem()] * 6,
+        out_specs=[vmem()] * 7,
         scratch_shapes=[
             pltpu.SMEM(margins.shape, jnp.int32),
-            pltpu.VMEM(weight.shape, BF16),
             pltpu.SemaphoreType.DMA((4,)),
         ],
         compiler_params=params(),
@@ -453,6 +459,16 @@
         name="mix",
     )(kvt, prob, grads, weight)
 
+    parts = pl.pallas_call(
+        kernel_own_grad,
+        out_shape=(struct((TOKENS, feat), F32), struct((TOKENS, feat), F32), struct((TOKENS, 128), F32)),
+        in_specs=[vmem()] * 3,
+        out_specs=[vmem()] * 3,
+        compiler_params=params(12),
+        cost_estimate=cost(6 * TOKENS * feat * feat, 5e6),
+        name="own_grad",
+    )(tok_near, weight, grads)
+
     total = keep + exchange(send, "sample", 1).astype(F32)
     half = row_split(feat, n_space) * n_space
     first, second = total[:half], total[half:]
@@ -479,7 +495,7 @@
             out = jnp.concatenate([out, rims[step]], axis=0)
         other = exchange(out, *two)
         if step in TIES:
-            got, other = lax.optimization_barrier((got, other))
+            got, other, *parts = lax.optimization_barrier((got, other, *parts))
         if ride:
             arrived.append(other[lower.shape[0] :])
         if step == len(over_cols):
@@ -497,7 +513,7 @@
         compiler_params=params(16),
         cost_estimate=cost(6 * TOKENS * feat * feat, 5e6),
         name="final",
-    )(tok_near, weight, jnp.asarray(rim_index), grads, *arrived, *after)
+    )(*parts, jnp.asarray(rim_index), *arrived, *after)
     return (attention[None, None], token_grad[None, None], weight_grad)
 
 

time: 47.6 us -> 47.6 us (level)
    pallas_call x0 -> x1, Pallas kernels: none -> 1.06 us  [local(): pl.pallas_call(kernel_own_grad, out_shape=(struct((TOKENS, feat), F32), s...]
    pallas_call x1, Pallas kernels: 2.12 us -> 1.28 us  [local(): pl.pallas_call(functools.partial(kernel_final, sizes, len(steps)), out_sh...]
where the time goes in v6:
time: 47.6 us; the launch traced here: 47.4 us
  Pallas kernels  20 us (42%)
  starting transfers between devices  14.6 us (31%)
  waiting for transfers between devices  10.9 us (23%)
  other arithmetic  1.07 us (2%)
  between operations  0.78 us (2%)
    ppermute x9, starting transfers between devices, exchange(): return lax.ppermute(value, axis, [(i, i ^ mask) for i in range(count)])  14.6 us
    pallas_call x1, Pallas kernels, local(): pl.pallas_call(functools.partial(kernel_attend, sizes, n_sample, spans),...  11.3 us
    ppermute x9, waiting for transfers between devices, exchange(): return lax.ppermute(value, axis, [(i, i ^ mask) for i in range(count)])  10.9 us
    pallas_call x1, Pallas kernels, local(): pl.pallas_call(functools.partial(kernel_own, sizes, pieces), out_shape=(s...  2.87 us
    pallas_call x1, Pallas kernels, local(): pl.pallas_call(functools.partial(kernel_mix, sizes, spans), out_shape=(st...  2.23 us
    pallas_call x1, Pallas kernels, local(): pl.pallas_call(functools.partial(kernel_final, sizes, len(steps)), out_sh...  1.28 us
    pallas_call x1, Pallas kernels, local(): pl.pallas_call(functools.partial(kernel_pack, sizes, pieces), out_shape=[...  1.27 us
    pallas_call x1, Pallas kernels, local(): pl.pallas_call(kernel_own_grad, out_shape=(struct((TOKENS, feat), F32), s...  1.06 us
  transfers between devices with their start and end apart: 9, of which 6 were waited for; matrix products, arithmetic and copies ran while one was open for 0% of the time, Pallas kernels for 16%

profile of v6, /device:TPU:0, one launch (start us, length us, event | category | flops | bytes accessed | tf_op | source)
XLA Modules:
  0.0 47.4 jit_solution(17291141211247181033)
XLA Ops:
  0.6 1.3 %pack.1 = (bf16[48,512]{1,0:T(8,128)(2,1)S(1)}, bf16[48,512]{1,0:T(8,128)(2,1)S(1)}, bf16[512,512]{1,0:T(8,128)(2,1)S(1)}) custom-call(bf16[512,512]{1,0:T(8,128)(2,1)} %bitcast.6), custom_call_target="tpu_custom_call" | custom-call | flops 50331648 | bytes 1000000 | tf_op jit(solution)/shard_map/pack/pallas_call | solution.py:383
  1.9 3.1 %collective-permute-start = (bf16[48,512]{1,0:T(8,128)(2,1)S(1)}, bf16[48,512]{1,0:T(8,128)(2,1)S(1)}, u32[]{:S(2)}, u32[]{:S(2)}) collective-permute-start(bf16[48,512]{1,0:T(8,128)(2,1)S(1)} %get-tuple-element.34), channel_id=1, source_target_pairs={{0,4},{4,0},{8,12},{12,8},{1,5},{5,1},{9,13},{13,9},{2,6},{6,2},{1... | collective-permute-start | bytes 147464 | tf_op jit(solution)/shard_map/ppermute | solution.py:355
  5.0 2.5 %collective-permute-start.1 = (bf16[48,512]{1,0:T(8,128)(2,1)S(1)}, bf16[48,512]{1,0:T(8,128)(2,1)S(1)}, u32[]{:S(2)}, u32[]{:S(2)}) collective-permute-start(bf16[48,512]{1,0:T(8,128)(2,1)S(1)} %get-tuple-element.35), channel_id=1, source_target_pairs={{0,12},{4,8},{8,4},{12,0},{1,13},{5,9},{9,5},{13,1},{2,14},{6,10},... | collective-permute-start | bytes 147464 | tf_op jit(solution)/shard_map/ppermute | solution.py:355
  7.5 0.0 copy-start.1
  7.5 2.9 %own.1 = (bf16[512,512]{1,0:T(8,128)(2,1)S(1)}, bf16[640,1024]{1,0:T(8,128)(2,1)S(1)}, bf16[1024,640]{1,0:T(8,128)(2,1)S(1)}, bf16[512,640]{1,0:T(8,128)(2,1)S(1...) custom-call(s32[1,4]{1,0:T(1,128)} %margin_hbm.1, ...), custom_call_target="tpu_custom_call" | custom-call | flops 1073741824 | bytes 7000000 | tf_op jit(solution)/shard_map/own/pallas_call | solution.py:399
  10.4 0.0 collective-permute-done.refs_0_
  10.4 0.5 %collective-permute-done.1.refs_1_ = bf16[48,512]{1,0:T(8,128)(2,1)S(1)} collective-permute-done((bf16[48,512]{1,0:T(8,128)(2,1)S(1)}, bf16[48,512]{1,0:T(8,128)(2,1)S(1)}, u32[]{:S(2)}, u32[]{:S(2)}) %collective-permute-start.1) | collective-permute-done | bytes 49184 | tf_op jit(solution)/shard_map/ppermute | solution.py:355
  10.9 0.0 copy-done.1
  10.9 11.3 %attend.1 = (bf16[640,1024]{1,0:T(8,128)(2,1)S(1)}, bf16[1024,640]{1,0:T(8,128)(2,1)S(1)}, bf16[512,640]{1,0:T(8,128)(2,1)S(1)}, bf16[4,640,1024]{2,1,0:T(8,128)...) custom-call(bf16[512,512]{1,0:T(8,128)(2,1)S(1)} %get-tuple-element., ...), custom_call_target="tpu_custom_call", output_to_operand_aliasing={{0}: (7, {}), {1}: (8, {}), {2}: (9, {})} | custom-call | flops 8053063680 | bytes 6000000 | tf_op jit(solution)/shard_map/attend/pallas_call | solution.py:422
  22.2 0.1 collective-permute-start.2
  22.2 2.2 %mix.1 = (bf16[512,512]{1,0:T(8,128)(2,1)}, bf16[32,768]{1,0:T(8,128)(2,1)S(1)}, bf16[32,768]{1,0:T(8,128)(2,1)S(1)}) custom-call(bf16[1024,640]{1,0:T(8,128)(2,1)S(1)} %get-tuple-element.39.kvt_ref, bf16[4,640,1024]{2,1,0:T(8,128)(2,1)S(1)} %get-tuple-element.40.pb_ref, bf16[640,1536]{1,0:T(8,128)(2,1)S(1)} %get-tuple-element.41.grad_ref, ...), custom_call_target="tpu_custom_call" | custom-call | flops 1342177280 | bytes 6000000 | tf_op jit(solution)/shard_map/mix/pallas_call | solution.py:448
  24.5 0.0 collective-permute-done.2
  24.5 0.2 fusion
  24.8 0.2 collective-permute-start.4
  25.0 1.6 %collective-permute-start.3 = (bf16[256,384]{1,0:T(8,128)(2,1)S(1)}, bf16[256,384]{1,0:T(8,128)(2,1)S(1)}, u32[]{:S(2)}, u32[]{:S(2)}) collective-permute-start(bf16[256,384]{1,0:T(8,128)(2,1)S(1)} %split.54), channel_id=1, source_target_pairs={{0,2},{1,3},{2,0},{3,1},{4,6},{5,7},{6,4},{7,5},{8,10},{9,11},{10,... | collective-permute-start | bytes 589832 | tf_op jit(solution)/shard_map/ppermute | solution.py:355
  26.6 1.1 %own_grad.1 = (f32[512,512]{1,0:T(8,128)S(1)}, f32[512,512]{1,0:T(8,128)S(1)}, f32[512,128]{1,0:T(8,128)S(1)}) custom-call(bf16[512,512]{1,0:T(8,128)(2,1)S(1)} %get-tuple-element.29.tok_ref, bf16[512,1536]{1,0:T(8,128)(2,1)S(1)} %get-tuple-element.31.w_ref, bf16[640,1536]{1,0:T(8,128)(2,1)S(1)} %get-tuple-element.41.grad_ref), custom_call_target="tpu_custom_call" | custom-call | flops 805306368 | bytes 5000000 | tf_op jit(solution)/shard_map/own_grad/pallas_call | solution.py:462
  27.7 4.5 %collective-permute-done.3 = bf16[256,384]{1,0:T(8,128)(2,1)S(1)} collective-permute-done((bf16[256,384]{1,0:T(8,128)(2,1)S(1)}, bf16[256,384]{1,0:T(8,128)(2,1)S(1)}, u32[]{:S(2)}, u32[]{:S(2)}) %collective-permute-start.3) | collective-permute-done | bytes 196640 | tf_op jit(solution)/shard_map/ppermute | solution.py:355
  32.2 0.9 %collective-permute-done.4 = bf16[160,768]{1,0:T(8,128)(2,1)S(1)} collective-permute-done((bf16[160,768]{1,0:T(8,128)(2,1)S(1)}, bf16[160,768]{1,0:T(8,128)(2,1)S(1)}, u32[]{:S(2)}, u32[]{:S(2)}) %collective-permute-start.4) | collective-permute-done | bytes 245792 | tf_op jit(solution)/shard_map/ppermute | solution.py:355
  33.2 0.0 copy-start
  33.3 0.9 %collective-permute-start.6 = (bf16[128,384]{1,0:T(8,128)(2,1)S(1)}, bf16[128,384]{1,0:T(8,128)(2,1)S(1)}, u32[]{:S(2)}, u32[]{:S(2)}) collective-permute-start(bf16[128,384]{1,0:T(8,128)(2,1)S(1)} %split.76), channel_id=1, source_target_pairs={{0,4},{4,0},{8,12},{12,8},{1,5},{5,1},{9,13},{13,9},{2,6},{6,2},{1... | collective-permute-start | bytes 294920 | tf_op jit(solution)/shard_map/ppermute | solution.py:355
  34.2 2.5 %collective-permute-start.5 = (bf16[96,768]{1,0:T(8,128)(2,1)S(1)}, bf16[96,768]{1,0:T(8,128)(2,1)S(1)}, u32[]{:S(2)}, u32[]{:S(2)}) collective-permute-start(bf16[96,768]{1,0:T(8,128)(2,1)S(1)} %pad_maximum_fusion.2), channel_id=1, source_target_pairs={{0,12},{4,8},{8,4},{12,0},{1,13},{5,9},{9,5},{13,1},{2,14},{6,10},... | collective-permute-start | bytes 442376 | tf_op jit(solution)/shard_map/ppermute | solution.py:355
  36.7 1.9 %collective-permute-done.6.refs_2_ = bf16[128,384]{1,0:T(8,128)(2,1)S(1)} collective-permute-done((bf16[128,384]{1,0:T(8,128)(2,1)S(1)}, bf16[128,384]{1,0:T(8,128)(2,1)S(1)}, u32[]{:S(2)}, u32[]{:S(2)}) %collective-permute-start.6) | collective-permute-done | bytes 98336 | tf_op jit(solution)/shard_map/ppermute | solution.py:355
  38.7 2.2 %collective-permute-start.7 = (bf16[64,384]{1,0:T(8,128)(2,1)S(1)}, bf16[64,384]{1,0:T(8,128)(2,1)S(1)}, u32[]{:S(2)}, u32[]{:S(2)}) collective-permute-start(bf16[64,384]{1,0:T(8,128)(2,1)S(1)} %split.79), channel_id=1, source_target_pairs={{0,12},{4,8},{8,4},{12,0},{1,13},{5,9},{9,5},{13,1},{2,14},{6,10},... | collective-permute-start | bytes 147464 | tf_op jit(solution)/shard_map/ppermute | solution.py:355
  40.9 1.6 %collective-permute-done.5 = bf16[96,768]{1,0:T(8,128)(2,1)S(1)} collective-permute-done((bf16[96,768]{1,0:T(8,128)(2,1)S(1)}, bf16[96,768]{1,0:T(8,128)(2,1)S(1)}, u32[]{:S(2)}, u32[]{:S(2)}) %collective-permute-start.5) | collective-permute-done | bytes 147488 | tf_op jit(solution)/shard_map/ppermute | solution.py:355
  42.5 1.6 %collective-permute-start.8 = (bf16[64,384]{1,0:T(8,128)(2,1)S(1)}, bf16[64,384]{1,0:T(8,128)(2,1)S(1)}, u32[]{:S(2)}, u32[]{:S(2)}) collective-permute-start(bf16[64,384]{1,0:T(8,128)(2,1)S(1)} %split.78), channel_id=1, source_target_pairs={{0,2},{1,3},{2,0},{3,1},{4,6},{5,7},{6,4},{7,5},{8,10},{9,11},{10,... | collective-permute-start | bytes 147464 | tf_op jit(solution)/shard_map/ppermute | solution.py:355
  44.1 0.0 copy-done
  44.1 1.3 %final.1 = bf16[512,512]{1,0:T(8,128)(2,1)} custom-call(f32[512,512]{1,0:T(8,128)S(1)} %get-tuple-element.49.total_ref, f32[512,512]{1,0:T(8,128)S(1)} %get-tuple-element.50.standard_ref, f32[512,128]{1,0:T(8,128)S(1)} %get-tuple-element.51.inv_ref, s32[1,128]{1,0:T(1,128)S(1)} %copy-done, bf16[32,768]{1,0:T(8,128)(2,1)S(1)} %slice.18.refs_0_, ...), custom_call_target="tpu_custom_call" | custom-call | flops 805306368 | bytes 5000000 | tf_op jit(solution)/shard_map/final/pallas_call | solution.py:508
  45.4 0.0 collective-permute-done.7
  45.4 1.3 %collective-permute-done.8 = bf16[64,384]{1,0:T(8,128)(2,1)S(1)} collective-permute-done((bf16[64,384]{1,0:T(8,128)(2,1)S(1)}, bf16[64,384]{1,0:T(8,128)(2,1)S(1)}, u32[]{:S(2)}, u32[]{:S(2)}) %collective-permute-start.8) | collective-permute-done | bytes 49184 | tf_op jit(solution)/shard_map/ppermute | solution.py:355
  46.7 0.7 %pad_maximum_fusion.1 = f32[128,384]{1,0:T(8,128)} fusion(f32[64,384]{1,0:T(8,128)S(1)} %slice_add_fusion.4, f32[64,384]{1,0:T(8,128)S(1)} %slice_add_fusion.5), kind=kLoop, calls=%fused_computation.8 | loop fusion | flops 49152 | bytes 393216 | tf_op jit(solution)/shard_map/concatenate | solution.py:506
  (16 shorter events, 0.2 us)
Async XLA Ops:
  1.9 8.5 %collective-permute-start = (bf16[48,512]{1,0:T(8,128)(2,1)S(1)}, bf16[48,512]{1,0:T(8,128)(2,1)S(1)}, u32[]{:S(2)}, u32[]{:S(2)}) collective-permute-start(bf16[48,512]{1,0:T(8,128)(2,1)S(1)} %get-tuple-element.34), channel_id=1, source_target_pairs={{0,4},{4,0},{8,12},{12,8},{1,5},{5,1},{9,13},{13,9},{2,6},{6,2},{1... | collective-permute-start | bytes 147464 | tf_op jit(solution)/shard_map/ppermute | solution.py:355
  5.0 5.9 %collective-permute-start.1 = (bf16[48,512]{1,0:T(8,128)(2,1)S(1)}, bf16[48,512]{1,0:T(8,128)(2,1)S(1)}, u32[]{:S(2)}, u32[]{:S(2)}) collective-permute-start(bf16[48,512]{1,0:T(8,128)(2,1)S(1)} %get-tuple-element.35), channel_id=1, source_target_pairs={{0,12},{4,8},{8,4},{12,0},{1,13},{5,9},{9,5},{13,1},{2,14},{6,10},... | collective-permute-start | bytes 147464 | tf_op jit(solution)/shard_map/ppermute | solution.py:355
  7.5 3.4 %copy-start.1 = (bf16[1,1,512,512]{3,2,1,0:T(8,128)(2,1)S(1)}, bf16[1,1,512,512]{3,2,1,0:T(8,128)(2,1)}, u32[]{:S(2)}) copy-start(bf16[1,1,512,512]{3,2,1,0:T(8,128)(2,1)} %param.6) | copy-start | bytes 1572868
  22.2 2.4 %collective-permute-start.2 = (bf16[512,768]{1,0:T(8,128)(2,1)S(1)}, bf16[512,768]{1,0:T(8,128)(2,1)S(1)}, u32[]{:S(2)}, u32[]{:S(2)}) collective-permute-start(bf16[512,768]{1,0:T(8,128)(2,1)S(1)} %get-tuple-element.44), channel_id=1, source_target_pairs={{0,1},{1,0},{2,3},{3,2},{4,5},{5,4},{6,7},{7,6},{8,9},{9,8},{10,11... | collective-permute-start | bytes 2359304 | tf_op jit(solution)/shard_map/ppermute | solution.py:355
  24.8 8.4 %collective-permute-start.4 = (bf16[160,768]{1,0:T(8,128)(2,1)S(1)}, bf16[160,768]{1,0:T(8,128)(2,1)S(1)}, u32[]{:S(2)}, u32[]{:S(2)}) collective-permute-start(bf16[160,768]{1,0:T(8,128)(2,1)S(1)} %pad_maximum_fusion), channel_id=1, source_target_pairs={{0,4},{4,0},{8,12},{12,8},{1,5},{5,1},{9,13},{13,9},{2,6},{6,2},{1... | collective-permute-start | bytes 737288 | tf_op jit(solution)/shard_map/ppermute | solution.py:355
  25.0 7.2 %collective-permute-start.3 = (bf16[256,384]{1,0:T(8,128)(2,1)S(1)}, bf16[256,384]{1,0:T(8,128)(2,1)S(1)}, u32[]{:S(2)}, u32[]{:S(2)}) collective-permute-start(bf16[256,384]{1,0:T(8,128)(2,1)S(1)} %split.54), channel_id=1, source_target_pairs={{0,2},{1,3},{2,0},{3,1},{4,6},{5,7},{6,4},{7,5},{8,10},{9,11},{10,... | collective-permute-start | bytes 589832 | tf_op jit(solution)/shard_map/ppermute | solution.py:355
  33.2 10.9 %copy-start = (s32[1,128]{1,0:T(1,128)S(1)}, s32[1,128]{1,0:T(1,128)}, u32[]{:S(2)}) copy-start(s32[1,128]{1,0:T(1,128)} %constant.2.clone.index_ref) | copy-start | bytes 1540
  33.3 5.4 %collective-permute-start.6 = (bf16[128,384]{1,0:T(8,128)(2,1)S(1)}, bf16[128,384]{1,0:T(8,128)(2,1)S(1)}, u32[]{:S(2)}, u32[]{:S(2)}) collective-permute-start(bf16[128,384]{1,0:T(8,128)(2,1)S(1)} %split.76), channel_id=1, source_target_pairs={{0,4},{4,0},{8,12},{12,8},{1,5},{5,1},{9,13},{13,9},{2,6},{6,2},{1... | collective-permute-start | bytes 294920 | tf_op jit(solution)/shard_map/ppermute | solution.py:355
  34.2 8.3 %collective-permute-start.5 = (bf16[96,768]{1,0:T(8,128)(2,1)S(1)}, bf16[96,768]{1,0:T(8,128)(2,1)S(1)}, u32[]{:S(2)}, u32[]{:S(2)}) collective-permute-start(bf16[96,768]{1,0:T(8,128)(2,1)S(1)} %pad_maximum_fusion.2), channel_id=1, source_target_pairs={{0,12},{4,8},{8,4},{12,0},{1,13},{5,9},{9,5},{13,1},{2,14},{6,10},... | collective-permute-start | bytes 442376 | tf_op jit(solution)/shard_map/ppermute | solution.py:355
  38.7 6.7 %collective-permute-start.7 = (bf16[64,384]{1,0:T(8,128)(2,1)S(1)}, bf16[64,384]{1,0:T(8,128)(2,1)S(1)}, u32[]{:S(2)}, u32[]{:S(2)}) collective-permute-start(bf16[64,384]{1,0:T(8,128)(2,1)S(1)} %split.79), channel_id=1, source_target_pairs={{0,12},{4,8},{8,4},{12,0},{1,13},{5,9},{9,5},{13,1},{2,14},{6,10},... | collective-permute-start | bytes 147464 | tf_op jit(solution)/shard_map/ppermute | solution.py:355
  42.5 4.2 %collective-permute-start.8 = (bf16[64,384]{1,0:T(8,128)(2,1)S(1)}, bf16[64,384]{1,0:T(8,128)(2,1)S(1)}, u32[]{:S(2)}, u32[]{:S(2)}) collective-permute-start(bf16[64,384]{1,0:T(8,128)(2,1)S(1)} %split.78), channel_id=1, source_target_pairs={{0,2},{1,3},{2,0},{3,1},{4,6},{5,7},{6,4},{7,5},{8,10},{9,11},{10,... | collective-permute-start | bytes 147464 | tf_op jit(solution)/shard_map/ppermute | solution.py:355
